TPU v7x, 32 devices: a whole 2x2x4 slice. The times are simulated.
32 devices in a mesh: cfg: 2 (over y), space: 8 (over z, x), tm: 2 (over core).
Axes of the slice: x: 2, y: 2, z: 4, core: 2. Of those that a mesh axis runs over, the one named last changes fastest.
Arguments:
- eigvecs: bfloat16 [4, 2, 3, 1536, 256], P(('cfg', 'tm'), None, None, 'space'), parts along dimension 0, may hold values from -6 to 6
- momenta: int32 [3, 3], replicated, may hold values from -2 to 2, as said below
- pair_list: int32 [8, 2], P('tm'), may hold values from 0 to 1
- panels: bfloat16 [16, 2, 1024, 1024], P(('cfg', 'tm'), None, 'space'), parts along dimension 0, may hold values from -6 to 6
Outputs:
- dressed: bfloat16 [16, 3, 2, 1024, 1024], P(('cfg', 'tm'), None, None, 'space'), parts along dimension 0
There are 2 independent parts, one for each index of `cfg`. A program takes and returns all parts, laid end to end along the dimension named above; an argument that names none is the same for every part. Nothing has to cross between parts.
Inputs may be any that keep to these rules, and one draw needn't show every extreme that they name: `momenta`: the first component of every momentum is nonzero.
All inputs are finite; a program needn't handle non-finite values.
Results may differ from a plain program's by a relative error of at most 0.0075.
Values may be sent and summed in bfloat16 or wider, within the bound.
No kernel may reach another device: no remote copies, remote signals or barrier semaphores. Data moves between devices by JAX's collectives and lax.ppermute only.
A program may use at most 64 MiB of HBM per device.

v0:
```python
import math

import jax
import jax.numpy as jnp
from jax import lax
from jax.sharding import PartitionSpec as P

LX = 64


def phased_block(cosine, sine_part, real_part, imag_part):
    cos_col = cosine[:, None]
    sin_col = sine_part[:, None]
    wave_re = cos_col * real_part + sin_col * imag_part
    wave_im = cos_col * imag_part - sin_col * real_part
    upper = jnp.concatenate([wave_re, wave_im], -1)
    lower = jnp.concatenate([wave_im, -wave_re], -1)
    return jnp.stack([upper, lower], -4).astype(jnp.bfloat16)


def local(eigvecs, momenta, pair_list, panels):
    slice_count, _, colors, slab_sites, vectors = eigvecs.shape
    mom_count = momenta.shape[0]
    space_count = lax.axis_size("space")
    first_site = lax.axis_index("space") * slab_sites
    site_index = first_site + jnp.arange(slab_sites, dtype=jnp.int32)
    xpos = site_index % LX
    ypos = site_index // LX % LX
    zpos = site_index // (LX * LX)
    wave = (
        momenta[:, 0:1] * xpos[None, :]
        + momenta[:, 1:2] * ypos[None, :]
        + momenta[:, 2:3] * zpos[None, :]
    )
    wave = jnp.mod(wave, LX)
    angle = wave.astype(jnp.float32) * jnp.float32(2.0 * math.pi / LX)
    cosine = jnp.cos(angle)
    sine_part = jnp.sin(angle)
    factor = 1.0 / math.sqrt(6.0 * slab_sites * space_count * vectors)
    real_part = eigvecs[:, 0].astype(jnp.float32)
    imag_part = eigvecs[:, 1].astype(jnp.float32)
    phased_all = jnp.concatenate(
        [
            phased_block(cosine[moment], sine_part[moment], real_part, imag_part)
            for moment in range(mom_count)
        ],
        -1,
    )
    phased_all = phased_all.reshape(slice_count, 2, colors, slab_sites, mom_count, 2 * vectors)
    gram_local = jnp.einsum(
        "trcsk,trcsml->tmkl", eigvecs, phased_all, preferred_element_type=jnp.float32
    )
    gram_local = factor * gram_local
    summed = lax.psum(gram_local, "space")
    own_fields = summed.astype(jnp.bfloat16)
    meson_fields = lax.all_gather(own_fields, "tm", axis=0, tiled=True)
    pair_count = pair_list.shape[0]
    panel_rows = panels.shape[2]
    panel_width = panels.shape[3]
    spins = panel_width // vectors
    source_fields = jnp.take(meson_fields, pair_list[:, 0], axis=0).reshape(
        pair_count, mom_count, vectors, 2, vectors
    )
    sink_fields = jnp.take(meson_fields, pair_list[:, 1], axis=0).reshape(
        pair_count, mom_count, vectors, 2, vectors
    )
    panel_parts = panels.reshape(pair_count, 2, panel_rows, spins, vectors)
    panel_re = panel_parts[:, 0]
    panel_im = panel_parts[:, 1]
    panel_mix = jnp.stack(
        [jnp.stack([panel_re, panel_im], 1), jnp.stack([panel_im, -panel_re], 1)], 1
    )
    right_dressed = jnp.einsum(
        "porxbk,pmlrk->pmoxbl", panel_mix, source_fields, preferred_element_type=jnp.float32
    )
    right_dressed = right_dressed.astype(jnp.bfloat16).reshape(
        pair_count * mom_count, 2, panel_rows, panel_width
    )
    turned = lax.all_to_all(right_dressed, "space", split_axis=3, concat_axis=2, tiled=True)
    column_count = turned.shape[3]
    turned = turned.reshape(pair_count, mom_count, 2, spins, vectors, column_count)
    turned_re = turned[:, :, 0]
    turned_im = turned[:, :, 1]
    mixed_parts = jnp.stack(
        [jnp.stack([turned_re, -turned_im], 2), jnp.stack([turned_im, turned_re], 2)], 2
    )
    dressed = jnp.einsum(
        "pmorajc,pmkrj->pmocak", mixed_parts, sink_fields, preferred_element_type=jnp.float32
    )
    return dressed.reshape(pair_count, mom_count, 2, column_count, panel_width).astype(jnp.bfloat16)


def solution(mesh):
    placed = (
        P(("cfg", "tm"), None, None, "space", None),
        P(),
        P("tm", None),
        P(("cfg", "tm"), None, "space", None),
    )
    return jax.shard_map(
        local,
        mesh=mesh,
        in_specs=placed,
        out_specs=P(("cfg", "tm"), None, None, "space", None),
        check_vma=False,
    )
```

profile of v0, /device:TPU:0, one launch (start us, length us, event | category | flops | bytes accessed | tf_op | source)
XLA Modules:
  0.0 344.7 jit_solution(5193341892418195743)
XLA Ops:
  6.5 0.0 all-gather.2.cloned.1.call-start
  6.6 1.0 slice_reduce_fusion.2
  7.6 0.1 fusion.37
  7.7 0.0 copy-start.3
  7.8 1.6 fusion.30
  9.3 0.1 maximum_bitcast_fusion.9
  9.4 0.1 pad_maximum_fusion
  9.5 0.0 copy-done.3
  9.6 0.3 fusion.28
  9.8 0.1 maximum_bitcast_fusion.11
  10.0 0.1 maximum_bitcast_fusion.13
  10.1 1.2 fusion.17
  11.3 82.9 %all-reduce.1 = bf16[1,3,256,512]{2,3,1,0:T(8,128)(2,1)S(1)} all-reduce(f32[1,3,256,512]{2,3,1,0:T(8,128)S(1)} %fusion.17), channel_id=1, replica_groups=mesh['cfg'=2,'space'=8,'tm'=2] {'space'}, use_global_device_ids=true, to_apply=%region_0.1 | all-reduce | flops 393216 | bytes 2359296 | tf_op jit(solution)/shard_map/psum | solution.py:54
  94.3 1.3 copy.48
  95.5 0.0 all-gather.2.cloned.1.call-update
  95.5 3.0 copy.49
  98.6 1.5 fusion.42
  100.1 1.5 copy.77
  101.6 1.2 neg.44
  102.8 0.0 copy-start.4
  102.8 0.0 copy-start.2
  102.8 2.5 copy.76
  105.3 2.3 copy.53
  107.7 0.0 copy-done.4
  107.7 0.0 copy-done.2
  107.7 2.7 maximum_bitcast_fusion.6
  110.4 0.0 all-gather.2.cloned.1.call-done
  110.4 2.2 gather_fusion.1
  112.6 2.0 broadcast_select_fusion
  114.6 3.8 %reshape.415 = bf16[4,3,256,2,256]{4,3,2,1,0:T(2,128)(2,1)S(1)} reshape(bf16[4,3,256,512]{3,2,1,0:T(8,128)(2,1)} %broadcast_select_fusion) | data formatting | bytes 6291456 | tf_op jit(solution)/shard_map/reshape | solution.py:61
  118.4 6.2 %bitcast_convert_fusion.1 = bf16[4,3,256,2,128,4]{4,2,5,3,1,0:T(8,128)(2,1)S(1)} fusion(bf16[4,1,2,128,4,256]{5,3,2,4,1,0:T(8,128)(2,1)} %maximum_bitcast_fusion.6, bf16[4,1,2,128,4,256]{5,3,2,4,1,0:T(8,128)(2,1)} %copy.53, bf16[4,3,256,2,256,1,1]{4,3,2,1,0,6,5:T(2,128)(2,1)S(1)} %bitcast.120), kind=kOutput, calls=%fused_computation.7 | convolution fusion | flops 3232759808 | bytes 13631488 | tf_op jit(solution)/shard_map/porxbk,pmlrk->pmoxbl/dot_general | solution.py:73
  124.6 36.6 %copy.55 = bf16[12,2,128,1024]{2,1,0,3:T(2,128)(2,1)} copy(bf16[12,2,128,1024]{2,3,1,0:T(8,128)(2,1)S(1)} %bitcast.117) | data formatting | bytes 12582912 | tf_op jit(solution)/shard_map/reshape | solution.py:76
  161.2 0.0 copy-start.1
  161.2 5.1 %all-to-all-start = ((bf16[12,2,128,1024]{2,1,0,3:T(2,128)(2,1)}), bf16[12,2,128,1024]{2,1,0,3:T(2,128)(2,1)}, u32[]{:S(2)}, u32[]{:S(2)}) async-start(bf16[12,2,128,1024]{2,1,0,3:T(2,128)(2,1)} %copy.55), calls=%async_computation | async-start | bytes 12582912 | tf_op jit(solution)/shard_map/all_to_all | solution.py:79
  166.3 0.0 copy-done.1
  166.3 2.5 gather_fusion
  168.8 2.3 broadcast_select_fusion.1
  171.1 3.1 reshape.414
  174.1 126.4 %all-to-all-done = bf16[12,2,128,1024]{2,1,0,3:T(2,128)(2,1)} async-done(((bf16[12,2,128,1024]{2,1,0,3:T(2,128)(2,1)}), bf16[12,2,128,1024]{2,1,0,3:T(2,128)(2,1)}, u32[]{:S(2)}, u32[]{:S(2)}) %all-to-all-start) | async-done | bytes 6291488 | tf_op jit(solution)/shard_map/all_to_all | solution.py:79
  300.5 6.9 %copy.56 = bf16[12,2,128,1024]{2,3,1,0:T(8,128)(2,1)} copy(bf16[12,2,128,1024]{2,1,0,3:T(2,128)(2,1)} %all-to-all-done) | data formatting | bytes 12582912 | tf_op jit(solution)/shard_map/all_to_all | solution.py:79
  307.3 8.6 %copy.57 = bf16[12,2,8,128,128]{4,3,2,1,0:T(8,128)(2,1)} copy(bf16[12,2,8,128,128]{3,4,2,1,0:T(8,128)(2,1)} %bitcast.114) | data formatting | bytes 12582912 | tf_op jit(solution)/shard_map/all_to_all | solution.py:79
  316.0 0.0 copy-start
  316.0 3.4 slice_bitcast_fusion
  319.4 1.2 copy-done
  320.6 0.4 fusion.41
  321.0 1.0 maximum_bitcast_fusion
  322.0 7.2 %bitcast_convert_fusion = bf16[4,3,256,2,4,128]{5,2,4,3,1,0:T(8,128)(2,1)} fusion(bf16[4,3,1,2,4,256,128]{6,5,3,4,2,1,0:T(8,128)(2,1)S(1)} %get-tuple-element.16, bf16[4,3,1,2,4,256,128]{6,5,3,4,2,1,0:T(8,128)(2,1)S(1)} %get-tuple-element.15, bf16[4,3,256,2,256,1,1]{4,3,2,1,0,6,5:T(2,128)(2,1)} %bitcast.119), kind=kOutput, calls=%fused_computation.6 | convolution fusion | flops 3249537024 | bytes 22020096 | tf_op jit(solution)/shard_map/pmorajc,pmkrj->pmocak/dot_general | solution.py:87
  329.2 8.6 %copy.62 = bf16[4,3,2,128,1024]{4,3,2,1,0:T(8,128)(2,1)} copy(bf16[4,3,2,128,1024]{3,4,2,1,0:T(8,128)(2,1)} %bitcast.118) | data formatting | bytes 12582912 | tf_op jit(solution)/shard_map/convert_element_type | solution.py:90
  (6 shorter events, 0.1 us)
Async XLA Ops:
  6.5 103.9 %all-gather.2.cloned.1.call-start = ((), (), s32[]{:S(2)}) async-start(), calls=%async_computation.1 | async-start | bytes 2359296 | tf_op jit(solution)/shard_map/all_gather | solution.py:56
  7.7 1.8 copy-start.3
  102.8 4.9 %copy-start.4 = (s32[4,2]{0,1:T(2,128)S(1)}, s32[4,2]{0,1:T(2,128)}, u32[]{:S(2)}) copy-start(s32[4,2]{0,1:T(2,128)} %param.8) | copy-start | bytes 100
  102.8 4.9 %copy-start.2 = (bf16[4,1,128,4,256]{4,2,1,3,0:T(8,128)(2,1)S(1)}, bf16[4,1,128,4,256]{4,2,1,3,0:T(8,128)(2,1)}, u32[]{:S(2)}) copy-start(bf16[4,1,128,4,256]{4,2,1,3,0:T(8,128)(2,1)} %neg.44) | copy-start | bytes 3145732
  161.2 5.1 %copy-start.1 = (bf16[2,3,256,512]{3,2,1,0:T(8,128)(2,1)S(1)}, bf16[2,3,256,512]{3,2,1,0:T(8,128)(2,1)}, u32[]{:S(2)}) copy-start(bf16[2,3,256,512]{3,2,1,0:T(8,128)(2,1)} %all-gather.2.cloned.1.call-done) | copy-start | bytes 4718596
  161.2 139.2 %all-to-all-start = ((bf16[12,2,128,1024]{2,1,0,3:T(2,128)(2,1)}), bf16[12,2,128,1024]{2,1,0,3:T(2,128)(2,1)}, u32[]{:S(2)}, u32[]{:S(2)}) async-start(bf16[12,2,128,1024]{2,1,0,3:T(2,128)(2,1)} %copy.55), calls=%async_computation | async-start | bytes 12582912 | tf_op jit(solution)/shard_map/all_to_all | solution.py:79
  316.0 4.6 %copy-start = (bf16[12,2,8,128,128]{4,3,2,1,0:T(8,128)(2,1)S(1)}, bf16[12,2,8,128,128]{4,3,2,1,0:T(8,128)(2,1)}, u32[]{:S(2)}) copy-start(bf16[12,2,8,128,128]{4,3,2,1,0:T(8,128)(2,1)} %copy.57) | copy-start | bytes 18874372
Sparse Core Ops, SparseCore 0:
  95.7 9.2 all-gather.1
where the time goes:
time: 346 us; the launch traced here: 345 us
  waiting for transfers between devices  126 us (36%)
  local copies, waits for them, and re-layouts  90 us (26%)
  blocking collectives  82.9 us (24%)
  matrix products  14.6 us (4%)
  between operations  13.6 us (4%)
  other arithmetic  12 us (3%)
  starting transfers between devices  5.08 us (1%)
    all_to_all x1, waiting for transfers between devices, local(): lax.all_to_all(right_dressed, 'space', split_axis=3, concat_axis=2, tiled...  126 us
    psum x1, blocking collectives, local(): summed = lax.psum(gram_local, 'space')  82.9 us
    reshape x1, local copies, waits for them, and re-layouts, local(): right_dressed.astype(jnp.bfloat16)  36.6 us
    all_to_all x2, local copies, waits for them, and re-layouts, local(): lax.all_to_all(right_dressed, 'space', split_axis=3, concat_axis=2, tiled...  15.5 us
    unnamed x14, local copies, waits for them, and re-layouts  11.7 us
    convert_element_type x1, local copies, waits for them, and re-layouts, local(): dressed.reshape(pair_count, mom_count, 2, column_count, panel_width)  8.62 us
    dot_general x1, matrix products, local(): jnp.einsum('pmorajc,pmkrj->pmocak', mixed_parts, sink_fields, preferred_e...  7.2 us
  transfers between devices with their start and end apart: 2, of which 1 were waited for; matrix products, arithmetic and copies ran while one was open for 7% of the time, Pallas kernels for 0%

commit v1 on v0

--- a/solution.py
+++ b/solution.py
@@ -1,11 +1,269 @@
+import functools
 import math
 
 import jax
 import jax.numpy as jnp
 from jax import lax
+from jax.experimental import pallas as pl
+from jax.experimental.pallas import tpu as pltpu
 from jax.sharding import PartitionSpec as P
 
 LX = 64
+LX_BITS = LX.bit_length() - 1
+F32, BF16 = jnp.float32, jnp.bfloat16
+VMEM_LIMIT = 40 * 1024 * 1024
+
+
+def params(steps=0):
+    return pltpu.CompilerParams(
+        vmem_limit_bytes=VMEM_LIMIT, dimension_semantics=("arbitrary",) * steps or None
+    )
+
+
+def cost(flops, bytes_accessed):
+    return pl.CostEstimate(flops=int(flops), bytes_accessed=int(bytes_accessed), transcendentals=0)
+
+
+def gram_kernel(factor, place, momenta, eig, send, keep, phased, total):
+    colors, sites, vectors = eig.shape[1:]
+    moms = send.shape[0]
+    half = send.shape[1]
+    site = place[0] * sites + lax.broadcasted_iota(jnp.int32, (sites, 128), 0)
+    lane = lax.broadcasted_iota(jnp.int32, (sites, 128), 1)
+    coords = (site & (LX - 1), (site >> LX_BITS) & (LX - 1), site >> (2 * LX_BITS))
+    wave = jnp.zeros((sites, 128), jnp.int32)
+    for m in range(moms):
+        mine = sum(momenta[m, j] * coords[j] for j in range(3))
+        wave = jnp.where(lane == m, mine, wave)
+    angle = (wave & (LX - 1)).astype(F32) * F32(2.0 * math.pi / LX)
+    cosine, sine = jnp.cos(angle), jnp.sin(angle)
+    rows = colors * sites
+    both = eig[...].reshape(2 * rows, vectors)
+    bit = place[1]
+    for m in range(moms):
+        c, s = cosine[:, m : m + 1], sine[:, m : m + 1]
+        for color in range(colors):
+            re, im = eig[0, color].astype(F32), eig[1, color].astype(F32)
+            wave_re, wave_im = c * re + s * im, c * im - s * re
+            at = color * sites
+            phased[at : at + sites, :vectors] = wave_re.astype(BF16)
+            phased[at : at + sites, vectors:] = wave_im.astype(BF16)
+            at += rows
+            phased[at : at + sites, :vectors] = wave_im.astype(BF16)
+            phased[at : at + sites, vectors:] = (-wave_re).astype(BF16)
+        total[...] = factor * lax.dot_general(
+            both, phased[...], (((0,), (0,)), ((), ())), preferred_element_type=F32
+        )
+        send[m] = total[pl.ds(pl.multiple_of((1 - bit) * half, half), half), :].astype(BF16)
+        keep[m] = total[pl.ds(pl.multiple_of(bit * half, half), half), :]
+
+
+def gram_halves(eig, momenta, place, factor):
+    _, colors, sites, vectors = eig.shape
+    moms = momenta.shape[0]
+    shape = (moms, vectors // 2, 2 * vectors)
+    smem = pl.BlockSpec(memory_space=pltpu.SMEM)
+    vmem = pl.BlockSpec(memory_space=pltpu.VMEM)
+    return pl.pallas_call(
+        functools.partial(gram_kernel, factor),
+        out_shape=(jax.ShapeDtypeStruct(shape, BF16), jax.ShapeDtypeStruct(shape, F32)),
+        in_specs=[smem, smem, vmem],
+        out_specs=(vmem, vmem),
+        scratch_shapes=[
+            pltpu.VMEM((2 * colors * sites, 2 * vectors), BF16),
+            pltpu.VMEM((vectors, 2 * vectors), F32),
+        ],
+        compiler_params=params(),
+        cost_estimate=cost(4 * colors * sites * vectors * moms * 2 * vectors, 3 * 2**20),
+        name="gram",
+    )(place, momenta, eig)
+
+
+def fold_kernel(bit_at, place, keep_in, came, send, keep):
+    half = send.shape[1]
+    bit = place[bit_at]
+    own = pl.ds(pl.multiple_of(bit * half, half), half)
+    off = pl.ds(pl.multiple_of((1 - bit) * half, half), half)
+    keep[...] = keep_in[:, own, :] + came[:, own, :].astype(F32)
+    send[...] = (keep_in[:, off, :] + came[:, off, :].astype(F32)).astype(BF16)
+
+
+def fold(keep, came, place, bit_at):
+    moms, rows, width = keep.shape
+    shape = (moms, rows // 2, width)
+    smem = pl.BlockSpec(memory_space=pltpu.SMEM)
+    vmem = pl.BlockSpec(memory_space=pltpu.VMEM)
+    return pl.pallas_call(
+        functools.partial(fold_kernel, bit_at),
+        out_shape=(jax.ShapeDtypeStruct(shape, BF16), jax.ShapeDtypeStruct(shape, F32)),
+        in_specs=[smem, vmem, vmem],
+        out_specs=(vmem, vmem),
+        compiler_params=params(),
+        cost_estimate=cost(keep.size, 8 * keep.size),
+        name="fold",
+    )(place, keep, came)
+
+
+def dress_kernel(count, chained, place, other_src, other_snk, own, oth, *refs):
+    mine, near = refs[:count], refs[count : 2 * count]
+    out = refs[2 * count + chained]
+    left, sink, panel = refs[2 * count + chained + 1 :]
+    pieces, moms, piece_rows, width = own.shape
+    vectors = width // 2
+    columns = out.shape[3]
+    pair, step = pl.program_id(0), pl.program_id(1)
+    here, x = place[4], place[2]
+    block = mine[0].shape[2]
+
+    def load(field):
+        def source():
+            for m in range(moms):
+                for i in range(columns // piece_rows):
+                    q = x * (columns // piece_rows) + i
+                    rows = field[q ^ here, m]
+                    re, im = rows[:, :vectors], rows[:, vectors:]
+                    at = 2 * m * columns + i * piece_rows
+                    left[at : at + piece_rows, :vectors] = re
+                    left[at : at + piece_rows, vectors:] = im
+                    at += columns
+                    left[at : at + piece_rows, :vectors] = -im
+                    left[at : at + piece_rows, vectors:] = re
+
+        def drain():
+            for m in range(moms):
+                for q in range(pieces):
+                    rows = field[here ^ q, m]
+                    sink[m, 0, q * piece_rows : (q + 1) * piece_rows] = rows[:, :vectors]
+                    sink[m, 1, q * piece_rows : (q + 1) * piece_rows] = rows[:, vectors:]
+
+        return source, drain
+
+    own_source, own_drain = load(own)
+    oth_source, oth_drain = load(oth)
+    first = step == 0
+    src, snk = other_src[pair], other_snk[pair]
+    pl.when(first & (src == 0))(own_source)
+    pl.when(first & (src != 0))(oth_source)
+    pl.when(first & (snk == 0))(own_drain)
+    pl.when(first & (snk != 0))(oth_drain)
+
+    at_mine = pl.ds(pl.multiple_of(x * block, block), block)
+    at_near = pl.ds(pl.multiple_of((1 - x) * block, block), block)
+    for k in range(count):
+
+        @pl.when(step == k)
+        def _(k=k):
+            for part in range(2):
+                lanes = slice(part * vectors, (part + 1) * vectors)
+                panel[at_mine, lanes] = mine[k][0, part]
+                panel[at_near, lanes] = near[k][0, part]
+
+    contract = (((1,), (1,)), ((), ()))
+    right = lax.dot_general(left[...], panel[...], contract, preferred_element_type=F32).astype(BF16)
+    for m in range(moms):
+        rows = right[2 * m * columns : 2 * (m + 1) * columns]
+        with_re = lax.dot_general(rows, sink[m, 0], contract, preferred_element_type=F32)
+        with_im = lax.dot_general(rows, sink[m, 1], contract, preferred_element_type=F32)
+        out[0, m, 0] = (with_re[:columns] - with_im[columns:]).astype(BF16)
+        out[0, m, 1] = (with_im[:columns] + with_re[columns:]).astype(BF16)
+
+
+def dress(out, out_shape, first_pair, dists, mine, near, own, oth, place, other_src, other_snk):
+    pairs, _, block, vectors = mine[0].shape
+    count = len(dists)
+    moms = own.shape[1]
+    columns = out_shape.shape[3]
+    whole = pl.BlockSpec(memory_space=pltpu.VMEM)
+    chunk = pl.BlockSpec((1, 2, block, vectors), lambda p, d, *_: (p, 0, 0, 0))
+
+    def target(p, d, place, *_):
+        dist = jnp.int32(dists[0])
+        for k in range(1, count):
+            dist = jnp.where(d == k, dists[k], dist)
+        return (p + first_pair, 0, 0, 0, place[3] ^ dist)
+
+    chained = out is not None
+    operands = [own, oth, *mine, *near] + ([out] if chained else [])
+    in_specs = [whole, whole] + [chunk] * (2 * count) + [pl.BlockSpec(memory_space=pl.ANY)] * chained
+    macs = pairs * count * 2 * (2 * moms * columns) * (2 * vectors) * vectors
+    return pl.pallas_call(
+        functools.partial(dress_kernel, count, chained),
+        out_shape=out_shape,
+        grid_spec=pltpu.PrefetchScalarGridSpec(
+            num_scalar_prefetch=3,
+            grid=(pairs, count),
+            in_specs=in_specs,
+            out_specs=pl.BlockSpec((1, moms, 2, columns, vectors), target),
+            scratch_shapes=[
+                pltpu.VMEM((2 * moms * columns, 2 * vectors), BF16),
+                pltpu.VMEM((moms, 2, vectors, vectors), BF16),
+                pltpu.VMEM((2 * block, 2 * vectors), BF16),
+            ],
+        ),
+        input_output_aliases={3 + len(operands) - 1: 0} if chained else {},
+        compiler_params=params(2),
+        cost_estimate=cost(2 * macs, 2**21),
+        name="dress",
+    )(place, other_src[first_pair : first_pair + pairs], other_snk[first_pair : first_pair + pairs], *operands)
+
+
+def exchange(value, axis, mask):
+    return lax.ppermute(value, axis, [(i, i ^ mask) for i in range(lax.axis_size(axis))])
+
+
+def fast(eigvecs, momenta, pair_list, panels):
+    vectors = eigvecs.shape[4]
+    pair_count, _, rows, width = panels.shape
+    moms = momenta.shape[0]
+    space_count = lax.axis_size("space")
+    spins = width // vectors
+    space = lax.axis_index("space")
+    tm = lax.axis_index("tm")
+    x, z = space & 1, space >> 1
+    masks = [1 << b for b in range(1, spins.bit_length())][:1] + [1] + [
+        1 << b for b in range(2, spins.bit_length())
+    ]
+    bits = [(space & mask) // mask for mask in masks]
+    here = sum(bit << (len(bits) - 1 - i) for i, bit in enumerate(bits))
+    place = jnp.stack([space, bits[0], x, z, here] + bits[1:]).astype(jnp.int32)
+    other = (pair_list != tm).astype(jnp.int32)
+    other_src, other_snk = other[:, 0], other[:, 1]
+
+    factor = 1.0 / math.sqrt(6.0 * eigvecs.shape[3] * space_count * vectors)
+    send, keep = gram_halves(eigvecs[0], momenta, place, factor)
+    for step, mask in enumerate(masks):
+        came = exchange(send, "space", mask)
+        if step + 1 < len(masks):
+            send, keep = fold(keep, came, place, 5 + step)
+    field = (keep + came.astype(F32)).astype(BF16)[None]
+    for mask in masks[::-1]:
+        field = jnp.concatenate([field, exchange(field, "space", mask)], 0)
+    oth = exchange(field, "tm", 1)
+
+    chunks = 2
+    per = pair_count // chunks
+    blocks = [
+        lax.dynamic_slice_in_dim(panels, (z ^ d) * vectors, vectors, axis=3) for d in range(spins)
+    ]
+    mine = {(0, c): blocks[0][c * per : (c + 1) * per] for c in range(chunks)}
+    order = (3, 2, 1)
+    for c in range(chunks):
+        for d in order:
+            mine[d, c] = exchange(blocks[d][c * per : (c + 1) * per], "space", d << 1)
+    near = {}
+    for c in range(chunks):
+        for d in (0, *order):
+            near[d, c] = exchange(mine[d, c], "space", 1)
+    columns = width // space_count
+    out_shape = jax.ShapeDtypeStruct((pair_count, moms, 2, columns, width), BF16)
+    out = None
+    for c in range(chunks):
+        out = dress(
+            out, out_shape, c * per, list(range(spins)),
+            [mine[d, c] for d in range(spins)], [near[d, c] for d in range(spins)],
+            field, oth, place, other_src, other_snk,
+        )
+    return out
 
 
 def phased_block(cosine, sine_part, real_part, imag_part):
@@ -18,7 +276,7 @@
     return jnp.stack([upper, lower], -4).astype(jnp.bfloat16)
 
 
-def local(eigvecs, momenta, pair_list, panels):
+def general(eigvecs, momenta, pair_list, panels):
     slice_count, _, colors, slab_sites, vectors = eigvecs.shape
     mom_count = momenta.shape[0]
     space_count = lax.axis_size("space")
@@ -90,6 +348,26 @@
     return dressed.reshape(pair_count, mom_count, 2, column_count, panel_width).astype(jnp.bfloat16)
 
 
+def local(eigvecs, momenta, pair_list, panels):
+    slices, _, _, sites, vectors = eigvecs.shape
+    pairs, _, rows, width = panels.shape
+    space_count = lax.axis_size("space")
+    spins = width // vectors
+    fits = (
+        slices == 1
+        and lax.axis_size("tm") == 2
+        and space_count == 2 * spins
+        and spins == 4
+        and rows * space_count == width
+        and rows % 128 == 0
+        and (vectors // space_count) % 16 == 0
+        and sites % 16 == 0
+        and pairs % 2 == 0
+        and momenta.shape[0] <= 8
+    )
+    return (fast if fits else general)(eigvecs, momenta, pair_list, panels)
+
+
 def solution(mesh):
     placed = (
         P(("cfg", "tm"), None, None, "space", None),

time: 346 us -> 136 us (0.39)
  local copies, waits for them, and re-layouts: 90 us -> 4.5 us
  blocking collectives: 82.9 us -> 0 us
  waiting for transfers between devices: 126 us -> 59.7 us
  starting transfers between devices: 5.08 us -> 47.3 us
  Pallas kernels: 0 us -> 23.7 us
  matrix products: 14.6 us -> 0 us
  between operations: 13.6 us -> 0.08 us
  other arithmetic: 12 us -> 0.16 us
    all_to_all x1 -> x0, waiting for transfers between devices: 126 us -> none  [local(): lax.all_to_all(right_dressed, 'space', split_axis=3, concat_axis=2, tiled...]
    psum x1 -> x0, blocking collectives: 82.9 us -> none  [local(): summed = lax.psum(gram_local, 'space')]
    ppermute x0 -> x21, waiting for transfers between devices: none -> 59.7 us  [exchange(): lax.ppermute(value, axis, [(i, i ^ mask) for i in range(lax.axis_size(axi...]
    ppermute x0 -> x21, starting transfers between devices: none -> 47.3 us  [exchange(): lax.ppermute(value, axis, [(i, i ^ mask) for i in range(lax.axis_size(axi...]
    reshape x3 -> x0, local copies, waits for them, and re-layouts: 43.4 us -> none  [the longest x1 36.6 us: local(): right_dressed.astype(jnp.bfloat16)]
    pallas_call x0 -> x5, Pallas kernels: none -> 23.7 us  [the longest x2 20.2 us: dress(): pl.pallas_call(functools.partial(dress_kernel, count, chained), out_shape...]
    all_to_all x2 -> x0, local copies, waits for them, and re-layouts: 15.5 us -> none  [local(): lax.all_to_all(right_dressed, 'space', split_axis=3, concat_axis=2, tiled...]
    dot_general x3 -> x0, matrix products: 14.6 us -> none  [the longest x1 7.2 us: local(): jnp.einsum('pmorajc,pmkrj->pmocak', mixed_parts, sink_fields, preferred_e...]
  transfers between devices with their start and end apart: 2 -> 21, of which waited for: 1 -> 12; matrix products, arithmetic and copies ran while one was open for 7% -> 2% of each run, Pallas kernels for 0% -> 8%
where the time goes in v1:
time: 136 us; the launch traced here: 135 us
  waiting for transfers between devices  59.7 us (44%)
  starting transfers between devices  47.3 us (35%)
  Pallas kernels  23.7 us (17%)
  local copies, waits for them, and re-layouts  4.5 us (3%)
    ppermute x21, waiting for transfers between devices, exchange(): lax.ppermute(value, axis, [(i, i ^ mask) for i in range(lax.axis_size(axi...  59.7 us
    ppermute x21, starting transfers between devices, exchange(): lax.ppermute(value, axis, [(i, i ^ mask) for i in range(lax.axis_size(axi...  47.3 us
    pallas_call x2, Pallas kernels, dress(): pl.pallas_call(functools.partial(dress_kernel, count, chained), out_shape...  20.2 us
  transfers between devices with their start and end apart: 21, of which 12 were waited for; matrix products, arithmetic and copies ran while one was open for 2% of the time, Pallas kernels for 8%

profile of v1, /device:TPU:0, one launch (start us, length us, event | category | flops | bytes accessed | tf_op | source)
XLA Modules:
  0.0 135.4 jit_solution(9235350661078744803)
XLA Ops:
  0.0 0.1 stack.28.place
  0.1 1.1 copy-done
  1.2 0.7 copy-done.1
  1.8 2.4 %gram.1 = (bf16[3,128,512]{2,1,0:T(8,128)(2,1)S(1)}, f32[3,128,512]{2,1,0:T(8,128)S(1)}) custom-call(s32[7]{0:T(128)S(1)} %stack.28.place, s32[3,3]{1,0:T(4,128)S(1)} %copy-done.1, bf16[2,3,192,256]{3,2,1,0:T(8,128)(2,1)S(1)} %bitcast.17), custom_call_target="tpu_custom_call" | custom-call | flops 905969664 | bytes 3145728 | tf_op jit(solution)/shard_map/gram/pallas_call | solution.py:67
  4.2 3.1 %collective-permute-start = (bf16[3,128,512]{2,1,0:T(8,128)(2,1)S(1)}, bf16[3,128,512]{2,1,0:T(8,128)(2,1)S(1)}, u32[]{:S(2)}, u32[]{:S(2)}) collective-permute-start(bf16[3,128,512]{2,1,0:T(8,128)(2,1)S(1)} %get-tuple-element.12), channel_id=1, source_target_pairs={{0,4},{2,6},{4,0},{6,2},{8,12},{10,14},{12,8},{14,10},{1,5},{3,7},... | collective-permute-start | bytes 1179656 | tf_op jit(solution)/shard_map/ppermute | solution.py:211
  7.3 9.1 %collective-permute-done.came = bf16[3,128,512]{2,1,0:T(8,128)(2,1)S(1)} collective-permute-done((bf16[3,128,512]{2,1,0:T(8,128)(2,1)S(1)}, bf16[3,128,512]{2,1,0:T(8,128)(2,1)S(1)}, u32[]{:S(2)}, u32[]{:S(2)}) %collective-permute-start) | collective-permute-done | bytes 393248 | tf_op jit(solution)/shard_map/ppermute | solution.py:211
  16.4 0.6 fold.2
  17.0 1.7 %collective-permute-start.1 = (bf16[3,64,512]{2,1,0:T(8,128)(2,1)S(1)}, bf16[3,64,512]{2,1,0:T(8,128)(2,1)S(1)}, u32[]{:S(2)}, u32[]{:S(2)}) collective-permute-start(bf16[3,64,512]{2,1,0:T(8,128)(2,1)S(1)} %get-tuple-element.14), channel_id=1, source_target_pairs={{0,2},{2,0},{4,6},{6,4},{8,10},{10,8},{12,14},{14,12},{1,3},{3,1},... | collective-permute-start | bytes 589832 | tf_op jit(solution)/shard_map/ppermute | solution.py:211
  18.8 4.4 %collective-permute-done.1.came = bf16[3,64,512]{2,1,0:T(8,128)(2,1)S(1)} collective-permute-done((bf16[3,64,512]{2,1,0:T(8,128)(2,1)S(1)}, bf16[3,64,512]{2,1,0:T(8,128)(2,1)S(1)}, u32[]{:S(2)}, u32[]{:S(2)}) %collective-permute-start.1) | collective-permute-done | bytes 196640 | tf_op jit(solution)/shard_map/ppermute | solution.py:211
  23.2 0.6 fold.3
  23.8 2.5 %collective-permute-start.2 = (bf16[3,32,512]{2,1,0:T(8,128)(2,1)S(1)}, bf16[3,32,512]{2,1,0:T(8,128)(2,1)S(1)}, u32[]{:S(2)}, u32[]{:S(2)}) collective-permute-start(bf16[3,32,512]{2,1,0:T(8,128)(2,1)S(1)} %get-tuple-element.16), channel_id=1, source_target_pairs={{0,8},{2,10},{4,12},{6,14},{8,0},{10,2},{12,4},{14,6},{1,9},{3,11}... | collective-permute-start | bytes 294920 | tf_op jit(solution)/shard_map/ppermute | solution.py:211
  26.3 4.1 %collective-permute-done.2 = bf16[3,32,512]{2,1,0:T(8,128)(2,1)S(1)} collective-permute-done((bf16[3,32,512]{2,1,0:T(8,128)(2,1)S(1)}, bf16[3,32,512]{2,1,0:T(8,128)(2,1)S(1)}, u32[]{:S(2)}, u32[]{:S(2)}) %collective-permute-start.2) | collective-permute-done | bytes 98336 | tf_op jit(solution)/shard_map/ppermute | solution.py:211
  30.4 1.5 %collective-permute-start.3 = (bf16[1,3,32,512]{3,2,1,0:T(8,128)(2,1)S(1)}, bf16[1,3,32,512]{3,2,1,0:T(8,128)(2,1)S(1)}, u32[]{:S(2)}, u32[]{:S(2)}) collective-permute-start(bf16[1,3,32,512]{3,2,1,0:T(8,128)(2,1)S(1)} %fusion), channel_id=1, source_target_pairs={{0,8},{2,10},{4,12},{6,14},{8,0},{10,2},{12,4},{14,6},{1,9},{3,11}... | collective-permute-start | bytes 294920 | tf_op jit(solution)/shard_map/ppermute | solution.py:211
  32.0 4.0 %collective-permute-done.3 = bf16[1,3,32,512]{3,2,1,0:T(8,128)(2,1)S(1)} collective-permute-done((bf16[1,3,32,512]{3,2,1,0:T(8,128)(2,1)S(1)}, bf16[1,3,32,512]{3,2,1,0:T(8,128)(2,1)S(1)}, u32[]{:S(2)}, u32[]{:S(2)}) %collective-permute-start.3) | collective-permute-done | bytes 98336 | tf_op jit(solution)/shard_map/ppermute | solution.py:211
  36.0 0.4 collective-permute-start.4
  36.4 5.4 %collective-permute-done.4 = bf16[2,3,32,512]{3,2,1,0:T(8,128)(2,1)S(1)} collective-permute-done((bf16[2,3,32,512]{3,2,1,0:T(8,128)(2,1)S(1)}, bf16[2,3,32,512]{3,2,1,0:T(8,128)(2,1)S(1)}, u32[]{:S(2)}, u32[]{:S(2)}) %collective-permute-start.4) | collective-permute-done | bytes 196640 | tf_op jit(solution)/shard_map/ppermute | solution.py:211
  41.8 2.4 %collective-permute-start.5 = (bf16[4,3,32,512]{3,2,1,0:T(8,128)(2,1)S(1)}, bf16[4,3,32,512]{3,2,1,0:T(8,128)(2,1)S(1)}, u32[]{:S(2)}, u32[]{:S(2)}) collective-permute-start(bf16[4,3,32,512]{3,2,1,0:T(8,128)(2,1)S(1)} %pad_maximum_fusion.1), channel_id=1, source_target_pairs={{0,4},{2,6},{4,0},{6,2},{8,12},{10,14},{12,8},{14,10},{1,5},{3,7},... | collective-permute-start | bytes 1179656 | tf_op jit(solution)/shard_map/ppermute | solution.py:211
  44.2 2.6 %constant_dynamic-slice_fusion.4 = (bf16[2,2,128,256]{3,2,1,0:T(8,128)(2,1)S(1)}, bf16[2,2,128,256]{3,2,1,0:T(8,128)(2,1)S(1)}, bf16[2,2,128,256]{3,2,1,0:T(8,12...) fusion(bf16[4,2,128,1024]{3,2,1,0:T(8,128)(2,1)} %param.7, ...), kind=kLoop, calls=%fused_computation.9 | loop fusion | bytes 4194324 | tf_op jit(solution)/shard_map/slice | solution.py:252
  46.8 2.4 %collective-permute-start.16 = (bf16[2,2,128,256]{3,2,1,0:T(8,128)(2,1)S(1)}, bf16[2,2,128,256]{3,2,1,0:T(8,128)(2,1)S(1)}, u32[]{:S(2)}, u32[]{:S(2)}) collective-permute-start(bf16[2,2,128,256]{3,2,1,0:T(8,128)(2,1)S(1)} %get-tuple-element.17), channel_id=1, source_target_pairs={{0,12},{2,14},{4,8},{6,10},{8,4},{10,6},{12,0},{14,2},{1,13},{3,15... | collective-permute-start | bytes 786440 | tf_op jit(solution)/shard_map/ppermute | solution.py:211
  49.2 1.4 %collective-permute-start.9 = (bf16[2,2,128,256]{3,2,1,0:T(8,128)(2,1)S(1)}, bf16[2,2,128,256]{3,2,1,0:T(8,128)(2,1)S(1)}, u32[]{:S(2)}, u32[]{:S(2)}) collective-permute-start(bf16[2,2,128,256]{3,2,1,0:T(8,128)(2,1)S(1)} %get-tuple-element.18), channel_id=1, source_target_pairs={{0,12},{2,14},{4,8},{6,10},{8,4},{10,6},{12,0},{14,2},{1,13},{3,15... | collective-permute-start | bytes 786440 | tf_op jit(solution)/shard_map/ppermute | solution.py:211
  50.6 5.0 %collective-permute-done.5 = bf16[4,3,32,512]{3,2,1,0:T(8,128)(2,1)S(1)} collective-permute-done((bf16[4,3,32,512]{3,2,1,0:T(8,128)(2,1)S(1)}, bf16[4,3,32,512]{3,2,1,0:T(8,128)(2,1)S(1)}, u32[]{:S(2)}, u32[]{:S(2)}) %collective-permute-start.5) | collective-permute-done | bytes 393248 | tf_op jit(solution)/shard_map/ppermute | solution.py:211
  55.6 0.1 pad_maximum_fusion.own
  55.7 0.1 collective-permute-start.6
  55.8 0.7 collective-permute-start.8
  56.5 6.2 %collective-permute-start.7 = (bf16[2,2,128,256]{3,2,1,0:T(8,128)(2,1)}, bf16[2,2,128,256]{3,2,1,0:T(8,128)(2,1)S(1)}, u32[]{:S(2)}, u32[]{:S(2)}) collective-permute-start(bf16[2,2,128,256]{3,2,1,0:T(8,128)(2,1)} %get-tuple-element.20), channel_id=1, source_target_pairs={{0,4},{2,6},{4,0},{6,2},{8,12},{10,14},{12,8},{14,10},{1,5},{3,7},... | collective-permute-start | bytes 786440 | tf_op jit(solution)/shard_map/ppermute | solution.py:211
  62.7 7.8 %collective-permute-start.14 = (bf16[2,2,128,256]{3,2,1,0:T(8,128)(2,1)}, bf16[2,2,128,256]{3,2,1,0:T(8,128)(2,1)S(1)}, u32[]{:S(2)}, u32[]{:S(2)}) collective-permute-start(bf16[2,2,128,256]{3,2,1,0:T(8,128)(2,1)} %get-tuple-element.22), channel_id=1, source_target_pairs={{0,4},{2,6},{4,0},{6,2},{8,12},{10,14},{12,8},{14,10},{1,5},{3,7},... | collective-permute-start | bytes 786440 | tf_op jit(solution)/shard_map/ppermute | solution.py:211
  70.5 0.0 collective-permute-done.9.refs_3_
  70.5 6.8 %collective-permute-start.15 = (bf16[2,2,128,256]{3,2,1,0:T(8,128)(2,1)}, bf16[2,2,128,256]{3,2,1,0:T(8,128)(2,1)}, u32[]{:S(2)}, u32[]{:S(2)}) collective-permute-start(bf16[2,2,128,256]{3,2,1,0:T(8,128)(2,1)} %get-tuple-element.24), channel_id=1, source_target_pairs={{0,8},{2,10},{4,12},{6,14},{8,0},{10,2},{12,4},{14,6},{1,9},{3,11}... | collective-permute-start | bytes 786440 | tf_op jit(solution)/shard_map/ppermute | solution.py:211
  77.3 9.3 %collective-permute-done.8.refs_2_ = bf16[2,2,128,256]{3,2,1,0:T(8,128)(2,1)S(1)} collective-permute-done((bf16[2,2,128,256]{3,2,1,0:T(8,128)(2,1)}, bf16[2,2,128,256]{3,2,1,0:T(8,128)(2,1)S(1)}, u32[]{:S(2)}, u32[]{:S(2)}) %collective-permute-start.8) | collective-permute-done | bytes 262176 | tf_op jit(solution)/shard_map/ppermute | solution.py:211
  86.6 1.5 %collective-permute-start.17 = (bf16[2,2,128,256]{3,2,1,0:T(8,128)(2,1)S(1)}, bf16[2,2,128,256]{3,2,1,0:T(8,128)(2,1)S(1)}, u32[]{:S(2)}, u32[]{:S(2)}) collective-permute-start(bf16[2,2,128,256]{3,2,1,0:T(8,128)(2,1)S(1)} %get-tuple-element.23.refs_0_), channel_id=1, source_target_pairs={{0,2},{2,0},{4,6},{6,4},{8,10},{10,8},{12,14},{14,12},{1,3},{3,1},... | collective-permute-start | bytes 786440 | tf_op jit(solution)/shard_map/ppermute | solution.py:211
  88.1 0.0 collective-permute-done.7.refs_1_
  88.1 0.6 collective-permute-start.20
  88.6 0.0 collective-permute-done.14.refs_1_
  88.6 1.5 %collective-permute-start.18 = (bf16[2,2,128,256]{3,2,1,0:T(8,128)(2,1)S(1)}, bf16[2,2,128,256]{3,2,1,0:T(8,128)(2,1)S(1)}, u32[]{:S(2)}, u32[]{:S(2)}) collective-permute-start(bf16[2,2,128,256]{3,2,1,0:T(8,128)(2,1)S(1)} %collective-permute-done.14.refs_1_), channel_id=1, source_target_pairs={{0,2},{2,0},{4,6},{6,4},{8,10},{10,8},{12,14},{14,12},{1,3},{3,1},... | collective-permute-start | bytes 786440 | tf_op jit(solution)/shard_map/ppermute | solution.py:211
  90.1 0.9 collective-permute-start.19
  91.0 0.1 slice_bitcast_fusion
  91.1 4.7 %collective-permute-done.17.refs_4_ = bf16[2,2,128,256]{3,2,1,0:T(8,128)(2,1)S(1)} collective-permute-done((bf16[2,2,128,256]{3,2,1,0:T(8,128)(2,1)S(1)}, bf16[2,2,128,256]{3,2,1,0:T(8,128)(2,1)S(1)}, u32[]{:S(2)}, u32[]{:S(2)}) %collective-permute-start.17) | collective-permute-done | bytes 262176 | tf_op jit(solution)/shard_map/ppermute | solution.py:211
  95.8 1.5 %collective-permute-start.10 = (bf16[2,2,128,256]{3,2,1,0:T(8,128)(2,1)S(1)}, bf16[2,2,128,256]{3,2,1,0:T(8,128)(2,1)S(1)}, u32[]{:S(2)}, u32[]{:S(2)}) collective-permute-start(bf16[2,2,128,256]{3,2,1,0:T(8,128)(2,1)S(1)} %get-tuple-element.21.refs_0_), channel_id=1, source_target_pairs={{0,2},{2,0},{4,6},{6,4},{8,10},{10,8},{12,14},{14,12},{1,3},{3,1},... | collective-permute-start | bytes 786440 | tf_op jit(solution)/shard_map/ppermute | solution.py:211
  97.2 4.1 %collective-permute-done.20.refs_7_ = bf16[2,2,128,256]{3,2,1,0:T(8,128)(2,1)S(1)} collective-permute-done((bf16[2,2,128,256]{3,2,1,0:T(8,128)(2,1)S(1)}, bf16[2,2,128,256]{3,2,1,0:T(8,128)(2,1)S(1)}, u32[]{:S(2)}, u32[]{:S(2)}) %collective-permute-start.20) | collective-permute-done | bytes 262176 | tf_op jit(solution)/shard_map/ppermute | solution.py:211
  101.4 1.5 %collective-permute-start.13 = (bf16[2,2,128,256]{3,2,1,0:T(8,128)(2,1)S(1)}, bf16[2,2,128,256]{3,2,1,0:T(8,128)(2,1)S(1)}, u32[]{:S(2)}, u32[]{:S(2)}) collective-permute-start(bf16[2,2,128,256]{3,2,1,0:T(8,128)(2,1)S(1)} %collective-permute-done.9.refs_3_), channel_id=1, source_target_pairs={{0,2},{2,0},{4,6},{6,4},{8,10},{10,8},{12,14},{14,12},{1,3},{3,1},... | collective-permute-start | bytes 786440 | tf_op jit(solution)/shard_map/ppermute | solution.py:211
  102.8 4.1 %collective-permute-done.18.refs_5_ = bf16[2,2,128,256]{3,2,1,0:T(8,128)(2,1)S(1)} collective-permute-done((bf16[2,2,128,256]{3,2,1,0:T(8,128)(2,1)S(1)}, bf16[2,2,128,256]{3,2,1,0:T(8,128)(2,1)S(1)}, u32[]{:S(2)}, u32[]{:S(2)}) %collective-permute-start.18) | collective-permute-done | bytes 262176 | tf_op jit(solution)/shard_map/ppermute | solution.py:211
  107.0 1.5 %collective-permute-start.12 = (bf16[2,2,128,256]{3,2,1,0:T(8,128)(2,1)S(1)}, bf16[2,2,128,256]{3,2,1,0:T(8,128)(2,1)S(1)}, u32[]{:S(2)}, u32[]{:S(2)}) collective-permute-start(bf16[2,2,128,256]{3,2,1,0:T(8,128)(2,1)S(1)} %collective-permute-done.8.refs_2_), channel_id=1, source_target_pairs={{0,2},{2,0},{4,6},{6,4},{8,10},{10,8},{12,14},{14,12},{1,3},{3,1},... | collective-permute-start | bytes 786440 | tf_op jit(solution)/shard_map/ppermute | solution.py:211
  108.5 4.1 %collective-permute-done.19.refs_6_ = bf16[2,2,128,256]{3,2,1,0:T(8,128)(2,1)S(1)} collective-permute-done((bf16[2,2,128,256]{3,2,1,0:T(8,128)(2,1)}, bf16[2,2,128,256]{3,2,1,0:T(8,128)(2,1)S(1)}, u32[]{:S(2)}, u32[]{:S(2)}) %collective-permute-start.19) | collective-permute-done | bytes 262176 | tf_op jit(solution)/shard_map/ppermute | solution.py:211
  112.6 1.5 %collective-permute-start.11 = (bf16[2,2,128,256]{3,2,1,0:T(8,128)(2,1)S(1)}, bf16[2,2,128,256]{3,2,1,0:T(8,128)(2,1)S(1)}, u32[]{:S(2)}, u32[]{:S(2)}) collective-permute-start(bf16[2,2,128,256]{3,2,1,0:T(8,128)(2,1)S(1)} %collective-permute-done.7.refs_1_), channel_id=1, source_target_pairs={{0,2},{2,0},{4,6},{6,4},{8,10},{10,8},{12,14},{14,12},{1,3},{3,1},... | collective-permute-start | bytes 786440 | tf_op jit(solution)/shard_map/ppermute | solution.py:211
  114.1 10.5 %dress.2.refs_8_ = bf16[4,3,2,128,1024]{4,3,2,1,0:T(8,128)(2,1)} custom-call(s32[7]{0:T(128)S(1)} %stack.28.place, s32[2]{0:T(128)S(1)} %get-tuple-element.26.other_src, s32[2]{0:T(128)S(1)} %get-tuple-element.25.other_snk, bf16[8,3,32,512]{3,2,1,0:T(8,128)(2,1)S(1)} %pad_maximum_fusion.own, bf16[8,3,32,512]{3,2,1,0:T(8,128)(2,1)S(1)} %collective-permute-done.6.oth, ...), custom_call_target="tpu_custom_call" | custom-call | flops 3221225472 | bytes 2097152 | tf_op jit(solution)/shard_map/dress/pallas_call | solution.py:189
  124.6 0.0 collective-permute-done.10.refs_4_
  124.6 1.1 collective-permute-done.11.refs_5_
  125.8 9.6 %dress.3 = bf16[4,3,2,128,1024]{4,3,2,1,0:T(8,128)(2,1)} custom-call(s32[7]{0:T(128)S(1)} %stack.28.place, s32[2]{0:T(128)S(1)} %get-tuple-element.28.other_src, s32[2]{0:T(128)S(1)} %get-tuple-element.27.other_snk, bf16[8,3,32,512]{3,2,1,0:T(8,128)(2,1)S(1)} %pad_maximum_fusion.own, ...), custom_call_target="tpu_custom_call", output_to_operand_aliasing={{}: (13, {})} | custom-call | flops 3221225472 | bytes 2097152 | tf_op jit(solution)/shard_map/dress/pallas_call | solution.py:189
  (13 shorter events, 0.1 us)
Async XLA Ops:
  0.0 91.0 %copy-start.2 = (s32[4,2]{0,1:T(2,128)S(1)}, s32[4,2]{0,1:T(2,128)}, u32[]{:S(2)}) copy-start(s32[4,2]{0,1:T(2,128)} %param.6) | copy-start | bytes 100
  0.1 1.1 copy-start
  1.2 0.7 copy-start.1
  4.2 12.2 %collective-permute-start = (bf16[3,128,512]{2,1,0:T(8,128)(2,1)S(1)}, bf16[3,128,512]{2,1,0:T(8,128)(2,1)S(1)}, u32[]{:S(2)}, u32[]{:S(2)}) collective-permute-start(bf16[3,128,512]{2,1,0:T(8,128)(2,1)S(1)} %get-tuple-element.12), channel_id=1, source_target_pairs={{0,4},{2,6},{4,0},{6,2},{8,12},{10,14},{12,8},{14,10},{1,5},{3,7},... | collective-permute-start | bytes 1179656 | tf_op jit(solution)/shard_map/ppermute | solution.py:211
  17.0 6.2 %collective-permute-start.1 = (bf16[3,64,512]{2,1,0:T(8,128)(2,1)S(1)}, bf16[3,64,512]{2,1,0:T(8,128)(2,1)S(1)}, u32[]{:S(2)}, u32[]{:S(2)}) collective-permute-start(bf16[3,64,512]{2,1,0:T(8,128)(2,1)S(1)} %get-tuple-element.14), channel_id=1, source_target_pairs={{0,2},{2,0},{4,6},{6,4},{8,10},{10,8},{12,14},{14,12},{1,3},{3,1},... | collective-permute-start | bytes 589832 | tf_op jit(solution)/shard_map/ppermute | solution.py:211
  23.8 6.6 %collective-permute-start.2 = (bf16[3,32,512]{2,1,0:T(8,128)(2,1)S(1)}, bf16[3,32,512]{2,1,0:T(8,128)(2,1)S(1)}, u32[]{:S(2)}, u32[]{:S(2)}) collective-permute-start(bf16[3,32,512]{2,1,0:T(8,128)(2,1)S(1)} %get-tuple-element.16), channel_id=1, source_target_pairs={{0,8},{2,10},{4,12},{6,14},{8,0},{10,2},{12,4},{14,6},{1,9},{3,11}... | collective-permute-start | bytes 294920 | tf_op jit(solution)/shard_map/ppermute | solution.py:211
  30.4 5.6 %collective-permute-start.3 = (bf16[1,3,32,512]{3,2,1,0:T(8,128)(2,1)S(1)}, bf16[1,3,32,512]{3,2,1,0:T(8,128)(2,1)S(1)}, u32[]{:S(2)}, u32[]{:S(2)}) collective-permute-start(bf16[1,3,32,512]{3,2,1,0:T(8,128)(2,1)S(1)} %fusion), channel_id=1, source_target_pairs={{0,8},{2,10},{4,12},{6,14},{8,0},{10,2},{12,4},{14,6},{1,9},{3,11}... | collective-permute-start | bytes 294920 | tf_op jit(solution)/shard_map/ppermute | solution.py:211
  36.0 5.7 %collective-permute-start.4 = (bf16[2,3,32,512]{3,2,1,0:T(8,128)(2,1)S(1)}, bf16[2,3,32,512]{3,2,1,0:T(8,128)(2,1)S(1)}, u32[]{:S(2)}, u32[]{:S(2)}) collective-permute-start(bf16[2,3,32,512]{3,2,1,0:T(8,128)(2,1)S(1)} %pad_maximum_fusion.2), channel_id=1, source_target_pairs={{0,2},{2,0},{4,6},{6,4},{8,10},{10,8},{12,14},{14,12},{1,3},{3,1},... | collective-permute-start | bytes 589832 | tf_op jit(solution)/shard_map/ppermute | solution.py:211
  41.8 13.8 %collective-permute-start.5 = (bf16[4,3,32,512]{3,2,1,0:T(8,128)(2,1)S(1)}, bf16[4,3,32,512]{3,2,1,0:T(8,128)(2,1)S(1)}, u32[]{:S(2)}, u32[]{:S(2)}) collective-permute-start(bf16[4,3,32,512]{3,2,1,0:T(8,128)(2,1)S(1)} %pad_maximum_fusion.1), channel_id=1, source_target_pairs={{0,4},{2,6},{4,0},{6,2},{8,12},{10,14},{12,8},{14,10},{1,5},{3,7},... | collective-permute-start | bytes 1179656 | tf_op jit(solution)/shard_map/ppermute | solution.py:211
  46.8 15.9 %collective-permute-start.16 = (bf16[2,2,128,256]{3,2,1,0:T(8,128)(2,1)S(1)}, bf16[2,2,128,256]{3,2,1,0:T(8,128)(2,1)S(1)}, u32[]{:S(2)}, u32[]{:S(2)}) collective-permute-start(bf16[2,2,128,256]{3,2,1,0:T(8,128)(2,1)S(1)} %get-tuple-element.17), channel_id=1, source_target_pairs={{0,12},{2,14},{4,8},{6,10},{8,4},{10,6},{12,0},{14,2},{1,13},{3,15... | collective-permute-start | bytes 786440 | tf_op jit(solution)/shard_map/ppermute | solution.py:211
  49.2 21.3 %collective-permute-start.9 = (bf16[2,2,128,256]{3,2,1,0:T(8,128)(2,1)S(1)}, bf16[2,2,128,256]{3,2,1,0:T(8,128)(2,1)S(1)}, u32[]{:S(2)}, u32[]{:S(2)}) collective-permute-start(bf16[2,2,128,256]{3,2,1,0:T(8,128)(2,1)S(1)} %get-tuple-element.18), channel_id=1, source_target_pairs={{0,12},{2,14},{4,8},{6,10},{8,4},{10,6},{12,0},{14,2},{1,13},{3,15... | collective-permute-start | bytes 786440 | tf_op jit(solution)/shard_map/ppermute | solution.py:211
  55.7 58.4 %collective-permute-start.6 = (bf16[8,3,32,512]{3,2,1,0:T(8,128)(2,1)S(1)}, bf16[8,3,32,512]{3,2,1,0:T(8,128)(2,1)S(1)}, u32[]{:S(2)}, u32[]{:S(2)}) collective-permute-start(bf16[8,3,32,512]{3,2,1,0:T(8,128)(2,1)S(1)} %pad_maximum_fusion.own), channel_id=1, source_target_pairs={{0,1},{1,0},{2,3},{3,2},{4,5},{5,4},{6,7},{7,6},{8,9},{9,8},{10,11... | collective-permute-start | bytes 2359304 | tf_op jit(solution)/shard_map/ppermute | solution.py:211
  55.8 30.8 %collective-permute-start.8 = (bf16[2,2,128,256]{3,2,1,0:T(8,128)(2,1)}, bf16[2,2,128,256]{3,2,1,0:T(8,128)(2,1)S(1)}, u32[]{:S(2)}, u32[]{:S(2)}) collective-permute-start(bf16[2,2,128,256]{3,2,1,0:T(8,128)(2,1)} %get-tuple-element.19), channel_id=1, source_target_pairs={{0,8},{2,10},{4,12},{6,14},{8,0},{10,2},{12,4},{14,6},{1,9},{3,11}... | collective-permute-start | bytes 786440 | tf_op jit(solution)/shard_map/ppermute | solution.py:211
  56.5 31.6 %collective-permute-start.7 = (bf16[2,2,128,256]{3,2,1,0:T(8,128)(2,1)}, bf16[2,2,128,256]{3,2,1,0:T(8,128)(2,1)S(1)}, u32[]{:S(2)}, u32[]{:S(2)}) collective-permute-start(bf16[2,2,128,256]{3,2,1,0:T(8,128)(2,1)} %get-tuple-element.20), channel_id=1, source_target_pairs={{0,4},{2,6},{4,0},{6,2},{8,12},{10,14},{12,8},{14,10},{1,5},{3,7},... | collective-permute-start | bytes 786440 | tf_op jit(solution)/shard_map/ppermute | solution.py:211
  62.7 25.9 %collective-permute-start.14 = (bf16[2,2,128,256]{3,2,1,0:T(8,128)(2,1)}, bf16[2,2,128,256]{3,2,1,0:T(8,128)(2,1)S(1)}, u32[]{:S(2)}, u32[]{:S(2)}) collective-permute-start(bf16[2,2,128,256]{3,2,1,0:T(8,128)(2,1)} %get-tuple-element.22), channel_id=1, source_target_pairs={{0,4},{2,6},{4,0},{6,2},{8,12},{10,14},{12,8},{14,10},{1,5},{3,7},... | collective-permute-start | bytes 786440 | tf_op jit(solution)/shard_map/ppermute | solution.py:211
  70.5 19.6 %collective-permute-start.15 = (bf16[2,2,128,256]{3,2,1,0:T(8,128)(2,1)}, bf16[2,2,128,256]{3,2,1,0:T(8,128)(2,1)}, u32[]{:S(2)}, u32[]{:S(2)}) collective-permute-start(bf16[2,2,128,256]{3,2,1,0:T(8,128)(2,1)} %get-tuple-element.24), channel_id=1, source_target_pairs={{0,8},{2,10},{4,12},{6,14},{8,0},{10,2},{12,4},{14,6},{1,9},{3,11}... | collective-permute-start | bytes 786440 | tf_op jit(solution)/shard_map/ppermute | solution.py:211
  86.6 9.2 %collective-permute-start.17 = (bf16[2,2,128,256]{3,2,1,0:T(8,128)(2,1)S(1)}, bf16[2,2,128,256]{3,2,1,0:T(8,128)(2,1)S(1)}, u32[]{:S(2)}, u32[]{:S(2)}) collective-permute-start(bf16[2,2,128,256]{3,2,1,0:T(8,128)(2,1)S(1)} %get-tuple-element.23.refs_0_), channel_id=1, source_target_pairs={{0,2},{2,0},{4,6},{6,4},{8,10},{10,8},{12,14},{14,12},{1,3},{3,1},... | collective-permute-start | bytes 786440 | tf_op jit(solution)/shard_map/ppermute | solution.py:211
  88.1 13.3 %collective-permute-start.20 = (bf16[2,2,128,256]{3,2,1,0:T(8,128)(2,1)S(1)}, bf16[2,2,128,256]{3,2,1,0:T(8,128)(2,1)S(1)}, u32[]{:S(2)}, u32[]{:S(2)}) collective-permute-start(bf16[2,2,128,256]{3,2,1,0:T(8,128)(2,1)S(1)} %collective-permute-done.16.refs_3_), channel_id=1, source_target_pairs={{0,2},{2,0},{4,6},{6,4},{8,10},{10,8},{12,14},{14,12},{1,3},{3,1},... | collective-permute-start | bytes 786440 | tf_op jit(solution)/shard_map/ppermute | solution.py:211
  88.6 18.4 %collective-permute-start.18 = (bf16[2,2,128,256]{3,2,1,0:T(8,128)(2,1)S(1)}, bf16[2,2,128,256]{3,2,1,0:T(8,128)(2,1)S(1)}, u32[]{:S(2)}, u32[]{:S(2)}) collective-permute-start(bf16[2,2,128,256]{3,2,1,0:T(8,128)(2,1)S(1)} %collective-permute-done.14.refs_1_), channel_id=1, source_target_pairs={{0,2},{2,0},{4,6},{6,4},{8,10},{10,8},{12,14},{14,12},{1,3},{3,1},... | collective-permute-start | bytes 786440 | tf_op jit(solution)/shard_map/ppermute | solution.py:211
  90.1 22.5 %collective-permute-start.19 = (bf16[2,2,128,256]{3,2,1,0:T(8,128)(2,1)}, bf16[2,2,128,256]{3,2,1,0:T(8,128)(2,1)S(1)}, u32[]{:S(2)}, u32[]{:S(2)}) collective-permute-start(bf16[2,2,128,256]{3,2,1,0:T(8,128)(2,1)} %collective-permute-done.15.refs_2_), channel_id=1, source_target_pairs={{0,2},{2,0},{4,6},{6,4},{8,10},{10,8},{12,14},{14,12},{1,3},{3,1},... | collective-permute-start | bytes 786440 | tf_op jit(solution)/shard_map/ppermute | solution.py:211
  95.8 28.9 %collective-permute-start.10 = (bf16[2,2,128,256]{3,2,1,0:T(8,128)(2,1)S(1)}, bf16[2,2,128,256]{3,2,1,0:T(8,128)(2,1)S(1)}, u32[]{:S(2)}, u32[]{:S(2)}) collective-permute-start(bf16[2,2,128,256]{3,2,1,0:T(8,128)(2,1)S(1)} %get-tuple-element.21.refs_0_), channel_id=1, source_target_pairs={{0,2},{2,0},{4,6},{6,4},{8,10},{10,8},{12,14},{14,12},{1,3},{3,1},... | collective-permute-start | bytes 786440 | tf_op jit(solution)/shard_map/ppermute | solution.py:211
  101.4 23.3 %collective-permute-start.13 = (bf16[2,2,128,256]{3,2,1,0:T(8,128)(2,1)S(1)}, bf16[2,2,128,256]{3,2,1,0:T(8,128)(2,1)S(1)}, u32[]{:S(2)}, u32[]{:S(2)}) collective-permute-start(bf16[2,2,128,256]{3,2,1,0:T(8,128)(2,1)S(1)} %collective-permute-done.9.refs_3_), channel_id=1, source_target_pairs={{0,2},{2,0},{4,6},{6,4},{8,10},{10,8},{12,14},{14,12},{1,3},{3,1},... | collective-permute-start | bytes 786440 | tf_op jit(solution)/shard_map/ppermute | solution.py:211
  107.0 17.6 %collective-permute-start.12 = (bf16[2,2,128,256]{3,2,1,0:T(8,128)(2,1)S(1)}, bf16[2,2,128,256]{3,2,1,0:T(8,128)(2,1)S(1)}, u32[]{:S(2)}, u32[]{:S(2)}) collective-permute-start(bf16[2,2,128,256]{3,2,1,0:T(8,128)(2,1)S(1)} %collective-permute-done.8.refs_2_), channel_id=1, source_target_pairs={{0,2},{2,0},{4,6},{6,4},{8,10},{10,8},{12,14},{14,12},{1,3},{3,1},... | collective-permute-start | bytes 786440 | tf_op jit(solution)/shard_map/ppermute | solution.py:211
  112.6 13.2 %collective-permute-start.11 = (bf16[2,2,128,256]{3,2,1,0:T(8,128)(2,1)S(1)}, bf16[2,2,128,256]{3,2,1,0:T(8,128)(2,1)S(1)}, u32[]{:S(2)}, u32[]{:S(2)}) collective-permute-start(bf16[2,2,128,256]{3,2,1,0:T(8,128)(2,1)S(1)} %collective-permute-done.7.refs_1_), channel_id=1, source_target_pairs={{0,2},{2,0},{4,6},{6,4},{8,10},{10,8},{12,14},{14,12},{1,3},{3,1},... | collective-permute-start | bytes 786440 | tf_op jit(solution)/shard_map/ppermute | solution.py:211

commit v2 on v0

--- a/solution.py
+++ b/solution.py
@@ -1,11 +1,378 @@
+import functools
 import math
 
 import jax
 import jax.numpy as jnp
 from jax import lax
+from jax.experimental import pallas as pl
+from jax.experimental.pallas import tpu as pltpu
 from jax.sharding import PartitionSpec as P
 
 LX = 64
+LX_BITS = LX.bit_length() - 1
+F32, BF16 = jnp.float32, jnp.bfloat16
+SPACE, X, Z, Z_LOW, Z_HIGH, HERE_A, HERE_B = range(7)
+VMEM_LIMIT = 24 * 1024 * 1024
+CUT_VMEM = 24 * 1024 * 1024
+
+
+def params(steps=0):
+    return pltpu.CompilerParams(
+        vmem_limit_bytes=VMEM_LIMIT, dimension_semantics=("arbitrary",) * steps or None
+    )
+
+
+def cost(flops, bytes_accessed):
+    return pl.CostEstimate(flops=int(flops), bytes_accessed=int(bytes_accessed), transcendentals=0)
+
+
+def gram_kernel(factor, place, momenta, eig, send_a, send_b, keep_a, keep_b, phased, total):
+    colors, sites, vectors = eig.shape[1:]
+    moms, half = send_a.shape[:2]
+    site = place[SPACE] * sites + lax.broadcasted_iota(jnp.int32, (sites, 128), 0)
+    lane = lax.broadcasted_iota(jnp.int32, (sites, 128), 1)
+    coords = (site & (LX - 1), (site >> LX_BITS) & (LX - 1), site >> (2 * LX_BITS))
+    wave = jnp.zeros((sites, 128), jnp.int32)
+    for m in range(moms):
+        mine = sum(momenta[m, j] * coords[j] for j in range(3))
+        wave = jnp.where(lane == m, mine, wave)
+    angle = (wave & (LX - 1)).astype(F32) * F32(2.0 * math.pi / LX)
+    cosine, sine = jnp.cos(angle), jnp.sin(angle)
+    rows = colors * sites
+    both = eig[...].reshape(2 * rows, vectors)
+    for m in range(moms):
+        c, s = cosine[:, m : m + 1], sine[:, m : m + 1]
+        for color in range(colors):
+            re, im = eig[0, color].astype(F32), eig[1, color].astype(F32)
+            wave_re, wave_im = c * re + s * im, c * im - s * re
+            at = color * sites
+            phased[at : at + sites, :vectors] = wave_re.astype(BF16)
+            phased[at : at + sites, vectors:] = wave_im.astype(BF16)
+            at += rows
+            phased[at : at + sites, :vectors] = wave_im.astype(BF16)
+            phased[at : at + sites, vectors:] = (-wave_re).astype(BF16)
+        total[...] = factor * lax.dot_general(
+            both, phased[...], (((0,), (0,)), ((), ())), preferred_element_type=F32
+        )
+        for send, keep, bit, lanes in (
+            (send_a, keep_a, place[X], slice(None, vectors)),
+            (send_b, keep_b, place[Z_LOW], slice(vectors, None)),
+        ):
+            send[m] = total[pl.ds(pl.multiple_of((1 - bit) * half, half), half), lanes].astype(BF16)
+            keep[m] = total[pl.ds(pl.multiple_of(bit * half, half), half), lanes]
+
+
+def gram_halves(eig, momenta, place, factor):
+    _, colors, sites, vectors = eig.shape
+    moms = momenta.shape[0]
+    shape = (moms, vectors // 2, vectors)
+    smem = pl.BlockSpec(memory_space=pltpu.SMEM)
+    vmem = pl.BlockSpec(memory_space=pltpu.VMEM)
+    return pl.pallas_call(
+        functools.partial(gram_kernel, factor),
+        out_shape=[jax.ShapeDtypeStruct(shape, kind) for kind in (BF16, BF16, F32, F32)],
+        in_specs=[smem, smem, vmem],
+        out_specs=[vmem] * 4,
+        scratch_shapes=[
+            pltpu.VMEM((2 * colors * sites, 2 * vectors), BF16),
+            pltpu.VMEM((vectors, 2 * vectors), F32),
+        ],
+        compiler_params=params(),
+        cost_estimate=cost(4 * colors * sites * vectors * moms * 2 * vectors, 3 * 2**20),
+        name="gram",
+    )(place, momenta, eig)
+
+
+def cut_kernel(plan, place, panels, *refs):
+    cuts, sems = refs[:-1], refs[-1]
+    vectors = cuts[0].shape[3]
+    copies = []
+    for i, (d, first, _) in enumerate(plan):
+        lanes = pl.ds(pl.multiple_of((place[Z] ^ d) * vectors, vectors), vectors)
+        source = panels.at[first : first + cuts[i].shape[0], :, :, lanes]
+        copies.append(pltpu.make_async_copy(source, cuts[i], sems.at[i]))
+        copies[-1].start()
+    for copy in copies:
+        copy.wait()
+
+
+def cut_panels(panels, vectors, plan, vmem, place):
+    cuts = pl.pallas_call(
+        functools.partial(cut_kernel, plan),
+        out_shape=[jax.ShapeDtypeStruct((size, *panels.shape[1:3], vectors), BF16) for _, _, size in plan],
+        in_specs=[pl.BlockSpec(memory_space=pltpu.SMEM), pl.BlockSpec(memory_space=pl.ANY)],
+        out_specs=[pl.BlockSpec(memory_space=pltpu.VMEM)] * len(plan),
+        scratch_shapes=[pltpu.SemaphoreType.DMA((len(plan),))],
+        compiler_params=pltpu.CompilerParams(vmem_limit_bytes=vmem),
+        cost_estimate=cost(0, 4 * panels.size),
+        name="cut",
+    )(place, panels)
+    return {(d, first // size): cut for (d, first, size), cut in zip(plan, cuts)}
+
+
+def fold_kernel(place, keep_a, keep_b, came_a, came_b, send_a, send_b, left_a, left_b):
+    half = send_a.shape[1]
+    for keep, came, bit, send, left in (
+        (keep_a, came_a, place[Z_LOW], send_a, left_a),
+        (keep_b, came_b, place[X], send_b, left_b),
+    ):
+        own = pl.ds(pl.multiple_of(bit * half, half), half)
+        off = pl.ds(pl.multiple_of((1 - bit) * half, half), half)
+        left[...] = keep[:, own, :] + came[:, own, :].astype(F32)
+        send[...] = (keep[:, off, :] + came[:, off, :].astype(F32)).astype(BF16)
+
+
+def join_kernel(place, keep_a, keep_b, came_a, came_b, send, left):
+    half, width = send.shape[1:]
+    bit = place[Z_HIGH]
+    own = pl.ds(pl.multiple_of(bit * half, half), half)
+    off = pl.ds(pl.multiple_of((1 - bit) * half, half), half)
+    for keep, came, lanes in (
+        (keep_a, came_a, slice(None, width // 2)),
+        (keep_b, came_b, slice(width // 2, None)),
+    ):
+        left[:, :, lanes] = keep[:, own, :] + came[:, own, :].astype(F32)
+        send[:, :, lanes] = (keep[:, off, :] + came[:, off, :].astype(F32)).astype(BF16)
+
+
+def fold(kernel, keep_a, keep_b, came_a, came_b, place):
+    moms, rows, width = keep_a.shape
+    if kernel is join_kernel:
+        shape, kinds = (moms, rows // 2, 2 * width), (BF16, F32)
+    else:
+        shape, kinds = (moms, rows // 2, width), (BF16, BF16, F32, F32)
+    vmem = pl.BlockSpec(memory_space=pltpu.VMEM)
+    return pl.pallas_call(
+        kernel,
+        out_shape=[jax.ShapeDtypeStruct(shape, kind) for kind in kinds],
+        in_specs=[pl.BlockSpec(memory_space=pltpu.SMEM)] + [vmem] * 4,
+        out_specs=[vmem] * len(kinds),
+        compiler_params=params(),
+        cost_estimate=cost(2 * keep_a.size, 16 * keep_a.size),
+        name="fold",
+    )(place, keep_a, keep_b, came_a, came_b)
+
+
+def prepare_kernel(place, own_a, own_b, oth_a, oth_b, left, sink):
+    pieces, moms, piece_rows, vectors = own_a.shape
+    columns = left.shape[1] // (2 * moms)
+    here_a, here_b, x = place[HERE_A], place[HERE_B], place[X]
+    for t, (part_a, part_b) in enumerate(((own_a, own_b), (oth_a, oth_b))):
+        for m in range(moms):
+            for i in range(columns // piece_rows):
+                q = x * (columns // piece_rows) + i
+                re, im = part_a[q ^ here_a, m], part_b[q ^ here_b, m]
+                at = 2 * m * columns + i * piece_rows
+                left[t, at : at + piece_rows, :vectors] = re
+                left[t, at : at + piece_rows, vectors:] = im
+                at += columns
+                left[t, at : at + piece_rows, :vectors] = -im
+                left[t, at : at + piece_rows, vectors:] = re
+            for q in range(pieces):
+                at = q * piece_rows
+                sink[t, m, at : at + piece_rows] = part_a[here_a ^ q, m]
+                sink[t, m, vectors + at : vectors + at + piece_rows] = part_b[here_b ^ q, m]
+
+
+def prepare(own, oth, columns, place):
+    pieces, moms, piece_rows, vectors = own[0].shape
+    vmem = pl.BlockSpec(memory_space=pltpu.VMEM)
+    return pl.pallas_call(
+        prepare_kernel,
+        out_shape=(
+            jax.ShapeDtypeStruct((2, 2 * moms * columns, 2 * vectors), BF16),
+            jax.ShapeDtypeStruct((2, moms, 2 * vectors, vectors), BF16),
+        ),
+        in_specs=[pl.BlockSpec(memory_space=pltpu.SMEM)] + [vmem] * 4,
+        out_specs=(vmem, vmem),
+        compiler_params=params(),
+        cost_estimate=cost(0, 16 * own[0].size),
+        name="prepare",
+    )(place, *own, *oth)
+
+
+def dress_kernel(dists, chained, first_pair, place, other_src, other_snk, left, sink, *refs):
+    count = len(dists)
+    mine, near = refs[:count], refs[count : 2 * count]
+    out, panel, done, sems = refs[2 * count + chained :]
+    moms, width, vectors = sink.shape[1:]
+    columns = out.shape[3]
+    pair, last = pl.program_id(0), pl.num_programs(0) - 1
+    x, z = place[X], place[Z]
+    src, snk = other_src[pair], other_snk[pair]
+    block = mine[0].shape[2]
+
+    def store(k, of_pair):
+        lanes = pl.ds(pl.multiple_of((z ^ dists[k]) * vectors, vectors), vectors)
+        return pltpu.make_async_copy(done.at[k], out.at[of_pair + first_pair, :, :, :, lanes], sems.at[k])
+
+    for k in range(count):
+        at_mine = pl.ds(pl.multiple_of(k * vectors + x * block, block), block)
+        at_near = pl.ds(pl.multiple_of(k * vectors + (1 - x) * block, block), block)
+        for part in range(2):
+            lanes = slice(part * vectors, (part + 1) * vectors)
+            panel[at_mine, lanes] = mine[k][0, part]
+            panel[at_near, lanes] = near[k][0, part]
+
+    contract = (((1,), (1,)), ((), ()))
+    right = lax.dot_general(left[src], panel[...], contract, preferred_element_type=F32).astype(BF16)
+    for k in range(count):
+        at = slice(k * vectors, (k + 1) * vectors)
+
+        @pl.when(pair > 0)
+        def _(k=k):
+            store(k, pair - 1).wait()
+
+        for m in range(moms):
+            rows = right[2 * m * columns : 2 * (m + 1) * columns, at]
+            both = lax.dot_general(rows, sink[snk, m], contract, preferred_element_type=F32)
+            done[k, m, 0] = (both[:columns, :vectors] - both[columns:, vectors:]).astype(BF16)
+            done[k, m, 1] = (both[:columns, vectors:] + both[columns:, :vectors]).astype(BF16)
+        store(k, pair).start()
+
+    @pl.when(pair == last)
+    def _():
+        for k in range(count):
+            store(k, pair).wait()
+
+
+def dress(out, out_shape, first_pair, pairs, dists, mine, near, left, sink, place, other_src, other_snk):
+    _, _, block, vectors = mine[0][0].shape
+    count = len(mine)
+    moms = sink.shape[1]
+    columns = out_shape.shape[3]
+    whole = pl.BlockSpec(memory_space=pltpu.VMEM)
+    chunks = [
+        pl.BlockSpec((1, 2, block, vectors), lambda p, *_, first=first: (p + first, 0, 0, 0))
+        for _, first in (*mine, *near)
+    ]
+    chained = out is not None
+    operands = [left, sink, *(part for part, _ in (*mine, *near))] + ([out] if chained else [])
+    in_specs = [whole, whole] + chunks + [pl.BlockSpec(memory_space=pl.ANY)] * chained
+    macs = pairs * count * 2 * (2 * moms * columns) * (2 * vectors) * vectors
+    return pl.pallas_call(
+        functools.partial(dress_kernel, dists, chained, first_pair),
+        out_shape=out_shape,
+        grid_spec=pltpu.PrefetchScalarGridSpec(
+            num_scalar_prefetch=3,
+            grid=(pairs,),
+            in_specs=in_specs,
+            out_specs=pl.BlockSpec(memory_space=pl.ANY),
+            scratch_shapes=[
+                pltpu.VMEM((count * 2 * block, 2 * vectors), BF16),
+                pltpu.VMEM((count, moms, 2, columns, vectors), BF16),
+                pltpu.SemaphoreType.DMA((count,)),
+            ],
+        ),
+        input_output_aliases={3 + len(operands) - 1: 0} if chained else {},
+        compiler_params=params(1),
+        cost_estimate=cost(2 * macs, 2**21),
+        name="dress",
+    )(place, other_src[first_pair : first_pair + pairs], other_snk[first_pair : first_pair + pairs], *operands)
+
+
+CHUNKS = (1, 2, 2, 2)
+HOOKS = [[], [('z', 3, 0)], [('x', 0, 0)], [], [('x', 3, 0), ('z', 1, 0)], [('z', 3, 1)], [('z', 2, 0), ('x', 1, 0), ('x', 3, 1)]]
+CALLS = ((0, 2, (0, 1, 2, 3)), (2, 2, (0, 1, 2, 3)))
+GATES = {}
+AFTER = {}
+FROM = {}
+
+
+def exchange(value, axis, mask, among=lambda i: True):
+    return lax.ppermute(value, axis, [(i, i ^ mask) for i in range(lax.axis_size(axis)) if among(i)])
+
+
+def fast(eigvecs, momenta, pair_list, panels):
+    vectors = eigvecs.shape[4]
+    pair_count, _, rows, width = panels.shape
+    moms = momenta.shape[0]
+    space_count = lax.axis_size("space")
+    spins = width // vectors
+    space = lax.axis_index("space")
+    tm = lax.axis_index("tm")
+    x, z = space & 1, space >> 1
+    low, high = z & 1, z >> 1
+    place = jnp.stack(
+        [space, x, z, low, high, x * 4 + low * 2 + high, low * 4 + x * 2 + high]
+    ).astype(jnp.int32)
+    other = (pair_list != tm).astype(jnp.int32)
+    other_src, other_snk = other[:, 0], other[:, 1]
+
+    factor = 1.0 / math.sqrt(6.0 * eigvecs.shape[3] * space_count * vectors)
+    plan = [
+        (d, c * (pair_count // n), pair_count // n) for d, n in enumerate(CHUNKS) for c in range(n)
+    ]
+    send_a, send_b, keep_a, keep_b = gram_halves(eigvecs[0], momenta, place, factor)
+    blocks = cut_panels(panels, vectors, plan, CUT_VMEM, place)
+
+    raw, held, steps = {}, {}, []
+
+    def fetch(name):
+        if name not in raw:
+            hop, d, c = name
+            value = blocks[d, c] if hop == "z" or d == 0 else fetch(("z", d, c))
+            if name in FROM:
+                value, _ = lax.optimization_barrier((value, steps[FROM[name]]))
+            raw[name] = exchange(meet(value, AFTER.get(name)), "space", 2 * d if hop == "z" else 1)
+        held.setdefault(name, raw[name])
+        return raw[name]
+
+    def meet(value, names):
+        if not names:
+            return value
+        for name in names:
+            fetch(name)
+        value, *came = lax.optimization_barrier((value, *(held[name] for name in names)))
+        held.update(zip(names, came))
+        return value
+
+    along_x, low_z, high_z = 1, 2, 4
+
+    def step(*sends):
+        came = [exchange(value, "space", mask) for value, mask in sends]
+        came[0] = meet(came[0], HOOKS[len(steps)])
+        steps.append(came[0])
+        return came
+
+    came = step((send_a, along_x), (send_b, low_z))
+    send_a, send_b, keep_a, keep_b = fold(fold_kernel, keep_a, keep_b, *came, place)
+    came = step((send_a, low_z), (send_b, along_x))
+    send, keep = fold(join_kernel, keep_a, keep_b, *came, place)
+    (came,) = step((send, high_z))
+    field = (keep + came.astype(F32)).astype(BF16)[None]
+    (came,) = step((field, high_z))
+    field = jnp.concatenate([field, came], 0)
+    parts = [field[..., :vectors], field[..., vectors:]]
+    came = step((parts[0], low_z), (parts[1], along_x))
+    parts = [jnp.concatenate([part, new], 0) for part, new in zip(parts, came)]
+    came = step((parts[0], along_x), (parts[1], low_z))
+    own = [jnp.concatenate([part, new], 0) for part, new in zip(parts, came)]
+    oth = [exchange(part, "tm", 1) for part in own]
+    oth[0] = meet(oth[0], HOOKS[6])
+
+    columns = width // space_count
+    out_shape = jax.ShapeDtypeStruct((pair_count, moms, 2, columns, width), BF16)
+
+    def part(hop, d, first):
+        c, at = divmod(first, pair_count // CHUNKS[d])
+        if (hop, d) == ("z", 0):
+            return blocks[0, c], at
+        fetch((hop, d, c))
+        return held[hop, d, c], at
+
+    left, sink = prepare(own, oth, columns, place)
+    out = None
+    for call, (first, pairs, dists) in enumerate(CALLS):
+        for _, d, c in GATES.get(call, ()):
+            value, out = lax.optimization_barrier((fetch(("z", d, c)), out))
+            raw["z", d, c] = held["z", d, c] = value
+        mine = [part("z", d, first) for d in dists]
+        near = [part("x", d, first) for d in dists]
+        out = dress(
+            out, out_shape, first, pairs, dists, mine, near, left, sink, place, other_src, other_snk
+        )
+    return out
 
 
 def phased_block(cosine, sine_part, real_part, imag_part):
@@ -18,7 +385,7 @@
     return jnp.stack([upper, lower], -4).astype(jnp.bfloat16)
 
 
-def local(eigvecs, momenta, pair_list, panels):
+def general(eigvecs, momenta, pair_list, panels):
     slice_count, _, colors, slab_sites, vectors = eigvecs.shape
     mom_count = momenta.shape[0]
     space_count = lax.axis_size("space")
@@ -90,6 +457,26 @@
     return dressed.reshape(pair_count, mom_count, 2, column_count, panel_width).astype(jnp.bfloat16)
 
 
+def local(eigvecs, momenta, pair_list, panels):
+    slices, _, _, sites, vectors = eigvecs.shape
+    pairs, _, rows, width = panels.shape
+    space_count = lax.axis_size("space")
+    spins = width // vectors
+    fits = (
+        slices == 1
+        and lax.axis_size("tm") == 2
+        and space_count == 2 * spins
+        and spins == 4
+        and rows * space_count == width
+        and rows % 128 == 0
+        and (vectors // space_count) % 16 == 0
+        and sites % 16 == 0
+        and pairs % 2 == 0
+        and momenta.shape[0] <= 8
+    )
+    return (fast if fits else general)(eigvecs, momenta, pair_list, panels)
+
+
 def solution(mesh):
     placed = (
         P(("cfg", "tm"), None, None, "space", None),

time: 346 us -> 100 us (0.29)
  waiting for transfers between devices: 126 us -> 37.6 us
  local copies, waits for them, and re-layouts: 90 us -> 1.78 us
  blocking collectives: 82.9 us -> 0 us
  starting transfers between devices: 5.08 us -> 36.5 us
  Pallas kernels: 0 us -> 20.6 us
  matrix products: 14.6 us -> 0 us
  between operations: 13.6 us -> 0.15 us
  other arithmetic: 12 us -> 3.58 us
    all_to_all x1 -> x0, waiting for transfers between devices: 126 us -> none  [local(): lax.all_to_all(right_dressed, 'space', split_axis=3, concat_axis=2, tiled...]
    psum x1 -> x0, blocking collectives: 82.9 us -> none  [local(): summed = lax.psum(gram_local, 'space')]
    reshape x3 -> x0, local copies, waits for them, and re-layouts: 43.4 us -> none  [the longest x1 36.6 us: local(): right_dressed.astype(jnp.bfloat16)]
    ppermute x0 -> x25, waiting for transfers between devices: none -> 37.6 us  [exchange(): lax.ppermute(value, axis, [(i, i ^ mask) for i in range(lax.axis_size(axi...]
    ppermute x0 -> x25, starting transfers between devices: none -> 36.5 us  [exchange(): lax.ppermute(value, axis, [(i, i ^ mask) for i in range(lax.axis_size(axi...]
    pallas_call x0 -> x7, Pallas kernels: none -> 20.6 us  [the longest x2 14.6 us: dress(): pl.pallas_call(functools.partial(dress_kernel, dists, chained, first_pair...]
    all_to_all x2 -> x0, local copies, waits for them, and re-layouts: 15.5 us -> none  [local(): lax.all_to_all(right_dressed, 'space', split_axis=3, concat_axis=2, tiled...]
    dot_general x3 -> x0, matrix products: 14.6 us -> none  [the longest x1 7.2 us: local(): jnp.einsum('pmorajc,pmkrj->pmocak', mixed_parts, sink_fields, preferred_e...]
  transfers between devices with their start and end apart: 2 -> 25, of which waited for: 1 -> 11; matrix products, arithmetic and copies ran while one was open for 7% -> 4% of each run, Pallas kernels for 0% -> 12%
where the time goes in v2:
time: 100 us
  waiting for transfers between devices  37.6 us (38%)
  starting transfers between devices  36.5 us (36%)
  Pallas kernels  20.6 us (21%)
  other arithmetic  3.58 us (4%)
  local copies, waits for them, and re-layouts  1.78 us (2%)
    ppermute x25, waiting for transfers between devices, exchange(): lax.ppermute(value, axis, [(i, i ^ mask) for i in range(lax.axis_size(axi...  37.6 us
    ppermute x25, starting transfers between devices, exchange(): lax.ppermute(value, axis, [(i, i ^ mask) for i in range(lax.axis_size(axi...  36.5 us
    pallas_call x2, Pallas kernels, dress(): pl.pallas_call(functools.partial(dress_kernel, dists, chained, first_pair...  14.6 us
    pallas_call x1, Pallas kernels, gram_halves(): pl.pallas_call(functools.partial(gram_kernel, factor), out_shape=[jax.Sha...  2.42 us
    concatenate x2, other arithmetic, fast(): own = [jnp.concatenate([part, new], 0) for part, new in zip(parts, came)]  2.11 us
  transfers between devices with their start and end apart: 25, of which 11 were waited for; matrix products, arithmetic and copies ran while one was open for 4% of the time, Pallas kernels for 12%

profile of v2, /device:TPU:0, one launch (start us, length us, event | category | flops | bytes accessed | tf_op | source)
XLA Modules:
  0.0 100.2 jit_solution(10203104796767339543)
XLA Ops:
  0.0 0.1 stack.31.place
  0.1 1.6 %copy-done = bf16[4,2,128,1024]{3,2,1,0:T(8,128)(2,1)S(1)} copy-done((bf16[4,2,128,1024]{3,2,1,0:T(8,128)(2,1)S(1)}, bf16[4,2,128,1024]{3,2,1,0:T(8,128)(2,1)}, u32[]{:S(2)}) %copy-start) | copy-done | bytes 2097176
  1.7 1.6 %cut.1 = (bf16[4,2,128,256]{3,2,1,0:T(8,128)(2,1)S(1)}, bf16[2,2,128,256]{3,2,1,0:T(8,128)(2,1)S(1)}, bf16[2,2,128,256]{3,2,1,0:T(8,128)(2,1)S(1)}, bf16[2,2,128...) custom-call(s32[7]{0:T(128)S(1)} %stack.31.place, ...), custom_call_target="tpu_custom_call" | custom-call | bytes 4194304 | tf_op jit(solution)/shard_map/cut/pallas_call | solution.py:100
  3.3 3.0 %collective-permute-start.6 = (bf16[4,2,128,256]{3,2,1,0:T(8,128)(2,1)S(1)}, bf16[4,2,128,256]{3,2,1,0:T(8,128)(2,1)S(1)}, u32[]{:S(2)}, u32[]{:S(2)}) collective-permute-start(bf16[4,2,128,256]{3,2,1,0:T(8,128)(2,1)S(1)} %get-tuple-element.49.refs_0_), channel_id=1, source_target_pairs={{0,2},{2,0},{4,6},{6,4},{8,10},{10,8},{12,14},{14,12},{1,3},{3,1},... | collective-permute-start | bytes 1572872 | tf_op jit(solution)/shard_map/ppermute | solution.py:283
  6.3 2.4 %gram.1 = (bf16[3,128,256]{2,1,0:T(8,128)(2,1)S(1)}, bf16[3,128,256]{2,1,0:T(8,128)(2,1)S(1)}, f32[3,128,256]{2,1,0:T(8,128)S(1)}, f32[3,128,256]{2,1,0:T(8,128)S(1)}) custom-call(s32[7]{0:T(128)S(1)} %stack.31.place, s32[3,3]{1,0:T(4,128)S(1)} %copy-done.2, bf16[2,3,192,256]{3,2,1,0:T(8,128)(2,1)S(1)} %bitcast.18), custom_call_target="tpu_custom_call" | custom-call | flops 905969664 | bytes 3145728 | tf_op jit(solution)/shard_map/gram/pallas_call | solution.py:71
  8.8 0.1 collective-permute-start
  8.9 2.1 %collective-permute-start.1 = (bf16[3,128,256]{2,1,0:T(8,128)(2,1)S(1)}, bf16[3,128,256]{2,1,0:T(8,128)(2,1)S(1)}, u32[]{:S(2)}, u32[]{:S(2)}) collective-permute-start(bf16[3,128,256]{2,1,0:T(8,128)(2,1)S(1)} %get-tuple-element.40), channel_id=1, source_target_pairs={{0,4},{2,6},{4,0},{6,2},{8,12},{10,14},{12,8},{14,10},{1,5},{3,7},... | collective-permute-start | bytes 589832 | tf_op jit(solution)/shard_map/ppermute | solution.py:283
  10.9 2.5 %collective-permute-start.3 = (bf16[2,2,128,256]{3,2,1,0:T(8,128)(2,1)S(1)}, bf16[2,2,128,256]{3,2,1,0:T(8,128)(2,1)S(1)}, u32[]{:S(2)}, u32[]{:S(2)}) collective-permute-start(bf16[2,2,128,256]{3,2,1,0:T(8,128)(2,1)S(1)} %get-tuple-element.44), channel_id=1, source_target_pairs={{0,12},{2,14},{4,8},{6,10},{8,4},{10,6},{12,0},{14,2},{1,13},{3,15... | collective-permute-start | bytes 786440 | tf_op jit(solution)/shard_map/ppermute | solution.py:283
  13.4 9.1 %collective-permute-done.came_a = bf16[3,128,256]{2,1,0:T(8,128)(2,1)S(1)} collective-permute-done((bf16[3,128,256]{2,1,0:T(8,128)(2,1)S(1)}, bf16[3,128,256]{2,1,0:T(8,128)(2,1)S(1)}, u32[]{:S(2)}, u32[]{:S(2)}) %collective-permute-start) | collective-permute-done | bytes 196640 | tf_op jit(solution)/shard_map/ppermute | solution.py:283
  22.5 0.0 collective-permute-done.1.came_b
  22.5 0.6 fold.2
  23.1 0.0 copy-start.6
  23.1 1.9 %collective-permute-start.2 = (bf16[3,64,256]{2,1,0:T(8,128)(2,1)S(1)}, bf16[3,64,256]{2,1,0:T(8,128)(2,1)S(1)}, u32[]{:S(2)}, u32[]{:S(2)}) collective-permute-start(bf16[3,64,256]{2,1,0:T(8,128)(2,1)S(1)} %get-tuple-element.43), channel_id=1, source_target_pairs={{0,4},{2,6},{4,0},{6,2},{8,12},{10,14},{12,8},{14,10},{1,5},{3,7},... | collective-permute-start | bytes 294920 | tf_op jit(solution)/shard_map/ppermute | solution.py:283
  25.0 1.5 %collective-permute-start.4 = (bf16[3,64,256]{2,1,0:T(8,128)(2,1)S(1)}, bf16[3,64,256]{2,1,0:T(8,128)(2,1)S(1)}, u32[]{:S(2)}, u32[]{:S(2)}) collective-permute-start(bf16[3,64,256]{2,1,0:T(8,128)(2,1)S(1)} %get-tuple-element.46), channel_id=1, source_target_pairs={{0,2},{2,0},{4,6},{6,4},{8,10},{10,8},{12,14},{14,12},{1,3},{3,1},... | collective-permute-start | bytes 294920 | tf_op jit(solution)/shard_map/ppermute | solution.py:283
  26.5 1.3 %collective-permute-done.2.came_a = bf16[3,64,256]{2,1,0:T(8,128)(2,1)S(1)} collective-permute-done((bf16[3,64,256]{2,1,0:T(8,128)(2,1)S(1)}, bf16[3,64,256]{2,1,0:T(8,128)(2,1)S(1)}, u32[]{:S(2)}, u32[]{:S(2)}) %collective-permute-start.2) | collective-permute-done | bytes 98336 | tf_op jit(solution)/shard_map/ppermute | solution.py:283
  27.8 1.8 %collective-permute-done.4.came_b = bf16[3,64,256]{2,1,0:T(8,128)(2,1)S(1)} collective-permute-done((bf16[3,64,256]{2,1,0:T(8,128)(2,1)S(1)}, bf16[3,64,256]{2,1,0:T(8,128)(2,1)S(1)}, u32[]{:S(2)}, u32[]{:S(2)}) %collective-permute-start.4) | collective-permute-done | bytes 98336 | tf_op jit(solution)/shard_map/ppermute | solution.py:283
  29.6 0.6 fold.3
  30.2 2.7 %collective-permute-start.5 = (bf16[3,32,512]{2,1,0:T(8,128)(2,1)S(1)}, bf16[3,32,512]{2,1,0:T(8,128)(2,1)S(1)}, u32[]{:S(2)}, u32[]{:S(2)}) collective-permute-start(bf16[3,32,512]{2,1,0:T(8,128)(2,1)S(1)} %get-tuple-element.48), channel_id=1, source_target_pairs={{0,8},{2,10},{4,12},{6,14},{8,0},{10,2},{12,4},{14,6},{1,9},{3,11}... | collective-permute-start | bytes 294920 | tf_op jit(solution)/shard_map/ppermute | solution.py:283
  32.8 5.4 %collective-permute-done.5 = bf16[3,32,512]{2,1,0:T(8,128)(2,1)S(1)} collective-permute-done((bf16[3,32,512]{2,1,0:T(8,128)(2,1)S(1)}, bf16[3,32,512]{2,1,0:T(8,128)(2,1)S(1)}, u32[]{:S(2)}, u32[]{:S(2)}) %collective-permute-start.5) | collective-permute-done | bytes 98336 | tf_op jit(solution)/shard_map/ppermute | solution.py:283
  38.2 0.3 collective-permute-start.7
  38.6 0.5 collective-permute-start.10
  39.1 1.5 %collective-permute-start.9 = (bf16[2,2,128,256]{3,2,1,0:T(8,128)(2,1)S(1)}, bf16[2,2,128,256]{3,2,1,0:T(8,128)(2,1)S(1)}, u32[]{:S(2)}, u32[]{:S(2)}) collective-permute-start(bf16[2,2,128,256]{3,2,1,0:T(8,128)(2,1)S(1)} %collective-permute-done.3.refs_3_), channel_id=1, source_target_pairs={{0,2},{2,0},{4,6},{6,4},{8,10},{10,8},{12,14},{14,12},{1,3},{3,1},... | collective-permute-start | bytes 786440 | tf_op jit(solution)/shard_map/ppermute | solution.py:283
  40.6 6.8 %collective-permute-done.7 = bf16[1,3,32,512]{3,2,1,0:T(8,128)(2,1)S(1)} collective-permute-done((bf16[1,3,32,512]{3,2,1,0:T(8,128)(2,1)S(1)}, bf16[1,3,32,512]{3,2,1,0:T(8,128)(2,1)S(1)}, u32[]{:S(2)}, u32[]{:S(2)}) %collective-permute-start.7) | collective-permute-done | bytes 98336 | tf_op jit(solution)/shard_map/ppermute | solution.py:283
  47.3 0.1 collective-permute-start.8
  47.4 0.5 collective-permute-start.12
  47.9 2.8 %collective-permute-start.13 = (bf16[2,3,32,256]{3,2,1,0:T(8,128)(2,1)S(1)}, bf16[2,3,32,256]{3,2,1,0:T(8,128)(2,1)S(1)}, u32[]{:S(2)}, u32[]{:S(2)}) collective-permute-start(bf16[2,3,32,256]{3,2,1,0:T(8,128)(2,1)S(1)} %get-tuple-element.69), channel_id=1, source_target_pairs={{0,2},{2,0},{4,6},{6,4},{8,10},{10,8},{12,14},{14,12},{1,3},{3,1},... | collective-permute-start | bytes 294920 | tf_op jit(solution)/shard_map/ppermute | solution.py:283
  50.7 4.5 %collective-permute-done.8 = bf16[2,3,32,256]{3,2,1,0:T(8,128)(2,1)S(1)} collective-permute-done((bf16[2,3,32,256]{3,2,1,0:T(8,128)(2,1)S(1)}, bf16[2,3,32,256]{3,2,1,0:T(8,128)(2,1)S(1)}, u32[]{:S(2)}, u32[]{:S(2)}) %collective-permute-start.8) | collective-permute-done | bytes 98336 | tf_op jit(solution)/shard_map/ppermute | solution.py:283
  55.2 0.7 pad_maximum_fusion.2
  56.0 6.0 %collective-permute-start.11 = (bf16[4,3,32,256]{3,2,1,0:T(8,128)(2,1)}, bf16[4,3,32,256]{3,2,1,0:T(8,128)(2,1)}, u32[]{:S(2)}, u32[]{:S(2)}) collective-permute-start(bf16[4,3,32,256]{3,2,1,0:T(8,128)(2,1)} %pad_maximum_fusion.2), channel_id=1, source_target_pairs={{0,2},{2,0},{4,6},{6,4},{8,10},{10,8},{12,14},{14,12},{1,3},{3,1},... | collective-permute-start | bytes 589832 | tf_op jit(solution)/shard_map/ppermute | solution.py:283
  62.0 0.7 pad_maximum_fusion.3
  62.7 2.0 %collective-permute-start.20 = (bf16[2,2,128,256]{3,2,1,0:T(8,128)(2,1)S(1)}, bf16[2,2,128,256]{3,2,1,0:T(8,128)(2,1)S(1)}, u32[]{:S(2)}, u32[]{:S(2)}) collective-permute-start(bf16[2,2,128,256]{3,2,1,0:T(8,128)(2,1)S(1)} %get-tuple-element.59), channel_id=1, source_target_pairs={{0,4},{2,6},{4,0},{6,2},{8,12},{10,14},{12,8},{14,10},{1,5},{3,7},... | collective-permute-start | bytes 786440 | tf_op jit(solution)/shard_map/ppermute | solution.py:283
  64.7 2.9 %collective-permute-start.21 = (bf16[2,2,128,256]{3,2,1,0:T(8,128)(2,1)S(1)}, bf16[2,2,128,256]{3,2,1,0:T(8,128)(2,1)S(1)}, u32[]{:S(2)}, u32[]{:S(2)}) collective-permute-start(bf16[2,2,128,256]{3,2,1,0:T(8,128)(2,1)S(1)} %get-tuple-element.60), channel_id=1, source_target_pairs={{0,8},{2,10},{4,12},{6,14},{8,0},{10,2},{12,4},{14,6},{1,9},{3,11}... | collective-permute-start | bytes 786440 | tf_op jit(solution)/shard_map/ppermute | solution.py:283
  67.6 0.5 collective-permute-done.11
  68.1 2.0 %collective-permute-start.17 = (bf16[2,2,128,256]{3,2,1,0:T(8,128)(2,1)S(1)}, bf16[2,2,128,256]{3,2,1,0:T(8,128)(2,1)S(1)}, u32[]{:S(2)}, u32[]{:S(2)}) collective-permute-start(bf16[2,2,128,256]{3,2,1,0:T(8,128)(2,1)S(1)} %collective-permute-done.10.refs_1_), channel_id=1, source_target_pairs={{0,2},{2,0},{4,6},{6,4},{8,10},{10,8},{12,14},{14,12},{1,3},{3,1},... | collective-permute-start | bytes 786440 | tf_op jit(solution)/shard_map/ppermute | solution.py:283
  70.1 1.1 %pad_maximum_fusion.own_a = bf16[8,3,32,256]{3,2,1,0:T(8,128)(2,1)S(1)} fusion(bf16[4,3,32,256]{3,2,1,0:T(8,128)(2,1)} %collective-permute-done.11, bf16[2,3,32,256]{3,2,1,0:T(8,128)(2,1)} %copy-done.5, bf16[2,3,32,256]{3,2,1,0:T(8,128)(2,1)} %copy-done.3), kind=kLoop, calls=%fused_computation | loop fusion | flops 393216 | bytes 786432 | tf_op jit(solution)/shard_map/concatenate | solution.py:350
  71.2 0.6 collective-permute-done.16.refs_2_
  71.8 1.6 %collective-permute-start.18 = (bf16[2,2,128,256]{3,2,1,0:T(8,128)(2,1)S(1)}, bf16[2,2,128,256]{3,2,1,0:T(8,128)(2,1)S(1)}, u32[]{:S(2)}, u32[]{:S(2)}) collective-permute-start(bf16[2,2,128,256]{3,2,1,0:T(8,128)(2,1)S(1)} %collective-permute-done.12.refs_3_), channel_id=1, source_target_pairs={{0,2},{2,0},{4,6},{6,4},{8,10},{10,8},{12,14},{14,12},{1,3},{3,1},... | collective-permute-start | bytes 786440 | tf_op jit(solution)/shard_map/ppermute | solution.py:283
  73.4 1.5 %collective-permute-done.14 = bf16[4,3,32,256]{3,2,1,0:T(8,128)(2,1)} collective-permute-done((bf16[4,3,32,256]{3,2,1,0:T(8,128)(2,1)}, bf16[4,3,32,256]{3,2,1,0:T(8,128)(2,1)}, u32[]{:S(2)}, u32[]{:S(2)}) %collective-permute-start.14) | collective-permute-done | bytes 196640 | tf_op jit(solution)/shard_map/ppermute | solution.py:283
  75.0 1.0 %pad_maximum_fusion.1.own_b = bf16[8,3,32,256]{3,2,1,0:T(8,128)(2,1)S(1)} fusion(bf16[4,3,32,256]{3,2,1,0:T(8,128)(2,1)} %collective-permute-done.14, bf16[2,3,32,256]{3,2,1,0:T(8,128)(2,1)} %copy-done.4, bf16[2,3,32,256]{3,2,1,0:T(8,128)(2,1)S(1)} %get-tuple-element.69), kind=kLoop, calls=%fused_computation.1 | loop fusion | flops 393216 | bytes 786432 | tf_op jit(solution)/shard_map/concatenate | solution.py:350
  76.0 2.4 %collective-permute-done.20.refs_1_ = bf16[2,2,128,256]{3,2,1,0:T(8,128)(2,1)S(1)} collective-permute-done((bf16[2,2,128,256]{3,2,1,0:T(8,128)(2,1)S(1)}, bf16[2,2,128,256]{3,2,1,0:T(8,128)(2,1)S(1)}, u32[]{:S(2)}, u32[]{:S(2)}) %collective-permute-start.20) | collective-permute-done | bytes 262176 | tf_op jit(solution)/shard_map/ppermute | solution.py:283
  78.4 0.5 collective-permute-start.19
  78.9 0.1 slice_bitcast_fusion
  79.0 0.7 collective-permute-start.22
  79.8 1.3 %collective-permute-start.23 = (bf16[2,2,128,256]{3,2,1,0:T(8,128)(2,1)S(1)}, bf16[2,2,128,256]{3,2,1,0:T(8,128)(2,1)S(1)}, u32[]{:S(2)}, u32[]{:S(2)}) collective-permute-start(bf16[2,2,128,256]{3,2,1,0:T(8,128)(2,1)S(1)} %collective-permute-done.21.refs_2_), channel_id=1, source_target_pairs={{0,2},{2,0},{4,6},{6,4},{8,10},{10,8},{12,14},{14,12},{1,3},{3,1},... | collective-permute-start | bytes 786440 | tf_op jit(solution)/shard_map/ppermute | solution.py:283
  81.0 0.8 prepare.1
  81.8 7.3 %dress.2.refs_8_ = bf16[4,3,2,128,1024]{4,3,2,1,0:T(8,128)(2,1)} custom-call(s32[7]{0:T(128)S(1)} %stack.31.place, s32[2]{0:T(128)S(1)} %get-tuple-element.72.other_src, s32[2]{0:T(128)S(1)} %get-tuple-element.71.other_snk, bf16[2,768,512]{2,1,0:T(8,128)(2,1)S(1)} %get-tuple-element.57.left, bf16[2,3,512,256]{3,2,1,0:T(8,128)(2,1)S(1)} %get-tuple-element.58.sink, ...), custom_call_target="tpu_custom_call" | custom-call | flops 3221225472 | bytes 2097152 | tf_op jit(solution)/shard_map/dress/pallas_call | solution.py:253
  89.1 3.7 %collective-permute-done.23.refs_6_ = bf16[2,2,128,256]{3,2,1,0:T(8,128)(2,1)S(1)} collective-permute-done((bf16[2,2,128,256]{3,2,1,0:T(8,128)(2,1)S(1)}, bf16[2,2,128,256]{3,2,1,0:T(8,128)(2,1)S(1)}, u32[]{:S(2)}, u32[]{:S(2)}) %collective-permute-start.23) | collective-permute-done | bytes 262176 | tf_op jit(solution)/shard_map/ppermute | solution.py:283
  92.9 7.3 %dress.3 = bf16[4,3,2,128,1024]{4,3,2,1,0:T(8,128)(2,1)} custom-call(s32[7]{0:T(128)S(1)} %stack.31.place, s32[2]{0:T(128)S(1)} %get-tuple-element.74.other_src, s32[2]{0:T(128)S(1)} %get-tuple-element.73.other_snk, bf16[2,768,512]{2,1,0:T(8,128)(2,1)S(1)} %get-tuple-element.57.left, ...), custom_call_target="tpu_custom_call", output_to_operand_aliasing={{}: (13, {})} | custom-call | flops 3221225472 | bytes 2097152 | tf_op jit(solution)/shard_map/dress/pallas_call | solution.py:253
  (32 shorter events, 0.1 us)
Async XLA Ops:
  0.0 6.3 %copy-start.2 = (s32[3,3]{1,0:T(4,128)S(1)}, s32[3,3]{1,0:T(4,128)}, u32[]{:S(2)}) copy-start(s32[3,3]{1,0:T(4,128)} %momenta.1) | copy-start | bytes 112
  0.1 1.6 %copy-start = (bf16[4,2,128,1024]{3,2,1,0:T(8,128)(2,1)S(1)}, bf16[4,2,128,1024]{3,2,1,0:T(8,128)(2,1)}, u32[]{:S(2)}) copy-start(bf16[4,2,128,1024]{3,2,1,0:T(8,128)(2,1)} %panels.1) | copy-start | bytes 6291460
  1.7 4.7 %copy-start.1 = (bf16[1,2,3,192,256]{4,3,2,1,0:T(8,128)(2,1)S(1)}, bf16[1,2,3,192,256]{4,3,2,1,0:T(8,128)(2,1)}, u32[]{:S(2)}) copy-start(bf16[1,2,3,192,256]{4,3,2,1,0:T(8,128)(2,1)} %param.4) | copy-start | bytes 1769476
  3.3 34.9 %collective-permute-start.6 = (bf16[4,2,128,256]{3,2,1,0:T(8,128)(2,1)S(1)}, bf16[4,2,128,256]{3,2,1,0:T(8,128)(2,1)S(1)}, u32[]{:S(2)}, u32[]{:S(2)}) collective-permute-start(bf16[4,2,128,256]{3,2,1,0:T(8,128)(2,1)S(1)} %get-tuple-element.49.refs_0_), channel_id=1, source_target_pairs={{0,2},{2,0},{4,6},{6,4},{8,10},{10,8},{12,14},{14,12},{1,3},{3,1},... | collective-permute-start | bytes 1572872 | tf_op jit(solution)/shard_map/ppermute | solution.py:283
  8.8 13.7 %collective-permute-start = (bf16[3,128,256]{2,1,0:T(8,128)(2,1)S(1)}, bf16[3,128,256]{2,1,0:T(8,128)(2,1)S(1)}, u32[]{:S(2)}, u32[]{:S(2)}) collective-permute-start(bf16[3,128,256]{2,1,0:T(8,128)(2,1)S(1)} %get-tuple-element.39), channel_id=1, source_target_pairs={{0,2},{2,0},{4,6},{6,4},{8,10},{10,8},{12,14},{14,12},{1,3},{3,1},... | collective-permute-start | bytes 589832 | tf_op jit(solution)/shard_map/ppermute | solution.py:283
  8.9 13.6 %collective-permute-start.1 = (bf16[3,128,256]{2,1,0:T(8,128)(2,1)S(1)}, bf16[3,128,256]{2,1,0:T(8,128)(2,1)S(1)}, u32[]{:S(2)}, u32[]{:S(2)}) collective-permute-start(bf16[3,128,256]{2,1,0:T(8,128)(2,1)S(1)} %get-tuple-element.40), channel_id=1, source_target_pairs={{0,4},{2,6},{4,0},{6,2},{8,12},{10,14},{12,8},{14,10},{1,5},{3,7},... | collective-permute-start | bytes 589832 | tf_op jit(solution)/shard_map/ppermute | solution.py:283
  10.9 15.5 %collective-permute-start.3 = (bf16[2,2,128,256]{3,2,1,0:T(8,128)(2,1)S(1)}, bf16[2,2,128,256]{3,2,1,0:T(8,128)(2,1)S(1)}, u32[]{:S(2)}, u32[]{:S(2)}) collective-permute-start(bf16[2,2,128,256]{3,2,1,0:T(8,128)(2,1)S(1)} %get-tuple-element.44), channel_id=1, source_target_pairs={{0,12},{2,14},{4,8},{6,10},{8,4},{10,6},{12,0},{14,2},{1,13},{3,15... | collective-permute-start | bytes 786440 | tf_op jit(solution)/shard_map/ppermute | solution.py:283
  23.1 55.8 %copy-start.6 = (s32[4,2]{0,1:T(2,128)S(1)}, s32[4,2]{0,1:T(2,128)}, u32[]{:S(2)}) copy-start(s32[4,2]{0,1:T(2,128)} %param.6) | copy-start | bytes 100
  23.1 4.7 %collective-permute-start.2 = (bf16[3,64,256]{2,1,0:T(8,128)(2,1)S(1)}, bf16[3,64,256]{2,1,0:T(8,128)(2,1)S(1)}, u32[]{:S(2)}, u32[]{:S(2)}) collective-permute-start(bf16[3,64,256]{2,1,0:T(8,128)(2,1)S(1)} %get-tuple-element.43), channel_id=1, source_target_pairs={{0,4},{2,6},{4,0},{6,2},{8,12},{10,14},{12,8},{14,10},{1,5},{3,7},... | collective-permute-start | bytes 294920 | tf_op jit(solution)/shard_map/ppermute | solution.py:283
  25.0 4.6 %collective-permute-start.4 = (bf16[3,64,256]{2,1,0:T(8,128)(2,1)S(1)}, bf16[3,64,256]{2,1,0:T(8,128)(2,1)S(1)}, u32[]{:S(2)}, u32[]{:S(2)}) collective-permute-start(bf16[3,64,256]{2,1,0:T(8,128)(2,1)S(1)} %get-tuple-element.46), channel_id=1, source_target_pairs={{0,2},{2,0},{4,6},{6,4},{8,10},{10,8},{12,14},{14,12},{1,3},{3,1},... | collective-permute-start | bytes 294920 | tf_op jit(solution)/shard_map/ppermute | solution.py:283
  30.2 8.0 %collective-permute-start.5 = (bf16[3,32,512]{2,1,0:T(8,128)(2,1)S(1)}, bf16[3,32,512]{2,1,0:T(8,128)(2,1)S(1)}, u32[]{:S(2)}, u32[]{:S(2)}) collective-permute-start(bf16[3,32,512]{2,1,0:T(8,128)(2,1)S(1)} %get-tuple-element.48), channel_id=1, source_target_pairs={{0,8},{2,10},{4,12},{6,14},{8,0},{10,2},{12,4},{14,6},{1,9},{3,11}... | collective-permute-start | bytes 294920 | tf_op jit(solution)/shard_map/ppermute | solution.py:283
  38.2 9.1 %collective-permute-start.7 = (bf16[1,3,32,512]{3,2,1,0:T(8,128)(2,1)S(1)}, bf16[1,3,32,512]{3,2,1,0:T(8,128)(2,1)S(1)}, u32[]{:S(2)}, u32[]{:S(2)}) collective-permute-start(bf16[1,3,32,512]{3,2,1,0:T(8,128)(2,1)S(1)} %fusion), channel_id=1, source_target_pairs={{0,8},{2,10},{4,12},{6,14},{8,0},{10,2},{12,4},{14,6},{1,9},{3,11}... | collective-permute-start | bytes 294920 | tf_op jit(solution)/shard_map/ppermute | solution.py:283
  38.6 12.1 %collective-permute-start.10 = (bf16[2,2,128,256]{3,2,1,0:T(8,128)(2,1)S(1)}, bf16[2,2,128,256]{3,2,1,0:T(8,128)(2,1)S(1)}, u32[]{:S(2)}, u32[]{:S(2)}) collective-permute-start(bf16[2,2,128,256]{3,2,1,0:T(8,128)(2,1)S(1)} %get-tuple-element.51), channel_id=1, source_target_pairs={{0,4},{2,6},{4,0},{6,2},{8,12},{10,14},{12,8},{14,10},{1,5},{3,7},... | collective-permute-start | bytes 786440 | tf_op jit(solution)/shard_map/ppermute | solution.py:283
  39.1 11.6 %collective-permute-start.9 = (bf16[2,2,128,256]{3,2,1,0:T(8,128)(2,1)S(1)}, bf16[2,2,128,256]{3,2,1,0:T(8,128)(2,1)S(1)}, u32[]{:S(2)}, u32[]{:S(2)}) collective-permute-start(bf16[2,2,128,256]{3,2,1,0:T(8,128)(2,1)S(1)} %collective-permute-done.3.refs_3_), channel_id=1, source_target_pairs={{0,2},{2,0},{4,6},{6,4},{8,10},{10,8},{12,14},{14,12},{1,3},{3,1},... | collective-permute-start | bytes 786440 | tf_op jit(solution)/shard_map/ppermute | solution.py:283
  47.3 14.6 %copy-start.3 = (bf16[2,3,32,256]{3,2,1,0:T(8,128)(2,1)}, bf16[2,3,32,256]{3,2,1,0:T(8,128)(2,1)S(1)}, u32[]{:S(2)}) copy-start(bf16[2,3,32,256]{3,2,1,0:T(8,128)(2,1)S(1)} %get-tuple-element.70) | copy-start | bytes 294916
  47.3 7.9 %collective-permute-start.8 = (bf16[2,3,32,256]{3,2,1,0:T(8,128)(2,1)S(1)}, bf16[2,3,32,256]{3,2,1,0:T(8,128)(2,1)S(1)}, u32[]{:S(2)}, u32[]{:S(2)}) collective-permute-start(bf16[2,3,32,256]{3,2,1,0:T(8,128)(2,1)S(1)} %get-tuple-element.70), channel_id=1, source_target_pairs={{0,4},{2,6},{4,0},{6,2},{8,12},{10,14},{12,8},{14,10},{1,5},{3,7},... | collective-permute-start | bytes 294920 | tf_op jit(solution)/shard_map/ppermute | solution.py:283
  47.4 17.3 %collective-permute-start.12 = (bf16[2,2,128,256]{3,2,1,0:T(8,128)(2,1)S(1)}, bf16[2,2,128,256]{3,2,1,0:T(8,128)(2,1)S(1)}, u32[]{:S(2)}, u32[]{:S(2)}) collective-permute-start(bf16[2,2,128,256]{3,2,1,0:T(8,128)(2,1)S(1)} %get-tuple-element.53), channel_id=1, source_target_pairs={{0,12},{2,14},{4,8},{6,10},{8,4},{10,6},{12,0},{14,2},{1,13},{3,15... | collective-permute-start | bytes 786440 | tf_op jit(solution)/shard_map/ppermute | solution.py:283
  47.9 14.0 %collective-permute-start.13 = (bf16[2,3,32,256]{3,2,1,0:T(8,128)(2,1)S(1)}, bf16[2,3,32,256]{3,2,1,0:T(8,128)(2,1)S(1)}, u32[]{:S(2)}, u32[]{:S(2)}) collective-permute-start(bf16[2,3,32,256]{3,2,1,0:T(8,128)(2,1)S(1)} %get-tuple-element.69), channel_id=1, source_target_pairs={{0,2},{2,0},{4,6},{6,4},{8,10},{10,8},{12,14},{14,12},{1,3},{3,1},... | collective-permute-start | bytes 294920 | tf_op jit(solution)/shard_map/ppermute | solution.py:283
  55.2 6.7 %copy-start.5 = (bf16[2,3,32,256]{3,2,1,0:T(8,128)(2,1)}, bf16[2,3,32,256]{3,2,1,0:T(8,128)(2,1)S(1)}, u32[]{:S(2)}) copy-start(bf16[2,3,32,256]{3,2,1,0:T(8,128)(2,1)S(1)} %collective-permute-done.8) | copy-start | bytes 294916
  56.0 12.1 %collective-permute-start.11 = (bf16[4,3,32,256]{3,2,1,0:T(8,128)(2,1)}, bf16[4,3,32,256]{3,2,1,0:T(8,128)(2,1)}, u32[]{:S(2)}, u32[]{:S(2)}) collective-permute-start(bf16[4,3,32,256]{3,2,1,0:T(8,128)(2,1)} %pad_maximum_fusion.2), channel_id=1, source_target_pairs={{0,2},{2,0},{4,6},{6,4},{8,10},{10,8},{12,14},{14,12},{1,3},{3,1},... | collective-permute-start | bytes 589832 | tf_op jit(solution)/shard_map/ppermute | solution.py:283
  61.9 9.9 %collective-permute-start.16 = (bf16[2,2,128,256]{3,2,1,0:T(8,128)(2,1)}, bf16[2,2,128,256]{3,2,1,0:T(8,128)(2,1)S(1)}, u32[]{:S(2)}, u32[]{:S(2)}) collective-permute-start(bf16[2,2,128,256]{3,2,1,0:T(8,128)(2,1)} %get-tuple-element.55), channel_id=1, source_target_pairs={{0,8},{2,10},{4,12},{6,14},{8,0},{10,2},{12,4},{14,6},{1,9},{3,11}... | collective-permute-start | bytes 786440 | tf_op jit(solution)/shard_map/ppermute | solution.py:283
  62.0 2.7 %copy-start.4 = (bf16[2,3,32,256]{3,2,1,0:T(8,128)(2,1)}, bf16[2,3,32,256]{3,2,1,0:T(8,128)(2,1)S(1)}, u32[]{:S(2)}) copy-start(bf16[2,3,32,256]{3,2,1,0:T(8,128)(2,1)S(1)} %collective-permute-done.13) | copy-start | bytes 294916
  62.7 12.3 %collective-permute-start.14 = (bf16[4,3,32,256]{3,2,1,0:T(8,128)(2,1)}, bf16[4,3,32,256]{3,2,1,0:T(8,128)(2,1)}, u32[]{:S(2)}, u32[]{:S(2)}) collective-permute-start(bf16[4,3,32,256]{3,2,1,0:T(8,128)(2,1)} %pad_maximum_fusion.3), channel_id=1, source_target_pairs={{0,4},{2,6},{4,0},{6,2},{8,12},{10,14},{12,8},{14,10},{1,5},{3,7},... | collective-permute-start | bytes 589832 | tf_op jit(solution)/shard_map/ppermute | solution.py:283
  62.7 15.7 %collective-permute-start.20 = (bf16[2,2,128,256]{3,2,1,0:T(8,128)(2,1)S(1)}, bf16[2,2,128,256]{3,2,1,0:T(8,128)(2,1)S(1)}, u32[]{:S(2)}, u32[]{:S(2)}) collective-permute-start(bf16[2,2,128,256]{3,2,1,0:T(8,128)(2,1)S(1)} %get-tuple-element.59), channel_id=1, source_target_pairs={{0,4},{2,6},{4,0},{6,2},{8,12},{10,14},{12,8},{14,10},{1,5},{3,7},... | collective-permute-start | bytes 786440 | tf_op jit(solution)/shard_map/ppermute | solution.py:283
  64.7 13.7 %collective-permute-start.21 = (bf16[2,2,128,256]{3,2,1,0:T(8,128)(2,1)S(1)}, bf16[2,2,128,256]{3,2,1,0:T(8,128)(2,1)S(1)}, u32[]{:S(2)}, u32[]{:S(2)}) collective-permute-start(bf16[2,2,128,256]{3,2,1,0:T(8,128)(2,1)S(1)} %get-tuple-element.60), channel_id=1, source_target_pairs={{0,8},{2,10},{4,12},{6,14},{8,0},{10,2},{12,4},{14,6},{1,9},{3,11}... | collective-permute-start | bytes 786440 | tf_op jit(solution)/shard_map/ppermute | solution.py:283
  68.1 10.9 %collective-permute-start.17 = (bf16[2,2,128,256]{3,2,1,0:T(8,128)(2,1)S(1)}, bf16[2,2,128,256]{3,2,1,0:T(8,128)(2,1)S(1)}, u32[]{:S(2)}, u32[]{:S(2)}) collective-permute-start(bf16[2,2,128,256]{3,2,1,0:T(8,128)(2,1)S(1)} %collective-permute-done.10.refs_1_), channel_id=1, source_target_pairs={{0,2},{2,0},{4,6},{6,4},{8,10},{10,8},{12,14},{14,12},{1,3},{3,1},... | collective-permute-start | bytes 786440 | tf_op jit(solution)/shard_map/ppermute | solution.py:283
  71.8 7.9 %collective-permute-start.18 = (bf16[2,2,128,256]{3,2,1,0:T(8,128)(2,1)S(1)}, bf16[2,2,128,256]{3,2,1,0:T(8,128)(2,1)S(1)}, u32[]{:S(2)}, u32[]{:S(2)}) collective-permute-start(bf16[2,2,128,256]{3,2,1,0:T(8,128)(2,1)S(1)} %collective-permute-done.12.refs_3_), channel_id=1, source_target_pairs={{0,2},{2,0},{4,6},{6,4},{8,10},{10,8},{12,14},{14,12},{1,3},{3,1},... | collective-permute-start | bytes 786440 | tf_op jit(solution)/shard_map/ppermute | solution.py:283
  75.0 6.8 %collective-permute-start.24 = (bf16[2,2,128,256]{3,2,1,0:T(8,128)(2,1)S(1)}, bf16[2,2,128,256]{3,2,1,0:T(8,128)(2,1)S(1)}, u32[]{:S(2)}, u32[]{:S(2)}) collective-permute-start(bf16[2,2,128,256]{3,2,1,0:T(8,128)(2,1)S(1)} %collective-permute-done.16.refs_2_), channel_id=1, source_target_pairs={{0,2},{2,0},{4,6},{6,4},{8,10},{10,8},{12,14},{14,12},{1,3},{3,1},... | collective-permute-start | bytes 786440 | tf_op jit(solution)/shard_map/ppermute | solution.py:283
  78.4 2.6 %collective-permute-start.15 = (bf16[8,3,32,256]{3,2,1,0:T(8,128)(2,1)S(1)}, bf16[8,3,32,256]{3,2,1,0:T(8,128)(2,1)S(1)}, u32[]{:S(2)}, u32[]{:S(2)}) collective-permute-start(bf16[8,3,32,256]{3,2,1,0:T(8,128)(2,1)S(1)} %pad_maximum_fusion.own_a), channel_id=1, source_target_pairs={{0,1},{1,0},{2,3},{3,2},{4,5},{5,4},{6,7},{7,6},{8,9},{9,8},{10,11... | collective-permute-start | bytes 1179656 | tf_op jit(solution)/shard_map/ppermute | solution.py:283
  78.4 2.6 %collective-permute-start.19 = (bf16[8,3,32,256]{3,2,1,0:T(8,128)(2,1)S(1)}, bf16[8,3,32,256]{3,2,1,0:T(8,128)(2,1)S(1)}, u32[]{:S(2)}, u32[]{:S(2)}) collective-permute-start(bf16[8,3,32,256]{3,2,1,0:T(8,128)(2,1)S(1)} %pad_maximum_fusion.1.own_b), channel_id=1, source_target_pairs={{0,1},{1,0},{2,3},{3,2},{4,5},{5,4},{6,7},{7,6},{8,9},{9,8},{10,11... | collective-permute-start | bytes 1179656 | tf_op jit(solution)/shard_map/ppermute | solution.py:283
  79.0 10.1 %collective-permute-start.22 = (bf16[2,2,128,256]{3,2,1,0:T(8,128)(2,1)S(1)}, bf16[2,2,128,256]{3,2,1,0:T(8,128)(2,1)S(1)}, u32[]{:S(2)}, u32[]{:S(2)}) collective-permute-start(bf16[2,2,128,256]{3,2,1,0:T(8,128)(2,1)S(1)} %collective-permute-done.20.refs_1_), channel_id=1, source_target_pairs={{0,2},{2,0},{4,6},{6,4},{8,10},{10,8},{12,14},{14,12},{1,3},{3,1},... | collective-permute-start | bytes 786440 | tf_op jit(solution)/shard_map/ppermute | solution.py:283
  79.8 13.1 %collective-permute-start.23 = (bf16[2,2,128,256]{3,2,1,0:T(8,128)(2,1)S(1)}, bf16[2,2,128,256]{3,2,1,0:T(8,128)(2,1)S(1)}, u32[]{:S(2)}, u32[]{:S(2)}) collective-permute-start(bf16[2,2,128,256]{3,2,1,0:T(8,128)(2,1)S(1)} %collective-permute-done.21.refs_2_), channel_id=1, source_target_pairs={{0,2},{2,0},{4,6},{6,4},{8,10},{10,8},{12,14},{14,12},{1,3},{3,1},... | collective-permute-start | bytes 786440 | tf_op jit(solution)/shard_map/ppermute | solution.py:283

commit v3 on v2

--- a/solution.py
+++ b/solution.py
@@ -11,7 +11,7 @@
 LX = 64
 LX_BITS = LX.bit_length() - 1
 F32, BF16 = jnp.float32, jnp.bfloat16
-SPACE, X, Z, Z_LOW, Z_HIGH, HERE_A, HERE_B = range(7)
+SPACE, X, Z, Z_LOW, Z_HIGH, HERE_A, HERE_B, MOMENTA = range(8)
 VMEM_LIMIT = 24 * 1024 * 1024
 CUT_VMEM = 24 * 1024 * 1024
 
@@ -26,7 +26,7 @@
     return pl.CostEstimate(flops=int(flops), bytes_accessed=int(bytes_accessed), transcendentals=0)
 
 
-def gram_kernel(factor, place, momenta, eig, send_a, send_b, keep_a, keep_b, phased, total):
+def gram_kernel(factor, place, eig, send_a, send_b, keep_a, keep_b, phased, total):
     colors, sites, vectors = eig.shape[1:]
     moms, half = send_a.shape[:2]
     site = place[SPACE] * sites + lax.broadcasted_iota(jnp.int32, (sites, 128), 0)
@@ -34,7 +34,7 @@
     coords = (site & (LX - 1), (site >> LX_BITS) & (LX - 1), site >> (2 * LX_BITS))
     wave = jnp.zeros((sites, 128), jnp.int32)
     for m in range(moms):
-        mine = sum(momenta[m, j] * coords[j] for j in range(3))
+        mine = sum(place[MOMENTA + 3 * m + j] * coords[j] for j in range(3))
         wave = jnp.where(lane == m, mine, wave)
     angle = (wave & (LX - 1)).astype(F32) * F32(2.0 * math.pi / LX)
     cosine, sine = jnp.cos(angle), jnp.sin(angle)
@@ -62,16 +62,15 @@
             keep[m] = total[pl.ds(pl.multiple_of(bit * half, half), half), lanes]
 
 
-def gram_halves(eig, momenta, place, factor):
+def gram_halves(eig, moms, place, factor):
     _, colors, sites, vectors = eig.shape
-    moms = momenta.shape[0]
     shape = (moms, vectors // 2, vectors)
     smem = pl.BlockSpec(memory_space=pltpu.SMEM)
     vmem = pl.BlockSpec(memory_space=pltpu.VMEM)
     return pl.pallas_call(
         functools.partial(gram_kernel, factor),
         out_shape=[jax.ShapeDtypeStruct(shape, kind) for kind in (BF16, BF16, F32, F32)],
-        in_specs=[smem, smem, vmem],
+        in_specs=[smem, vmem],
         out_specs=[vmem] * 4,
         scratch_shapes=[
             pltpu.VMEM((2 * colors * sites, 2 * vectors), BF16),
@@ -80,7 +79,7 @@
         compiler_params=params(),
         cost_estimate=cost(4 * colors * sites * vectors * moms * 2 * vectors, 3 * 2**20),
         name="gram",
-    )(place, momenta, eig)
+    )(place, eig)
 
 
 def cut_kernel(plan, place, panels, *refs):
@@ -153,40 +152,91 @@
     )(place, keep_a, keep_b, came_a, came_b)
 
 
-def prepare_kernel(place, own_a, own_b, oth_a, oth_b, left, sink):
-    pieces, moms, piece_rows, vectors = own_a.shape
-    columns = left.shape[1] // (2 * moms)
-    here_a, here_b, x = place[HERE_A], place[HERE_B], place[X]
-    for t, (part_a, part_b) in enumerate(((own_a, own_b), (oth_a, oth_b))):
-        for m in range(moms):
-            for i in range(columns // piece_rows):
-                q = x * (columns // piece_rows) + i
-                re, im = part_a[q ^ here_a, m], part_b[q ^ here_b, m]
-                at = 2 * m * columns + i * piece_rows
-                left[t, at : at + piece_rows, :vectors] = re
-                left[t, at : at + piece_rows, vectors:] = im
-                at += columns
-                left[t, at : at + piece_rows, :vectors] = -im
-                left[t, at : at + piece_rows, vectors:] = re
-            for q in range(pieces):
-                at = q * piece_rows
-                sink[t, m, at : at + piece_rows] = part_a[here_a ^ q, m]
-                sink[t, m, vectors + at : vectors + at + piece_rows] = part_b[here_b ^ q, m]
-
-
-def prepare(own, oth, columns, place):
-    pieces, moms, piece_rows, vectors = own[0].shape
+def halve_kernel(field, came, part_a, part_b, both):
+    vectors = part_a.shape[3]
+    for i, piece in enumerate((field, came)):
+        for j, part in enumerate((part_a, part_b)):
+            value = piece[0, :, :, j * vectors : (j + 1) * vectors]
+            part[i] = value
+            both[j, i] = value
+
+
+def pair_kernel(own_a, own_b, came_a, came_b, part_a, part_b, both):
+    count = own_a.shape[0]
+    for j, (own, came, part) in enumerate(((own_a, came_a, part_a), (own_b, came_b, part_b))):
+        part[:count] = own[...]
+        part[count:] = came[...]
+        both[j] = came[...]
+
+
+def both_kernel(came_a, came_b, both):
+    both[0] = came_a[...]
+    both[1] = came_b[...]
+
+
+def gather(kernel, *pieces):
+    count, moms, rows, width = pieces[0].shape
+    shapes = {
+        halve_kernel: [(2 * count, moms, rows, width // 2)] * 2 + [(2, 2 * count, moms, rows, width // 2)],
+        pair_kernel: [(2 * count, moms, rows, width)] * 2 + [(2, count, moms, rows, width)],
+        both_kernel: [(2, count, moms, rows, width)],
+    }[kernel]
     vmem = pl.BlockSpec(memory_space=pltpu.VMEM)
     return pl.pallas_call(
-        prepare_kernel,
+        kernel,
+        out_shape=[jax.ShapeDtypeStruct(shape, BF16) for shape in shapes],
+        in_specs=[vmem] * len(pieces),
+        out_specs=[vmem] * len(shapes),
+        compiler_params=params(),
+        cost_estimate=cost(0, 4 * len(pieces) * pieces[0].size),
+        name="gather",
+    )(*pieces)
+
+
+def prepare_kernel(groups, place, *refs):
+    fields, (left, sink) = refs[:-2], refs[-2:]
+    moms, piece_rows, vectors = fields[0].shape[2:]
+    columns = left.shape[1] // (2 * moms)
+    per = columns // piece_rows
+    x = place[X]
+    for t in range(2):
+        for p, here in enumerate((place[HERE_A], place[HERE_B])):
+            j = 0
+            for field in fields[t * groups : (t + 1) * groups]:
+                for i in range(field.shape[1]):
+                    q = here ^ j
+                    j += 1
+                    to_sink = pl.ds(pl.multiple_of(p * vectors + q * piece_rows, piece_rows), piece_rows)
+                    for m in range(moms):
+                        sink[t, m, to_sink] = field[p, i, m]
+
+                    @pl.when(q // per == x)
+                    def _(field=field, i=i, q=q):
+                        for m in range(moms):
+                            rows = field[p, i, m]
+                            at = pl.multiple_of(2 * m * columns + (q - x * per) * piece_rows, piece_rows)
+                            up, down = pl.ds(at, piece_rows), pl.ds(at + columns, piece_rows)
+                            if p == 0:
+                                left[t, up, :vectors] = rows
+                                left[t, down, vectors:] = rows
+                            else:
+                                left[t, up, vectors:] = rows
+                                left[t, down, :vectors] = -rows
+
+
+def prepare(own, oth, columns, place):
+    moms, piece_rows, vectors = own[0].shape[2:]
+    vmem = pl.BlockSpec(memory_space=pltpu.VMEM)
+    return pl.pallas_call(
+        functools.partial(prepare_kernel, len(own)),
         out_shape=(
             jax.ShapeDtypeStruct((2, 2 * moms * columns, 2 * vectors), BF16),
             jax.ShapeDtypeStruct((2, moms, 2 * vectors, vectors), BF16),
         ),
-        in_specs=[pl.BlockSpec(memory_space=pltpu.SMEM)] + [vmem] * 4,
+        in_specs=[pl.BlockSpec(memory_space=pltpu.SMEM)] + [vmem] * (len(own) + len(oth)),
         out_specs=(vmem, vmem),
         compiler_params=params(),
-        cost_estimate=cost(0, 16 * own[0].size),
+        cost_estimate=cost(0, 16 * own[-1].size),
         name="prepare",
     )(place, *own, *oth)
 
@@ -216,18 +266,22 @@
 
     contract = (((1,), (1,)), ((), ()))
     right = lax.dot_general(left[src], panel[...], contract, preferred_element_type=F32).astype(BF16)
+
+    @pl.when(pair > 0)
+    def _():
+        for k in range(count):
+            store(k, pair - 1).wait()
+
+    for m in range(moms):
+        part = right[2 * m * columns : 2 * (m + 1) * columns]
+        rows = jnp.concatenate([part[:, k * vectors : (k + 1) * vectors] for k in range(count)], 0)
+        both = lax.dot_general(rows, sink[snk, m], contract, preferred_element_type=F32)
+        for k in range(count):
+            re = both[2 * k * columns : (2 * k + 1) * columns]
+            im = both[(2 * k + 1) * columns : (2 * k + 2) * columns]
+            done[k, m, 0] = (re[:, :vectors] - im[:, vectors:]).astype(BF16)
+            done[k, m, 1] = (re[:, vectors:] + im[:, :vectors]).astype(BF16)
     for k in range(count):
-        at = slice(k * vectors, (k + 1) * vectors)
-
-        @pl.when(pair > 0)
-        def _(k=k):
-            store(k, pair - 1).wait()
-
-        for m in range(moms):
-            rows = right[2 * m * columns : 2 * (m + 1) * columns, at]
-            both = lax.dot_general(rows, sink[snk, m], contract, preferred_element_type=F32)
-            done[k, m, 0] = (both[:columns, :vectors] - both[columns:, vectors:]).astype(BF16)
-            done[k, m, 1] = (both[:columns, vectors:] + both[columns:, :vectors]).astype(BF16)
         store(k, pair).start()
 
     @pl.when(pair == last)
@@ -272,11 +326,12 @@
 
 
 CHUNKS = (1, 2, 2, 2)
-HOOKS = [[], [('z', 3, 0)], [('x', 0, 0)], [], [('x', 3, 0), ('z', 1, 0)], [('z', 3, 1)], [('z', 2, 0), ('x', 1, 0), ('x', 3, 1)]]
-CALLS = ((0, 2, (0, 1, 2, 3)), (2, 2, (0, 1, 2, 3)))
-GATES = {}
+HOOKS = [[], [('z', 3, 0)], [], [('x', 0, 0)], [('x', 3, 0), ('z', 1, 0)], [('z', 3, 1)], [('z', 2, 0), ('x', 1, 0), ('x', 3, 1), ('z', 1, 1)]]
+LOCK = (False, False)
+CALLS = ((0, 2, (0, 1, 2, 3)), (2, 2, (0, 1, 3)), (2, 2, (2,)))
+GATES = {1: [('x', 2, 1)]}
 AFTER = {}
-FROM = {}
+FROM = {('z', 2, 1): 5}
 
 
 def exchange(value, axis, mask, among=lambda i: True):
@@ -293,9 +348,8 @@
     tm = lax.axis_index("tm")
     x, z = space & 1, space >> 1
     low, high = z & 1, z >> 1
-    place = jnp.stack(
-        [space, x, z, low, high, x * 4 + low * 2 + high, low * 4 + x * 2 + high]
-    ).astype(jnp.int32)
+    where = [space, x, z, low, high, x * 4 + low * 2 + high, low * 4 + x * 2 + high]
+    place = jnp.stack([value.astype(jnp.int32) for value in (*where, *momenta.reshape(-1))])
     other = (pair_list != tm).astype(jnp.int32)
     other_src, other_snk = other[:, 0], other[:, 1]
 
@@ -303,7 +357,7 @@
     plan = [
         (d, c * (pair_count // n), pair_count // n) for d, n in enumerate(CHUNKS) for c in range(n)
     ]
-    send_a, send_b, keep_a, keep_b = gram_halves(eigvecs[0], momenta, place, factor)
+    send_a, send_b, keep_a, keep_b = gram_halves(eigvecs[0], moms, place, factor)
     blocks = cut_panels(panels, vectors, plan, CUT_VMEM, place)
 
     raw, held, steps = {}, {}, []
@@ -342,14 +396,29 @@
     (came,) = step((send, high_z))
     field = (keep + came.astype(F32)).astype(BF16)[None]
     (came,) = step((field, high_z))
-    field = jnp.concatenate([field, came], 0)
-    parts = [field[..., :vectors], field[..., vectors:]]
+    own, oth = [], []
+
+    def share(both):
+        own.append(both)
+        oth.append(exchange(both, "tm", 1))
+
+    def after_share(value, count):
+        if len(oth) >= count:
+            value, oth[count - 1] = lax.optimization_barrier((value, oth[count - 1]))
+        return value
+
+    *parts, both = gather(halve_kernel, field, came)
+    share(both)
     came = step((parts[0], low_z), (parts[1], along_x))
-    parts = [jnp.concatenate([part, new], 0) for part, new in zip(parts, came)]
+    if LOCK[0]:
+        came[0] = after_share(came[0], 1)
+    *parts, both = gather(pair_kernel, *parts, *came)
+    share(both)
     came = step((parts[0], along_x), (parts[1], low_z))
-    own = [jnp.concatenate([part, new], 0) for part, new in zip(parts, came)]
-    oth = [exchange(part, "tm", 1) for part in own]
-    oth[0] = meet(oth[0], HOOKS[6])
+    if LOCK[1]:
+        came[0] = after_share(came[0], 2)
+    share(*gather(both_kernel, *came))
+    oth[2] = meet(oth[2], HOOKS[6])
 
     columns = width // space_count
     out_shape = jax.ShapeDtypeStruct((pair_count, moms, 2, columns, width), BF16)

time: 100 us -> 92.9 us (0.929)
  starting transfers between devices: 36.5 us -> 31.3 us
  waiting for transfers between devices: 37.6 us -> 33.2 us
  other arithmetic: 3.58 us -> 0.03 us
  local copies, waits for them, and re-layouts: 1.78 us -> 5.19 us
  Pallas kernels: 20.6 us -> 22.8 us
    ppermute x25 -> x26, starting transfers between devices: 36.5 us -> 31.3 us  [exchange(): lax.ppermute(value, axis, [(i, i ^ mask) for i in range(lax.axis_size(axi...]
    ppermute x25 -> x26, waiting for transfers between devices: 37.6 us -> 33.2 us  [exchange(): lax.ppermute(value, axis, [(i, i ^ mask) for i in range(lax.axis_size(axi...]
    concatenate x5 -> x0, other arithmetic: 3.55 us -> none  [the longest x2 2.11 us: fast(): own = [jnp.concatenate([part, new], 0) for part, new in zip(parts, came)]]
    unnamed x14 -> x12, local copies, waits for them, and re-layouts: 1.62 us -> 4.26 us
    pallas_call x1 -> x4, Pallas kernels: 0.75 us -> 1.94 us  [the longest x1 1.09 us: prepare(): pl.pallas_call(functools.partial(prepare_kernel, len(own)), out_shape=(ja...]
    pallas_call x2 -> x3, Pallas kernels: 14.6 us -> 15.6 us  [dress(): pl.pallas_call(functools.partial(dress_kernel, dists, chained, first_pair...]
  transfers between devices with their start and end apart: 25 -> 26, of which waited for: 11 -> 10; matrix products, arithmetic and copies ran while one was open for 4% -> 0% of each run, Pallas kernels for 12% -> 18%
where the time goes in v3:
time: 92.9 us; the launch traced here: 92.6 us
  waiting for transfers between devices  33.2 us (36%)
  starting transfers between devices  31.3 us (34%)
  Pallas kernels  22.8 us (25%)
  local copies, waits for them, and re-layouts  5.19 us (6%)
    ppermute x26, waiting for transfers between devices, exchange(): lax.ppermute(value, axis, [(i, i ^ mask) for i in range(lax.axis_size(axi...  33.2 us
    ppermute x26, starting transfers between devices, exchange(): lax.ppermute(value, axis, [(i, i ^ mask) for i in range(lax.axis_size(axi...  31.3 us
    pallas_call x3, Pallas kernels, dress(): pl.pallas_call(functools.partial(dress_kernel, dists, chained, first_pair...  15.6 us
    unnamed x12, local copies, waits for them, and re-layouts  4.26 us
    pallas_call x1, Pallas kernels, gram_halves(): pl.pallas_call(functools.partial(gram_kernel, factor), out_shape=[jax.Sha...  2.35 us
  transfers between devices with their start and end apart: 26, of which 10 were waited for; matrix products, arithmetic and copies ran while one was open for 0% of the time, Pallas kernels for 18%

profile of v3, /device:TPU:0, one launch (start us, length us, event | category | flops | bytes accessed | tf_op | source)
XLA Modules:
  0.0 92.6 jit_solution(8775547783628350470)
XLA Ops:
  0.0 0.8 reshape.7
  0.8 0.1 stack.31.place
  0.9 1.1 %copy-done.3 = bf16[1,2,3,192,256]{4,3,2,1,0:T(8,128)(2,1)S(1)} copy-done((bf16[1,2,3,192,256]{4,3,2,1,0:T(8,128)(2,1)S(1)}, bf16[1,2,3,192,256]{4,3,2,1,0:T(8,128)(2,1)}, u32[]{:S(2)}) %copy-start.3) | copy-done | bytes 589848
  1.9 2.4 %gram.1 = (bf16[3,128,256]{2,1,0:T(8,128)(2,1)S(1)}, bf16[3,128,256]{2,1,0:T(8,128)(2,1)S(1)}, f32[3,128,256]{2,1,0:T(8,128)S(1)}, f32[3,128,256]{2,1,0:T(8,128)S(1)}) custom-call(s32[16]{0:T(128)S(1)} %stack.31.place, bf16[2,3,192,256]{3,2,1,0:T(8,128)(2,1)S(1)} %bitcast.18), custom_call_target="tpu_custom_call" | custom-call | flops 905969664 | bytes 3145728 | tf_op jit(solution)/shard_map/gram/pallas_call | solution.py:70
  4.3 3.0 %collective-permute-start = (bf16[3,128,256]{2,1,0:T(8,128)(2,1)S(1)}, bf16[3,128,256]{2,1,0:T(8,128)(2,1)S(1)}, u32[]{:S(2)}, u32[]{:S(2)}) collective-permute-start(bf16[3,128,256]{2,1,0:T(8,128)(2,1)S(1)} %get-tuple-element.49), channel_id=1, source_target_pairs={{0,2},{2,0},{4,6},{6,4},{8,10},{10,8},{12,14},{14,12},{1,3},{3,1},... | collective-permute-start | bytes 589832 | tf_op jit(solution)/shard_map/ppermute | solution.py:338
  7.3 1.6 %collective-permute-start.1 = (bf16[3,128,256]{2,1,0:T(8,128)(2,1)S(1)}, bf16[3,128,256]{2,1,0:T(8,128)(2,1)S(1)}, u32[]{:S(2)}, u32[]{:S(2)}) collective-permute-start(bf16[3,128,256]{2,1,0:T(8,128)(2,1)S(1)} %get-tuple-element.50), channel_id=1, source_target_pairs={{0,4},{2,6},{4,0},{6,2},{8,12},{10,14},{12,8},{14,10},{1,5},{3,7},... | collective-permute-start | bytes 589832 | tf_op jit(solution)/shard_map/ppermute | solution.py:338
  8.9 1.6 %copy-done = bf16[4,2,128,1024]{3,2,1,0:T(8,128)(2,1)S(1)} copy-done((bf16[4,2,128,1024]{3,2,1,0:T(8,128)(2,1)S(1)}, bf16[4,2,128,1024]{3,2,1,0:T(8,128)(2,1)}, u32[]{:S(2)}) %copy-start) | copy-done | bytes 2097176
  10.5 1.7 %cut.1 = (bf16[4,2,128,256]{3,2,1,0:T(8,128)(2,1)S(1)}, bf16[2,2,128,256]{3,2,1,0:T(8,128)(2,1)S(1)}, bf16[2,2,128,256]{3,2,1,0:T(8,128)(2,1)}, bf16[2,2,128,256...) custom-call(s32[16]{0:T(128)S(1)} %stack.31.place, ...), custom_call_target="tpu_custom_call" | custom-call | bytes 4194304 | tf_op jit(solution)/shard_map/cut/pallas_call | solution.py:99
  12.2 2.5 %collective-permute-start.3 = (bf16[2,2,128,256]{3,2,1,0:T(8,128)(2,1)S(1)}, bf16[2,2,128,256]{3,2,1,0:T(8,128)(2,1)S(1)}, u32[]{:S(2)}, u32[]{:S(2)}) collective-permute-start(bf16[2,2,128,256]{3,2,1,0:T(8,128)(2,1)S(1)} %get-tuple-element.54), channel_id=1, source_target_pairs={{0,12},{2,14},{4,8},{6,10},{8,4},{10,6},{12,0},{14,2},{1,13},{3,15... | collective-permute-start | bytes 786440 | tf_op jit(solution)/shard_map/ppermute | solution.py:338
  14.7 0.6 fold.2
  15.4 0.7 collective-permute-start.2
  16.1 0.5 collective-permute-start.4
  16.6 1.5 %collective-permute-start.7 = (bf16[4,2,128,256]{3,2,1,0:T(8,128)(2,1)S(1)}, bf16[4,2,128,256]{3,2,1,0:T(8,128)(2,1)S(1)}, u32[]{:S(2)}, u32[]{:S(2)}) collective-permute-start(bf16[4,2,128,256]{3,2,1,0:T(8,128)(2,1)S(1)} %get-tuple-element.59.refs_0_), channel_id=1, source_target_pairs={{0,2},{2,0},{4,6},{6,4},{8,10},{10,8},{12,14},{14,12},{1,3},{3,1},... | collective-permute-start | bytes 1572872 | tf_op jit(solution)/shard_map/ppermute | solution.py:338
  18.1 4.6 %collective-permute-done.3.refs_3_ = bf16[2,2,128,256]{3,2,1,0:T(8,128)(2,1)S(1)} collective-permute-done((bf16[2,2,128,256]{3,2,1,0:T(8,128)(2,1)S(1)}, bf16[2,2,128,256]{3,2,1,0:T(8,128)(2,1)S(1)}, u32[]{:S(2)}, u32[]{:S(2)}) %collective-permute-start.3) | collective-permute-done | bytes 262176 | tf_op jit(solution)/shard_map/ppermute | solution.py:338
  22.8 1.0 %collective-permute-done.2.came_a = bf16[3,64,256]{2,1,0:T(8,128)(2,1)S(1)} collective-permute-done((bf16[3,64,256]{2,1,0:T(8,128)(2,1)S(1)}, bf16[3,64,256]{2,1,0:T(8,128)(2,1)S(1)}, u32[]{:S(2)}, u32[]{:S(2)}) %collective-permute-start.2) | collective-permute-done | bytes 98336 | tf_op jit(solution)/shard_map/ppermute | solution.py:338
  23.8 0.6 fold.3
  24.3 4.3 %collective-permute-start.5 = (bf16[3,32,512]{2,1,0:T(8,128)(2,1)S(1)}, bf16[3,32,512]{2,1,0:T(8,128)(2,1)S(1)}, u32[]{:S(2)}, u32[]{:S(2)}) collective-permute-start(bf16[3,32,512]{2,1,0:T(8,128)(2,1)S(1)} %get-tuple-element.58), channel_id=1, source_target_pairs={{0,8},{2,10},{4,12},{6,14},{8,0},{10,2},{12,4},{14,6},{1,9},{3,11}... | collective-permute-start | bytes 294920 | tf_op jit(solution)/shard_map/ppermute | solution.py:338
  28.6 0.5 collective-permute-start.9
  29.2 3.0 %collective-permute-done.5 = bf16[3,32,512]{2,1,0:T(8,128)(2,1)S(1)} collective-permute-done((bf16[3,32,512]{2,1,0:T(8,128)(2,1)S(1)}, bf16[3,32,512]{2,1,0:T(8,128)(2,1)S(1)}, u32[]{:S(2)}, u32[]{:S(2)}) %collective-permute-start.5) | collective-permute-done | bytes 98336 | tf_op jit(solution)/shard_map/ppermute | solution.py:338
  32.2 3.1 %collective-permute-start.6 = (bf16[1,3,32,512]{3,2,1,0:T(8,128)(2,1)S(1)}, bf16[1,3,32,512]{3,2,1,0:T(8,128)(2,1)S(1)}, u32[]{:S(2)}, u32[]{:S(2)}) collective-permute-start(bf16[1,3,32,512]{3,2,1,0:T(8,128)(2,1)S(1)} %fusion.field), channel_id=1, source_target_pairs={{0,8},{2,10},{4,12},{6,14},{8,0},{10,2},{12,4},{14,6},{1,9},{3,11}... | collective-permute-start | bytes 294920 | tf_op jit(solution)/shard_map/ppermute | solution.py:338
  35.3 1.2 %collective-permute-start.13 = (bf16[2,2,128,256]{3,2,1,0:T(8,128)(2,1)S(1)}, bf16[2,2,128,256]{3,2,1,0:T(8,128)(2,1)S(1)}, u32[]{:S(2)}, u32[]{:S(2)}) collective-permute-start(bf16[2,2,128,256]{3,2,1,0:T(8,128)(2,1)S(1)} %get-tuple-element.68), channel_id=1, source_target_pairs={{0,12},{2,14},{4,8},{6,10},{8,4},{10,6},{12,0},{14,2},{1,13},{3,15... | collective-permute-start | bytes 786440 | tf_op jit(solution)/shard_map/ppermute | solution.py:338
  36.5 8.4 %collective-permute-done.6.came = bf16[1,3,32,512]{3,2,1,0:T(8,128)(2,1)S(1)} collective-permute-done((bf16[1,3,32,512]{3,2,1,0:T(8,128)(2,1)S(1)}, bf16[1,3,32,512]{3,2,1,0:T(8,128)(2,1)S(1)}, u32[]{:S(2)}, u32[]{:S(2)}) %collective-permute-start.6) | collective-permute-done | bytes 98336 | tf_op jit(solution)/shard_map/ppermute | solution.py:338
  45.1 0.6 collective-permute-start.11
  45.6 2.0 %collective-permute-start.18 = (bf16[2,2,128,256]{3,2,1,0:T(8,128)(2,1)}, bf16[2,2,128,256]{3,2,1,0:T(8,128)(2,1)S(1)}, u32[]{:S(2)}, u32[]{:S(2)}) collective-permute-start(bf16[2,2,128,256]{3,2,1,0:T(8,128)(2,1)} %get-tuple-element.71), channel_id=1, source_target_pairs={{0,8},{2,10},{4,12},{6,14},{8,0},{10,2},{12,4},{14,6},{1,9},{3,11}... | collective-permute-start | bytes 786440 | tf_op jit(solution)/shard_map/ppermute | solution.py:338
  47.6 2.7 %collective-permute-done.8.came_a = bf16[2,3,32,256]{3,2,1,0:T(8,128)(2,1)S(1)} collective-permute-done((bf16[2,3,32,256]{3,2,1,0:T(8,128)(2,1)S(1)}, bf16[2,3,32,256]{3,2,1,0:T(8,128)(2,1)S(1)}, u32[]{:S(2)}, u32[]{:S(2)}) %collective-permute-start.8) | collective-permute-done | bytes 98336 | tf_op jit(solution)/shard_map/ppermute | solution.py:338
  50.3 0.5 collective-permute-done.11.came_b
  50.8 0.8 gather.4
  51.6 0.7 copy-done.1
  52.3 0.5 collective-permute-start.12
  52.8 1.9 %collective-permute-start.14 = (bf16[4,3,32,256]{3,2,1,0:T(8,128)(2,1)}, bf16[4,3,32,256]{3,2,1,0:T(8,128)(2,1)S(1)}, u32[]{:S(2)}, u32[]{:S(2)}) collective-permute-start(bf16[4,3,32,256]{3,2,1,0:T(8,128)(2,1)} %get-tuple-element.70), channel_id=1, source_target_pairs={{0,4},{2,6},{4,0},{6,2},{8,12},{10,14},{12,8},{14,10},{1,5},{3,7},... | collective-permute-start | bytes 589832 | tf_op jit(solution)/shard_map/ppermute | solution.py:338
  54.7 0.1 collective-permute-start.21
  54.8 1.5 %collective-permute-start.19 = (bf16[2,2,128,256]{3,2,1,0:T(8,128)(2,1)S(1)}, bf16[2,2,128,256]{3,2,1,0:T(8,128)(2,1)S(1)}, u32[]{:S(2)}, u32[]{:S(2)}) collective-permute-start(bf16[2,2,128,256]{3,2,1,0:T(8,128)(2,1)S(1)} %collective-permute-done.10.refs_1_), channel_id=1, source_target_pairs={{0,2},{2,0},{4,6},{6,4},{8,10},{10,8},{12,14},{14,12},{1,3},{3,1},... | collective-permute-start | bytes 786440 | tf_op jit(solution)/shard_map/ppermute | solution.py:338
  56.3 5.1 %collective-permute-done.18.refs_2_ = bf16[2,2,128,256]{3,2,1,0:T(8,128)(2,1)S(1)} collective-permute-done((bf16[2,2,128,256]{3,2,1,0:T(8,128)(2,1)}, bf16[2,2,128,256]{3,2,1,0:T(8,128)(2,1)S(1)}, u32[]{:S(2)}, u32[]{:S(2)}) %collective-permute-start.18) | collective-permute-done | bytes 262176 | tf_op jit(solution)/shard_map/ppermute | solution.py:338
  61.4 0.5 collective-permute-start.20
  61.9 1.5 %collective-permute-start.23 = (bf16[2,2,128,256]{3,2,1,0:T(8,128)(2,1)S(1)}, bf16[2,2,128,256]{3,2,1,0:T(8,128)(2,1)S(1)}, u32[]{:S(2)}, u32[]{:S(2)}) collective-permute-start(bf16[2,2,128,256]{3,2,1,0:T(8,128)(2,1)S(1)} %collective-permute-done.18.refs_2_), channel_id=1, source_target_pairs={{0,2},{2,0},{4,6},{6,4},{8,10},{10,8},{12,14},{14,12},{1,3},{3,1},... | collective-permute-start | bytes 786440 | tf_op jit(solution)/shard_map/ppermute | solution.py:338
  63.5 2.1 %collective-permute-done.21.refs_1_ = bf16[2,2,128,256]{3,2,1,0:T(8,128)(2,1)S(1)} collective-permute-done((bf16[2,2,128,256]{3,2,1,0:T(8,128)(2,1)}, bf16[2,2,128,256]{3,2,1,0:T(8,128)(2,1)S(1)}, u32[]{:S(2)}, u32[]{:S(2)}) %collective-permute-start.21) | collective-permute-done | bytes 262176 | tf_op jit(solution)/shard_map/ppermute | solution.py:338
  65.7 0.5 collective-permute-start.16
  66.2 0.1 slice_bitcast_fusion
  66.3 4.4 %collective-permute-done.20.refs_5_ = bf16[2,2,128,256]{3,2,1,0:T(8,128)(2,1)S(1)} collective-permute-done((bf16[2,2,128,256]{3,2,1,0:T(8,128)(2,1)S(1)}, bf16[2,2,128,256]{3,2,1,0:T(8,128)(2,1)S(1)}, u32[]{:S(2)}, u32[]{:S(2)}) %collective-permute-start.20) | collective-permute-done | bytes 262176 | tf_op jit(solution)/shard_map/ppermute | solution.py:338
  70.6 0.5 collective-permute-start.25
  71.1 1.7 %collective-permute-start.22 = (bf16[2,2,128,256]{3,2,1,0:T(8,128)(2,1)}, bf16[2,2,128,256]{3,2,1,0:T(8,128)(2,1)S(1)}, u32[]{:S(2)}, u32[]{:S(2)}) collective-permute-start(bf16[2,2,128,256]{3,2,1,0:T(8,128)(2,1)} %copy-done.4), channel_id=1, source_target_pairs={{0,8},{2,10},{4,12},{6,14},{8,0},{10,2},{12,4},{14,6},{1,9},{3,11}... | collective-permute-start | bytes 786440 | tf_op jit(solution)/shard_map/ppermute | solution.py:338
  72.9 0.9 copy-done.2
  73.8 1.1 %prepare.1 = (bf16[2,768,512]{2,1,0:T(8,128)(2,1)S(1)}, bf16[2,3,512,256]{3,2,1,0:T(8,128)(2,1)S(1)}) custom-call(s32[16]{0:T(128)S(1)} %stack.31.place, bf16[2,2,3,32,256]{4,3,2,1,0:T(8,128)(2,1)S(1)} %get-tuple-element.61.refs_0_, bf16[2,2,3,32,256]{4,3,2,1,0:T(8,128)(2,1)S(1)} %copy-done.2, bf16[2,4,3,32,256]{4,3,2,1,0:T(8,128)(2,1)S(1)} %gather.5.refs_2_, ...), custom_call_target="tpu_custom_call" | custom-call | bytes 3145728 | tf_op jit(solution)/shard_map/prepare/pallas_call | solution.py:230
  74.9 1.4 %collective-permute-done.23.refs_6_ = bf16[2,2,128,256]{3,2,1,0:T(8,128)(2,1)S(1)} collective-permute-done((bf16[2,2,128,256]{3,2,1,0:T(8,128)(2,1)S(1)}, bf16[2,2,128,256]{3,2,1,0:T(8,128)(2,1)S(1)}, u32[]{:S(2)}, u32[]{:S(2)}) %collective-permute-start.23) | collective-permute-done | bytes 262176 | tf_op jit(solution)/shard_map/ppermute | solution.py:338
  76.2 6.0 %dress.3.refs_6_ = bf16[4,3,2,128,1024]{4,3,2,1,0:T(8,128)(2,1)} custom-call(s32[16]{0:T(128)S(1)} %stack.31.place, s32[2]{0:T(128)S(1)} %get-tuple-element.90.other_src, s32[2]{0:T(128)S(1)} %get-tuple-element.89.other_snk, bf16[2,768,512]{2,1,0:T(8,128)(2,1)S(1)} %get-tuple-element.74.left, bf16[2,3,512,256]{3,2,1,0:T(8,128)(2,1)S(1)} %get-tuple-element.75.sink, ...), custom_call_target="tpu_custom_call" | custom-call | flops 3221225472 | bytes 2097152 | tf_op jit(solution)/shard_map/dress/pallas_call | solution.py:307
  82.3 0.8 collective-permute-start.24
  83.0 5.7 %dress.4.refs_2_ = bf16[4,3,2,128,1024]{4,3,2,1,0:T(8,128)(2,1)} custom-call(s32[16]{0:T(128)S(1)} %stack.31.place, s32[2]{0:T(128)S(1)} %get-tuple-element.92.other_src, s32[2]{0:T(128)S(1)} %get-tuple-element.91.other_snk, bf16[2,768,512]{2,1,0:T(8,128)(2,1)S(1)} %get-tuple-element.74.left, ...), custom_call_target="tpu_custom_call", output_to_operand_aliasing={{}: (11, {})} | custom-call | flops 2415919104 | bytes 2097152 | tf_op jit(solution)/shard_map/dress/pallas_call | solution.py:307
  88.8 3.9 %dress.5 = bf16[4,3,2,128,1024]{4,3,2,1,0:T(8,128)(2,1)} custom-call(s32[16]{0:T(128)S(1)} %stack.31.place, s32[2]{0:T(128)S(1)} %get-tuple-element.92.other_src, s32[2]{0:T(128)S(1)} %get-tuple-element.91.other_snk, bf16[2,768,512]{2,1,0:T(8,128)(2,1)S(1)} %get-tuple-element.74.left, ...), custom_call_target="tpu_custom_call", output_to_operand_aliasing={{}: (7, {})} | custom-call | flops 805306368 | bytes 2097152 | tf_op jit(solution)/shard_map/dress/pallas_call | solution.py:307
  (32 shorter events, 0.3 us)
Async XLA Ops:
  0.0 63.5 %copy-start.5 = (s32[4,2]{0,1:T(2,128)S(1)}, s32[4,2]{0,1:T(2,128)}, u32[]{:S(2)}) copy-start(s32[4,2]{0,1:T(2,128)} %param.6) | copy-start | bytes 100
  0.9 1.1 %copy-start.3 = (bf16[1,2,3,192,256]{4,3,2,1,0:T(8,128)(2,1)S(1)}, bf16[1,2,3,192,256]{4,3,2,1,0:T(8,128)(2,1)}, u32[]{:S(2)}) copy-start(bf16[1,2,3,192,256]{4,3,2,1,0:T(8,128)(2,1)} %param.4) | copy-start | bytes 1769476
  4.3 10.4 %collective-permute-start = (bf16[3,128,256]{2,1,0:T(8,128)(2,1)S(1)}, bf16[3,128,256]{2,1,0:T(8,128)(2,1)S(1)}, u32[]{:S(2)}, u32[]{:S(2)}) collective-permute-start(bf16[3,128,256]{2,1,0:T(8,128)(2,1)S(1)} %get-tuple-element.49), channel_id=1, source_target_pairs={{0,2},{2,0},{4,6},{6,4},{8,10},{10,8},{12,14},{14,12},{1,3},{3,1},... | collective-permute-start | bytes 589832 | tf_op jit(solution)/shard_map/ppermute | solution.py:338
  7.3 7.5 %collective-permute-start.1 = (bf16[3,128,256]{2,1,0:T(8,128)(2,1)S(1)}, bf16[3,128,256]{2,1,0:T(8,128)(2,1)S(1)}, u32[]{:S(2)}, u32[]{:S(2)}) collective-permute-start(bf16[3,128,256]{2,1,0:T(8,128)(2,1)S(1)} %get-tuple-element.50), channel_id=1, source_target_pairs={{0,4},{2,6},{4,0},{6,2},{8,12},{10,14},{12,8},{14,10},{1,5},{3,7},... | collective-permute-start | bytes 589832 | tf_op jit(solution)/shard_map/ppermute | solution.py:338
  8.9 1.6 %copy-start = (bf16[4,2,128,1024]{3,2,1,0:T(8,128)(2,1)S(1)}, bf16[4,2,128,1024]{3,2,1,0:T(8,128)(2,1)}, u32[]{:S(2)}) copy-start(bf16[4,2,128,1024]{3,2,1,0:T(8,128)(2,1)} %panels.1) | copy-start | bytes 6291460
  12.2 42.6 %copy-start.4 = (bf16[2,2,128,256]{3,2,1,0:T(8,128)(2,1)}, bf16[2,2,128,256]{3,2,1,0:T(8,128)(2,1)S(1)}, u32[]{:S(2)}) copy-start(bf16[2,2,128,256]{3,2,1,0:T(8,128)(2,1)S(1)} %get-tuple-element.77) | copy-start | bytes 786436
  12.2 10.6 %collective-permute-start.3 = (bf16[2,2,128,256]{3,2,1,0:T(8,128)(2,1)S(1)}, bf16[2,2,128,256]{3,2,1,0:T(8,128)(2,1)S(1)}, u32[]{:S(2)}, u32[]{:S(2)}) collective-permute-start(bf16[2,2,128,256]{3,2,1,0:T(8,128)(2,1)S(1)} %get-tuple-element.54), channel_id=1, source_target_pairs={{0,12},{2,14},{4,8},{6,10},{8,4},{10,6},{12,0},{14,2},{1,13},{3,15... | collective-permute-start | bytes 786440 | tf_op jit(solution)/shard_map/ppermute | solution.py:338
  15.4 8.4 %collective-permute-start.2 = (bf16[3,64,256]{2,1,0:T(8,128)(2,1)S(1)}, bf16[3,64,256]{2,1,0:T(8,128)(2,1)S(1)}, u32[]{:S(2)}, u32[]{:S(2)}) collective-permute-start(bf16[3,64,256]{2,1,0:T(8,128)(2,1)S(1)} %get-tuple-element.53), channel_id=1, source_target_pairs={{0,4},{2,6},{4,0},{6,2},{8,12},{10,14},{12,8},{14,10},{1,5},{3,7},... | collective-permute-start | bytes 294920 | tf_op jit(solution)/shard_map/ppermute | solution.py:338
  16.1 7.7 %collective-permute-start.4 = (bf16[3,64,256]{2,1,0:T(8,128)(2,1)S(1)}, bf16[3,64,256]{2,1,0:T(8,128)(2,1)S(1)}, u32[]{:S(2)}, u32[]{:S(2)}) collective-permute-start(bf16[3,64,256]{2,1,0:T(8,128)(2,1)S(1)} %get-tuple-element.56), channel_id=1, source_target_pairs={{0,2},{2,0},{4,6},{6,4},{8,10},{10,8},{12,14},{14,12},{1,3},{3,1},... | collective-permute-start | bytes 294920 | tf_op jit(solution)/shard_map/ppermute | solution.py:338
  16.6 28.3 %collective-permute-start.7 = (bf16[4,2,128,256]{3,2,1,0:T(8,128)(2,1)S(1)}, bf16[4,2,128,256]{3,2,1,0:T(8,128)(2,1)S(1)}, u32[]{:S(2)}, u32[]{:S(2)}) collective-permute-start(bf16[4,2,128,256]{3,2,1,0:T(8,128)(2,1)S(1)} %get-tuple-element.59.refs_0_), channel_id=1, source_target_pairs={{0,2},{2,0},{4,6},{6,4},{8,10},{10,8},{12,14},{14,12},{1,3},{3,1},... | collective-permute-start | bytes 1572872 | tf_op jit(solution)/shard_map/ppermute | solution.py:338
  24.3 7.8 %collective-permute-start.5 = (bf16[3,32,512]{2,1,0:T(8,128)(2,1)S(1)}, bf16[3,32,512]{2,1,0:T(8,128)(2,1)S(1)}, u32[]{:S(2)}, u32[]{:S(2)}) collective-permute-start(bf16[3,32,512]{2,1,0:T(8,128)(2,1)S(1)} %get-tuple-element.58), channel_id=1, source_target_pairs={{0,8},{2,10},{4,12},{6,14},{8,0},{10,2},{12,4},{14,6},{1,9},{3,11}... | collective-permute-start | bytes 294920 | tf_op jit(solution)/shard_map/ppermute | solution.py:338
  28.6 17.0 %collective-permute-start.10 = (bf16[2,2,128,256]{3,2,1,0:T(8,128)(2,1)S(1)}, bf16[2,2,128,256]{3,2,1,0:T(8,128)(2,1)S(1)}, u32[]{:S(2)}, u32[]{:S(2)}) collective-permute-start(bf16[2,2,128,256]{3,2,1,0:T(8,128)(2,1)S(1)} %get-tuple-element.64), channel_id=1, source_target_pairs={{0,4},{2,6},{4,0},{6,2},{8,12},{10,14},{12,8},{14,10},{1,5},{3,7},... | collective-permute-start | bytes 786440 | tf_op jit(solution)/shard_map/ppermute | solution.py:338
  28.6 19.0 %collective-permute-start.9 = (bf16[2,2,128,256]{3,2,1,0:T(8,128)(2,1)S(1)}, bf16[2,2,128,256]{3,2,1,0:T(8,128)(2,1)S(1)}, u32[]{:S(2)}, u32[]{:S(2)}) collective-permute-start(bf16[2,2,128,256]{3,2,1,0:T(8,128)(2,1)S(1)} %collective-permute-done.3.refs_3_), channel_id=1, source_target_pairs={{0,2},{2,0},{4,6},{6,4},{8,10},{10,8},{12,14},{14,12},{1,3},{3,1},... | collective-permute-start | bytes 786440 | tf_op jit(solution)/shard_map/ppermute | solution.py:338
  32.2 12.7 %collective-permute-start.6 = (bf16[1,3,32,512]{3,2,1,0:T(8,128)(2,1)S(1)}, bf16[1,3,32,512]{3,2,1,0:T(8,128)(2,1)S(1)}, u32[]{:S(2)}, u32[]{:S(2)}) collective-permute-start(bf16[1,3,32,512]{3,2,1,0:T(8,128)(2,1)S(1)} %fusion.field), channel_id=1, source_target_pairs={{0,8},{2,10},{4,12},{6,14},{8,0},{10,2},{12,4},{14,6},{1,9},{3,11}... | collective-permute-start | bytes 294920 | tf_op jit(solution)/shard_map/ppermute | solution.py:338
  35.3 19.5 %collective-permute-start.13 = (bf16[2,2,128,256]{3,2,1,0:T(8,128)(2,1)S(1)}, bf16[2,2,128,256]{3,2,1,0:T(8,128)(2,1)S(1)}, u32[]{:S(2)}, u32[]{:S(2)}) collective-permute-start(bf16[2,2,128,256]{3,2,1,0:T(8,128)(2,1)S(1)} %get-tuple-element.68), channel_id=1, source_target_pairs={{0,12},{2,14},{4,8},{6,10},{8,4},{10,6},{12,0},{14,2},{1,13},{3,15... | collective-permute-start | bytes 786440 | tf_op jit(solution)/shard_map/ppermute | solution.py:338
  45.0 5.3 %collective-permute-start.8 = (bf16[2,3,32,256]{3,2,1,0:T(8,128)(2,1)S(1)}, bf16[2,3,32,256]{3,2,1,0:T(8,128)(2,1)S(1)}, u32[]{:S(2)}, u32[]{:S(2)}) collective-permute-start(bf16[2,3,32,256]{3,2,1,0:T(8,128)(2,1)S(1)} %get-tuple-element.62.own_a), channel_id=1, source_target_pairs={{0,4},{2,6},{4,0},{6,2},{8,12},{10,14},{12,8},{14,10},{1,5},{3,7},... | collective-permute-start | bytes 294920 | tf_op jit(solution)/shard_map/ppermute | solution.py:338
  45.1 5.7 %collective-permute-start.11 = (bf16[2,3,32,256]{3,2,1,0:T(8,128)(2,1)S(1)}, bf16[2,3,32,256]{3,2,1,0:T(8,128)(2,1)S(1)}, u32[]{:S(2)}, u32[]{:S(2)}) collective-permute-start(bf16[2,3,32,256]{3,2,1,0:T(8,128)(2,1)S(1)} %get-tuple-element.63.own_b), channel_id=1, source_target_pairs={{0,2},{2,0},{4,6},{6,4},{8,10},{10,8},{12,14},{14,12},{1,3},{3,1},... | collective-permute-start | bytes 294920 | tf_op jit(solution)/shard_map/ppermute | solution.py:338
  45.6 15.7 %collective-permute-start.18 = (bf16[2,2,128,256]{3,2,1,0:T(8,128)(2,1)}, bf16[2,2,128,256]{3,2,1,0:T(8,128)(2,1)S(1)}, u32[]{:S(2)}, u32[]{:S(2)}) collective-permute-start(bf16[2,2,128,256]{3,2,1,0:T(8,128)(2,1)} %get-tuple-element.71), channel_id=1, source_target_pairs={{0,8},{2,10},{4,12},{6,14},{8,0},{10,2},{12,4},{14,6},{1,9},{3,11}... | collective-permute-start | bytes 786440 | tf_op jit(solution)/shard_map/ppermute | solution.py:338
  51.6 0.7 copy-start.1
  52.3 9.6 %collective-permute-start.12 = (bf16[4,3,32,256]{3,2,1,0:T(8,128)(2,1)}, bf16[4,3,32,256]{3,2,1,0:T(8,128)(2,1)S(1)}, u32[]{:S(2)}, u32[]{:S(2)}) collective-permute-start(bf16[4,3,32,256]{3,2,1,0:T(8,128)(2,1)} %get-tuple-element.67), channel_id=1, source_target_pairs={{0,2},{2,0},{4,6},{6,4},{8,10},{10,8},{12,14},{14,12},{1,3},{3,1},... | collective-permute-start | bytes 589832 | tf_op jit(solution)/shard_map/ppermute | solution.py:338
  52.8 10.6 %collective-permute-start.14 = (bf16[4,3,32,256]{3,2,1,0:T(8,128)(2,1)}, bf16[4,3,32,256]{3,2,1,0:T(8,128)(2,1)S(1)}, u32[]{:S(2)}, u32[]{:S(2)}) collective-permute-start(bf16[4,3,32,256]{3,2,1,0:T(8,128)(2,1)} %get-tuple-element.70), channel_id=1, source_target_pairs={{0,4},{2,6},{4,0},{6,2},{8,12},{10,14},{12,8},{14,10},{1,5},{3,7},... | collective-permute-start | bytes 589832 | tf_op jit(solution)/shard_map/ppermute | solution.py:338
  54.7 10.9 %collective-permute-start.21 = (bf16[2,2,128,256]{3,2,1,0:T(8,128)(2,1)}, bf16[2,2,128,256]{3,2,1,0:T(8,128)(2,1)S(1)}, u32[]{:S(2)}, u32[]{:S(2)}) collective-permute-start(bf16[2,2,128,256]{3,2,1,0:T(8,128)(2,1)} %get-tuple-element.72), channel_id=1, source_target_pairs={{0,4},{2,6},{4,0},{6,2},{8,12},{10,14},{12,8},{14,10},{1,5},{3,7},... | collective-permute-start | bytes 786440 | tf_op jit(solution)/shard_map/ppermute | solution.py:338
  54.8 10.9 %collective-permute-start.19 = (bf16[2,2,128,256]{3,2,1,0:T(8,128)(2,1)S(1)}, bf16[2,2,128,256]{3,2,1,0:T(8,128)(2,1)S(1)}, u32[]{:S(2)}, u32[]{:S(2)}) collective-permute-start(bf16[2,2,128,256]{3,2,1,0:T(8,128)(2,1)S(1)} %collective-permute-done.10.refs_1_), channel_id=1, source_target_pairs={{0,2},{2,0},{4,6},{6,4},{8,10},{10,8},{12,14},{14,12},{1,3},{3,1},... | collective-permute-start | bytes 786440 | tf_op jit(solution)/shard_map/ppermute | solution.py:338
  61.4 9.2 %collective-permute-start.20 = (bf16[2,2,128,256]{3,2,1,0:T(8,128)(2,1)S(1)}, bf16[2,2,128,256]{3,2,1,0:T(8,128)(2,1)S(1)}, u32[]{:S(2)}, u32[]{:S(2)}) collective-permute-start(bf16[2,2,128,256]{3,2,1,0:T(8,128)(2,1)S(1)} %collective-permute-done.13.refs_2_), channel_id=1, source_target_pairs={{0,2},{2,0},{4,6},{6,4},{8,10},{10,8},{12,14},{14,12},{1,3},{3,1},... | collective-permute-start | bytes 786440 | tf_op jit(solution)/shard_map/ppermute | solution.py:338
  61.9 14.3 %collective-permute-start.23 = (bf16[2,2,128,256]{3,2,1,0:T(8,128)(2,1)S(1)}, bf16[2,2,128,256]{3,2,1,0:T(8,128)(2,1)S(1)}, u32[]{:S(2)}, u32[]{:S(2)}) collective-permute-start(bf16[2,2,128,256]{3,2,1,0:T(8,128)(2,1)S(1)} %collective-permute-done.18.refs_2_), channel_id=1, source_target_pairs={{0,2},{2,0},{4,6},{6,4},{8,10},{10,8},{12,14},{14,12},{1,3},{3,1},... | collective-permute-start | bytes 786440 | tf_op jit(solution)/shard_map/ppermute | solution.py:338
  63.4 7.7 %collective-permute-start.17 = (bf16[2,4,3,32,256]{4,3,2,1,0:T(8,128)(2,1)S(1)}, bf16[2,4,3,32,256]{4,3,2,1,0:T(8,128)(2,1)S(1)}, u32[]{:S(2)}, u32[]{:S(2)}) collective-permute-start(bf16[2,4,3,32,256]{4,3,2,1,0:T(8,128)(2,1)S(1)} %gather.5.refs_2_), channel_id=1, source_target_pairs={{0,1},{1,0},{2,3},{3,2},{4,5},{5,4},{6,7},{7,6},{8,9},{9,8},{10,11... | collective-permute-start | bytes 1179656 | tf_op jit(solution)/shard_map/ppermute | solution.py:338
  65.7 7.2 %collective-permute-start.15 = (bf16[2,2,3,32,256]{4,3,2,1,0:T(8,128)(2,1)S(1)}, bf16[2,2,3,32,256]{4,3,2,1,0:T(8,128)(2,1)S(1)}, u32[]{:S(2)}, u32[]{:S(2)}) collective-permute-start(bf16[2,2,3,32,256]{4,3,2,1,0:T(8,128)(2,1)S(1)} %get-tuple-element.61.refs_0_), channel_id=1, source_target_pairs={{0,1},{1,0},{2,3},{3,2},{4,5},{5,4},{6,7},{7,6},{8,9},{9,8},{10,11... | collective-permute-start | bytes 589832 | tf_op jit(solution)/shard_map/ppermute | solution.py:338
  65.7 7.2 %collective-permute-start.16 = (bf16[2,2,3,32,256]{4,3,2,1,0:T(8,128)(2,1)}, bf16[2,2,3,32,256]{4,3,2,1,0:T(8,128)(2,1)S(1)}, u32[]{:S(2)}, u32[]{:S(2)}) collective-permute-start(bf16[2,2,3,32,256]{4,3,2,1,0:T(8,128)(2,1)} %copy-done.1), channel_id=1, source_target_pairs={{0,1},{1,0},{2,3},{3,2},{4,5},{5,4},{6,7},{7,6},{8,9},{9,8},{10,11... | collective-permute-start | bytes 589832 | tf_op jit(solution)/shard_map/ppermute | solution.py:338
  70.6 12.4 %collective-permute-start.25 = (bf16[2,2,128,256]{3,2,1,0:T(8,128)(2,1)S(1)}, bf16[2,2,128,256]{3,2,1,0:T(8,128)(2,1)S(1)}, u32[]{:S(2)}, u32[]{:S(2)}) collective-permute-start(bf16[2,2,128,256]{3,2,1,0:T(8,128)(2,1)S(1)} %collective-permute-done.21.refs_1_), channel_id=1, source_target_pairs={{0,2},{2,0},{4,6},{6,4},{8,10},{10,8},{12,14},{14,12},{1,3},{3,1},... | collective-permute-start | bytes 786440 | tf_op jit(solution)/shard_map/ppermute | solution.py:338
  71.1 11.1 %collective-permute-start.22 = (bf16[2,2,128,256]{3,2,1,0:T(8,128)(2,1)}, bf16[2,2,128,256]{3,2,1,0:T(8,128)(2,1)S(1)}, u32[]{:S(2)}, u32[]{:S(2)}) collective-permute-start(bf16[2,2,128,256]{3,2,1,0:T(8,128)(2,1)} %copy-done.4), channel_id=1, source_target_pairs={{0,8},{2,10},{4,12},{6,14},{8,0},{10,2},{12,4},{14,6},{1,9},{3,11}... | collective-permute-start | bytes 786440 | tf_op jit(solution)/shard_map/ppermute | solution.py:338
  72.9 0.9 %copy-start.2 = (bf16[2,2,3,32,256]{4,3,2,1,0:T(8,128)(2,1)S(1)}, bf16[2,2,3,32,256]{4,3,2,1,0:T(8,128)(2,1)}, u32[]{:S(2)}) copy-start(bf16[2,2,3,32,256]{4,3,2,1,0:T(8,128)(2,1)} %copy-done.1) | copy-start | bytes 589828
  82.3 6.5 %collective-permute-start.24 = (bf16[2,2,128,256]{3,2,1,0:T(8,128)(2,1)S(1)}, bf16[2,2,128,256]{3,2,1,0:T(8,128)(2,1)S(1)}, u32[]{:S(2)}, u32[]{:S(2)}) collective-permute-start(bf16[2,2,128,256]{3,2,1,0:T(8,128)(2,1)S(1)} %collective-permute-done.22.refs_0_), channel_id=1, source_target_pairs={{0,2},{2,0},{4,6},{6,4},{8,10},{10,8},{12,14},{14,12},{1,3},{3,1},... | collective-permute-start | bytes 786440 | tf_op jit(solution)/shard_map/ppermute | solution.py:338

commit v4 on v3

--- a/solution.py
+++ b/solution.py
@@ -326,12 +326,12 @@
 
 
 CHUNKS = (1, 2, 2, 2)
-HOOKS = [[], [('z', 3, 0)], [], [('x', 0, 0)], [('x', 3, 0), ('z', 1, 0)], [('z', 3, 1)], [('z', 2, 0), ('x', 1, 0), ('x', 3, 1), ('z', 1, 1)]]
+HOOKS = [[], [('z', 3, 0)], [], [('x', 0, 0)], [('x', 3, 0), ('z', 1, 0)], [('z', 3, 1), ('x', 1, 0)], [('z', 2, 0), ('x', 3, 1), ('z', 1, 1)]]
 LOCK = (False, False)
-CALLS = ((0, 2, (0, 1, 2, 3)), (2, 2, (0, 1, 3)), (2, 2, (2,)))
-GATES = {1: [('x', 2, 1)]}
-AFTER = {}
-FROM = {('z', 2, 1): 5}
+CALLS = ((0, 2, (0, 1, 2, 3)), (2, 2, (0, 1, 2, 3)))
+GATES = {}
+AFTER = {('x', 2, 1): [('x', 1, 1)]}
+FROM = {('z', 2, 1): 4}
 
 
 def exchange(value, axis, mask, among=lambda i: True):

time: 92.9 us -> 87.6 us (0.943)
  waiting for transfers between devices: 33.2 us -> 30.1 us
  Pallas kernels: 22.8 us -> 20.1 us
    pallas_call x3 -> x2, Pallas kernels: 15.6 us -> 12 us  [dress(): pl.pallas_call(functools.partial(dress_kernel, dists, chained, first_pair...]
    ppermute x26, waiting for transfers between devices: 33.2 us -> 30.1 us  [exchange(): lax.ppermute(value, axis, [(i, i ^ mask) for i in range(lax.axis_size(axi...]
    pallas_call x3, Pallas kernels: 0.85 us -> 1.86 us  [gather(): pl.pallas_call(kernel, out_shape=[jax.ShapeDtypeStruct(shape, BF16) for s...]
    unnamed x12 -> x14, local copies, waits for them, and re-layouts: 4.26 us -> 4.28 us
  transfers between devices with their start and end apart: 26 -> 26, of which waited for: 10 -> 12; matrix products, arithmetic and copies ran while one was open for 0% -> 0% of each run, Pallas kernels for 18% -> 13%
where the time goes in v4:
time: 87.6 us; the launch traced here: 87.4 us
  starting transfers between devices  31.7 us (36%)
  waiting for transfers between devices  30.1 us (34%)
  Pallas kernels  20.1 us (23%)
  local copies, waits for them, and re-layouts  5.35 us (6%)
    ppermute x26, starting transfers between devices, exchange(): lax.ppermute(value, axis, [(i, i ^ mask) for i in range(lax.axis_size(axi...  31.7 us
    ppermute x26, waiting for transfers between devices, exchange(): lax.ppermute(value, axis, [(i, i ^ mask) for i in range(lax.axis_size(axi...  30.1 us
    pallas_call x2, Pallas kernels, dress(): pl.pallas_call(functools.partial(dress_kernel, dists, chained, first_pair...  12 us
    unnamed x14, local copies, waits for them, and re-layouts  4.28 us
    pallas_call x1, Pallas kernels, gram_halves(): pl.pallas_call(functools.partial(gram_kernel, factor), out_shape=[jax.Sha...  2.34 us
    pallas_call x3, Pallas kernels, gather(): pl.pallas_call(kernel, out_shape=[jax.ShapeDtypeStruct(shape, BF16) for s...  1.86 us
  transfers between devices with their start and end apart: 26, of which 12 were waited for; matrix products, arithmetic and copies ran while one was open for 0% of the time, Pallas kernels for 13%

profile of v4, /device:TPU:0, one launch (start us, length us, event | category | flops | bytes accessed | tf_op | source)
XLA Modules:
  0.0 87.4 jit_solution(11917685068844582982)
XLA Ops:
  0.0 0.9 %reshape.7 = s32[9]{0:T(128)S(1)} reshape(s32[3,3]{1,0:T(4,128)} %param.5) | data formatting | bytes 72 | tf_op jit(solution)/shard_map/reshape | solution.py:352
  0.9 0.1 stack.31.place
  1.0 1.1 %copy-done.5 = bf16[1,2,3,192,256]{4,3,2,1,0:T(8,128)(2,1)S(1)} copy-done((bf16[1,2,3,192,256]{4,3,2,1,0:T(8,128)(2,1)S(1)}, bf16[1,2,3,192,256]{4,3,2,1,0:T(8,128)(2,1)}, u32[]{:S(2)}) %copy-start.5) | copy-done | bytes 589848
  2.1 2.3 %gram.1 = (bf16[3,128,256]{2,1,0:T(8,128)(2,1)S(1)}, bf16[3,128,256]{2,1,0:T(8,128)(2,1)S(1)}, f32[3,128,256]{2,1,0:T(8,128)S(1)}, f32[3,128,256]{2,1,0:T(8,128)S(1)}) custom-call(s32[16]{0:T(128)S(1)} %stack.31.place, bf16[2,3,192,256]{3,2,1,0:T(8,128)(2,1)S(1)} %bitcast.18), custom_call_target="tpu_custom_call" | custom-call | flops 905969664 | bytes 3145728 | tf_op jit(solution)/shard_map/gram/pallas_call | solution.py:70
  4.4 3.0 %collective-permute-start = (bf16[3,128,256]{2,1,0:T(8,128)(2,1)S(1)}, bf16[3,128,256]{2,1,0:T(8,128)(2,1)S(1)}, u32[]{:S(2)}, u32[]{:S(2)}) collective-permute-start(bf16[3,128,256]{2,1,0:T(8,128)(2,1)S(1)} %get-tuple-element.48), channel_id=1, source_target_pairs={{0,2},{2,0},{4,6},{6,4},{8,10},{10,8},{12,14},{14,12},{1,3},{3,1},... | collective-permute-start | bytes 589832 | tf_op jit(solution)/shard_map/ppermute | solution.py:338
  7.4 1.6 %collective-permute-start.1 = (bf16[3,128,256]{2,1,0:T(8,128)(2,1)S(1)}, bf16[3,128,256]{2,1,0:T(8,128)(2,1)S(1)}, u32[]{:S(2)}, u32[]{:S(2)}) collective-permute-start(bf16[3,128,256]{2,1,0:T(8,128)(2,1)S(1)} %get-tuple-element.49), channel_id=1, source_target_pairs={{0,4},{2,6},{4,0},{6,2},{8,12},{10,14},{12,8},{14,10},{1,5},{3,7},... | collective-permute-start | bytes 589832 | tf_op jit(solution)/shard_map/ppermute | solution.py:338
  9.0 1.6 %cut.1 = (bf16[4,2,128,256]{3,2,1,0:T(8,128)(2,1)S(1)}, bf16[2,2,128,256]{3,2,1,0:T(8,128)(2,1)S(1)}, bf16[2,2,128,256]{3,2,1,0:T(8,128)(2,1)S(1)}, bf16[2,2,128...) custom-call(s32[16]{0:T(128)S(1)} %stack.31.place, ...), custom_call_target="tpu_custom_call" | custom-call | bytes 4194304 | tf_op jit(solution)/shard_map/cut/pallas_call | solution.py:99
  10.7 2.6 %collective-permute-start.3 = (bf16[2,2,128,256]{3,2,1,0:T(8,128)(2,1)S(1)}, bf16[2,2,128,256]{3,2,1,0:T(8,128)(2,1)S(1)}, u32[]{:S(2)}, u32[]{:S(2)}) collective-permute-start(bf16[2,2,128,256]{3,2,1,0:T(8,128)(2,1)S(1)} %get-tuple-element.53), channel_id=1, source_target_pairs={{0,12},{2,14},{4,8},{6,10},{8,4},{10,6},{12,0},{14,2},{1,13},{3,15... | collective-permute-start | bytes 786440 | tf_op jit(solution)/shard_map/ppermute | solution.py:338
  13.2 0.6 collective-permute-done.1.came_b
  13.8 0.6 fold.2
  14.4 1.9 %collective-permute-start.2 = (bf16[3,64,256]{2,1,0:T(8,128)(2,1)S(1)}, bf16[3,64,256]{2,1,0:T(8,128)(2,1)S(1)}, u32[]{:S(2)}, u32[]{:S(2)}) collective-permute-start(bf16[3,64,256]{2,1,0:T(8,128)(2,1)S(1)} %get-tuple-element.52), channel_id=1, source_target_pairs={{0,4},{2,6},{4,0},{6,2},{8,12},{10,14},{12,8},{14,10},{1,5},{3,7},... | collective-permute-start | bytes 294920 | tf_op jit(solution)/shard_map/ppermute | solution.py:338
  16.3 0.5 collective-permute-start.4
  16.8 1.5 %collective-permute-start.7 = (bf16[4,2,128,256]{3,2,1,0:T(8,128)(2,1)S(1)}, bf16[4,2,128,256]{3,2,1,0:T(8,128)(2,1)S(1)}, u32[]{:S(2)}, u32[]{:S(2)}) collective-permute-start(bf16[4,2,128,256]{3,2,1,0:T(8,128)(2,1)S(1)} %get-tuple-element.58.refs_0_), channel_id=1, source_target_pairs={{0,2},{2,0},{4,6},{6,4},{8,10},{10,8},{12,14},{14,12},{1,3},{3,1},... | collective-permute-start | bytes 1572872 | tf_op jit(solution)/shard_map/ppermute | solution.py:338
  18.3 4.3 %collective-permute-done.3.refs_3_ = bf16[2,2,128,256]{3,2,1,0:T(8,128)(2,1)S(1)} collective-permute-done((bf16[2,2,128,256]{3,2,1,0:T(8,128)(2,1)S(1)}, bf16[2,2,128,256]{3,2,1,0:T(8,128)(2,1)S(1)}, u32[]{:S(2)}, u32[]{:S(2)}) %collective-permute-start.3) | collective-permute-done | bytes 262176 | tf_op jit(solution)/shard_map/ppermute | solution.py:338
  22.6 0.2 collective-permute-done.2.came_a
  22.8 0.6 fold.3
  23.4 4.9 %collective-permute-start.5 = (bf16[3,32,512]{2,1,0:T(8,128)(2,1)S(1)}, bf16[3,32,512]{2,1,0:T(8,128)(2,1)S(1)}, u32[]{:S(2)}, u32[]{:S(2)}) collective-permute-start(bf16[3,32,512]{2,1,0:T(8,128)(2,1)S(1)} %get-tuple-element.57), channel_id=1, source_target_pairs={{0,8},{2,10},{4,12},{6,14},{8,0},{10,2},{12,4},{14,6},{1,9},{3,11}... | collective-permute-start | bytes 294920 | tf_op jit(solution)/shard_map/ppermute | solution.py:338
  28.3 0.1 collective-permute-start.10
  28.4 0.7 collective-permute-start.9
  29.1 2.8 %collective-permute-done.5 = bf16[3,32,512]{2,1,0:T(8,128)(2,1)S(1)} collective-permute-done((bf16[3,32,512]{2,1,0:T(8,128)(2,1)S(1)}, bf16[3,32,512]{2,1,0:T(8,128)(2,1)S(1)}, u32[]{:S(2)}, u32[]{:S(2)}) %collective-permute-start.5) | collective-permute-done | bytes 98336 | tf_op jit(solution)/shard_map/ppermute | solution.py:338
  32.0 3.0 %collective-permute-start.6 = (bf16[1,3,32,512]{3,2,1,0:T(8,128)(2,1)S(1)}, bf16[1,3,32,512]{3,2,1,0:T(8,128)(2,1)S(1)}, u32[]{:S(2)}, u32[]{:S(2)}) collective-permute-start(bf16[1,3,32,512]{3,2,1,0:T(8,128)(2,1)S(1)} %fusion.field), channel_id=1, source_target_pairs={{0,8},{2,10},{4,12},{6,14},{8,0},{10,2},{12,4},{14,6},{1,9},{3,11}... | collective-permute-start | bytes 294920 | tf_op jit(solution)/shard_map/ppermute | solution.py:338
  35.0 8.6 %collective-permute-done.6.came = bf16[1,3,32,512]{3,2,1,0:T(8,128)(2,1)S(1)} collective-permute-done((bf16[1,3,32,512]{3,2,1,0:T(8,128)(2,1)S(1)}, bf16[1,3,32,512]{3,2,1,0:T(8,128)(2,1)S(1)}, u32[]{:S(2)}, u32[]{:S(2)}) %collective-permute-start.6) | collective-permute-done | bytes 98336 | tf_op jit(solution)/shard_map/ppermute | solution.py:338
  43.7 0.7 copy-done.1
  44.3 2.0 %collective-permute-start.21 = (bf16[2,2,128,256]{3,2,1,0:T(8,128)(2,1)S(1)}, bf16[2,2,128,256]{3,2,1,0:T(8,128)(2,1)S(1)}, u32[]{:S(2)}, u32[]{:S(2)}) collective-permute-start(bf16[2,2,128,256]{3,2,1,0:T(8,128)(2,1)S(1)} %get-tuple-element.71), channel_id=1, source_target_pairs={{0,4},{2,6},{4,0},{6,2},{8,12},{10,14},{12,8},{14,10},{1,5},{3,7},... | collective-permute-start | bytes 786440 | tf_op jit(solution)/shard_map/ppermute | solution.py:338
  46.4 1.9 %collective-permute-start.11 = (bf16[2,3,32,256]{3,2,1,0:T(8,128)(2,1)S(1)}, bf16[2,3,32,256]{3,2,1,0:T(8,128)(2,1)S(1)}, u32[]{:S(2)}, u32[]{:S(2)}) collective-permute-start(bf16[2,3,32,256]{3,2,1,0:T(8,128)(2,1)S(1)} %get-tuple-element.62.own_b), channel_id=1, source_target_pairs={{0,2},{2,0},{4,6},{6,4},{8,10},{10,8},{12,14},{14,12},{1,3},{3,1},... | collective-permute-start | bytes 294920 | tf_op jit(solution)/shard_map/ppermute | solution.py:338
  48.2 2.5 %collective-permute-done.8.came_a = bf16[2,3,32,256]{3,2,1,0:T(8,128)(2,1)S(1)} collective-permute-done((bf16[2,3,32,256]{3,2,1,0:T(8,128)(2,1)S(1)}, bf16[2,3,32,256]{3,2,1,0:T(8,128)(2,1)S(1)}, u32[]{:S(2)}, u32[]{:S(2)}) %collective-permute-start.8) | collective-permute-done | bytes 98336 | tf_op jit(solution)/shard_map/ppermute | solution.py:338
  50.8 0.2 collective-permute-start.14
  51.0 0.8 collective-permute-done.11.came_b
  51.8 0.8 gather.4
  52.6 0.7 copy-done.3
  53.3 2.1 %collective-permute-start.12 = (bf16[4,3,32,256]{3,2,1,0:T(8,128)(2,1)}, bf16[4,3,32,256]{3,2,1,0:T(8,128)(2,1)}, u32[]{:S(2)}, u32[]{:S(2)}) collective-permute-start(bf16[4,3,32,256]{3,2,1,0:T(8,128)(2,1)} %get-tuple-element.66), channel_id=1, source_target_pairs={{0,2},{2,0},{4,6},{6,4},{8,10},{10,8},{12,14},{14,12},{1,3},{3,1},... | collective-permute-start | bytes 589832 | tf_op jit(solution)/shard_map/ppermute | solution.py:338
  55.4 1.1 %collective-permute-start.15 = (bf16[4,3,32,256]{3,2,1,0:T(8,128)(2,1)}, bf16[4,3,32,256]{3,2,1,0:T(8,128)(2,1)}, u32[]{:S(2)}, u32[]{:S(2)}) collective-permute-start(bf16[4,3,32,256]{3,2,1,0:T(8,128)(2,1)} %get-tuple-element.69), channel_id=1, source_target_pairs={{0,4},{2,6},{4,0},{6,2},{8,12},{10,14},{12,8},{14,10},{1,5},{3,7},... | collective-permute-start | bytes 589832 | tf_op jit(solution)/shard_map/ppermute | solution.py:338
  56.5 1.5 %collective-permute-done.21.refs_1_ = bf16[2,2,128,256]{3,2,1,0:T(8,128)(2,1)S(1)} collective-permute-done((bf16[2,2,128,256]{3,2,1,0:T(8,128)(2,1)S(1)}, bf16[2,2,128,256]{3,2,1,0:T(8,128)(2,1)S(1)}, u32[]{:S(2)}, u32[]{:S(2)}) %collective-permute-start.21) | collective-permute-done | bytes 262176 | tf_op jit(solution)/shard_map/ppermute | solution.py:338
  58.0 0.5 collective-permute-start.23
  58.6 3.2 %collective-permute-done.19.refs_2_ = bf16[2,2,128,256]{3,2,1,0:T(8,128)(2,1)S(1)} collective-permute-done((bf16[2,2,128,256]{3,2,1,0:T(8,128)(2,1)S(1)}, bf16[2,2,128,256]{3,2,1,0:T(8,128)(2,1)S(1)}, u32[]{:S(2)}, u32[]{:S(2)}) %collective-permute-start.19) | collective-permute-done | bytes 262176 | tf_op jit(solution)/shard_map/ppermute | solution.py:338
  61.8 0.5 collective-permute-start.22
  62.3 0.5 collective-permute-start.20
  62.8 1.5 %collective-permute-start.25 = (bf16[2,2,128,256]{3,2,1,0:T(8,128)(2,1)S(1)}, bf16[2,2,128,256]{3,2,1,0:T(8,128)(2,1)S(1)}, u32[]{:S(2)}, u32[]{:S(2)}) collective-permute-start(bf16[2,2,128,256]{3,2,1,0:T(8,128)(2,1)S(1)} %collective-permute-done.19.refs_2_), channel_id=1, source_target_pairs={{0,2},{2,0},{4,6},{6,4},{8,10},{10,8},{12,14},{14,12},{1,3},{3,1},... | collective-permute-start | bytes 786440 | tf_op jit(solution)/shard_map/ppermute | solution.py:338
  64.3 1.0 %gather.5.refs_2_ = bf16[2,4,3,32,256]{4,3,2,1,0:T(8,128)(2,1)S(1)} custom-call(bf16[4,3,32,256]{3,2,1,0:T(8,128)(2,1)} %collective-permute-done.12.came_a, bf16[4,3,32,256]{3,2,1,0:T(8,128)(2,1)} %collective-permute-done.15.came_b), custom_call_target="tpu_custom_call" | custom-call | bytes 786432 | tf_op jit(solution)/shard_map/gather/pallas_call | solution.py:185
  65.5 2.1 %collective-permute-done.23.refs_5_ = bf16[2,2,128,256]{3,2,1,0:T(8,128)(2,1)S(1)} collective-permute-done((bf16[2,2,128,256]{3,2,1,0:T(8,128)(2,1)S(1)}, bf16[2,2,128,256]{3,2,1,0:T(8,128)(2,1)S(1)}, u32[]{:S(2)}, u32[]{:S(2)}) %collective-permute-start.23) | collective-permute-done | bytes 262176 | tf_op jit(solution)/shard_map/ppermute | solution.py:338
  67.6 3.2 %collective-permute-done.22.refs_2_ = bf16[2,2,128,256]{3,2,1,0:T(8,128)(2,1)S(1)} collective-permute-done((bf16[2,2,128,256]{3,2,1,0:T(8,128)(2,1)}, bf16[2,2,128,256]{3,2,1,0:T(8,128)(2,1)S(1)}, u32[]{:S(2)}, u32[]{:S(2)}) %collective-permute-start.22) | collective-permute-done | bytes 262176 | tf_op jit(solution)/shard_map/ppermute | solution.py:338
  70.9 1.4 %collective-permute-start.24 = (bf16[2,2,128,256]{3,2,1,0:T(8,128)(2,1)S(1)}, bf16[2,2,128,256]{3,2,1,0:T(8,128)(2,1)S(1)}, u32[]{:S(2)}, u32[]{:S(2)}) collective-permute-start(bf16[2,2,128,256]{3,2,1,0:T(8,128)(2,1)S(1)} %collective-permute-done.22.refs_2_), channel_id=1, source_target_pairs={{0,2},{2,0},{4,6},{6,4},{8,10},{10,8},{12,14},{14,12},{1,3},{3,1},... | collective-permute-start | bytes 786440 | tf_op jit(solution)/shard_map/ppermute | solution.py:338
  72.3 0.1 collective-permute-done.17.refs_4_
  72.5 0.9 %copy-done.2 = bf16[2,2,3,32,256]{4,3,2,1,0:T(8,128)(2,1)S(1)} copy-done((bf16[2,2,3,32,256]{4,3,2,1,0:T(8,128)(2,1)S(1)}, bf16[2,2,3,32,256]{4,3,2,1,0:T(8,128)(2,1)}, u32[]{:S(2)}) %copy-start.2) | copy-done | bytes 196632
  73.4 0.9 %copy-done.4 = bf16[2,2,3,32,256]{4,3,2,1,0:T(8,128)(2,1)S(1)} copy-done((bf16[2,2,3,32,256]{4,3,2,1,0:T(8,128)(2,1)S(1)}, bf16[2,2,3,32,256]{4,3,2,1,0:T(8,128)(2,1)}, u32[]{:S(2)}) %copy-start.4) | copy-done | bytes 196632
  74.3 1.1 %prepare.1 = (bf16[2,768,512]{2,1,0:T(8,128)(2,1)S(1)}, bf16[2,3,512,256]{3,2,1,0:T(8,128)(2,1)S(1)}) custom-call(s32[16]{0:T(128)S(1)} %stack.31.place, bf16[2,2,3,32,256]{4,3,2,1,0:T(8,128)(2,1)S(1)} %copy-done.2, bf16[2,2,3,32,256]{4,3,2,1,0:T(8,128)(2,1)S(1)} %copy-done.4, bf16[2,4,3,32,256]{4,3,2,1,0:T(8,128)(2,1)S(1)} %gather.5.refs_2_, ...), custom_call_target="tpu_custom_call" | custom-call | bytes 3145728 | tf_op jit(solution)/shard_map/prepare/pallas_call | solution.py:230
  75.4 6.0 %dress.2.refs_8_ = bf16[4,3,2,128,1024]{4,3,2,1,0:T(8,128)(2,1)} custom-call(s32[16]{0:T(128)S(1)} %stack.31.place, s32[2]{0:T(128)S(1)} %get-tuple-element.88.other_src, s32[2]{0:T(128)S(1)} %get-tuple-element.87.other_snk, bf16[2,768,512]{2,1,0:T(8,128)(2,1)S(1)} %get-tuple-element.73.left, bf16[2,3,512,256]{3,2,1,0:T(8,128)(2,1)S(1)} %get-tuple-element.74.sink, ...), custom_call_target="tpu_custom_call" | custom-call | flops 3221225472 | bytes 2097152 | tf_op jit(solution)/shard_map/dress/pallas_call | solution.py:307
  81.4 6.0 %dress.3 = bf16[4,3,2,128,1024]{4,3,2,1,0:T(8,128)(2,1)} custom-call(s32[16]{0:T(128)S(1)} %stack.31.place, s32[2]{0:T(128)S(1)} %get-tuple-element.90.other_src, s32[2]{0:T(128)S(1)} %get-tuple-element.89.other_snk, bf16[2,768,512]{2,1,0:T(8,128)(2,1)S(1)} %get-tuple-element.73.left, ...), custom_call_target="tpu_custom_call", output_to_operand_aliasing={{}: (13, {})} | custom-call | flops 3221225472 | bytes 2097152 | tf_op jit(solution)/shard_map/dress/pallas_call | solution.py:307
  (33 shorter events, 0.3 us)
Async XLA Ops:
  0.0 9.0 %copy-start = (bf16[4,2,128,1024]{3,2,1,0:T(8,128)(2,1)S(1)}, bf16[4,2,128,1024]{3,2,1,0:T(8,128)(2,1)}, u32[]{:S(2)}) copy-start(bf16[4,2,128,1024]{3,2,1,0:T(8,128)(2,1)} %panels.1) | copy-start | bytes 6291460
  1.0 1.1 %copy-start.5 = (bf16[1,2,3,192,256]{4,3,2,1,0:T(8,128)(2,1)S(1)}, bf16[1,2,3,192,256]{4,3,2,1,0:T(8,128)(2,1)}, u32[]{:S(2)}) copy-start(bf16[1,2,3,192,256]{4,3,2,1,0:T(8,128)(2,1)} %param.4) | copy-start | bytes 1769476
  4.4 8.8 %collective-permute-start = (bf16[3,128,256]{2,1,0:T(8,128)(2,1)S(1)}, bf16[3,128,256]{2,1,0:T(8,128)(2,1)S(1)}, u32[]{:S(2)}, u32[]{:S(2)}) collective-permute-start(bf16[3,128,256]{2,1,0:T(8,128)(2,1)S(1)} %get-tuple-element.48), channel_id=1, source_target_pairs={{0,2},{2,0},{4,6},{6,4},{8,10},{10,8},{12,14},{14,12},{1,3},{3,1},... | collective-permute-start | bytes 589832 | tf_op jit(solution)/shard_map/ppermute | solution.py:338
  7.4 6.4 %collective-permute-start.1 = (bf16[3,128,256]{2,1,0:T(8,128)(2,1)S(1)}, bf16[3,128,256]{2,1,0:T(8,128)(2,1)S(1)}, u32[]{:S(2)}, u32[]{:S(2)}) collective-permute-start(bf16[3,128,256]{2,1,0:T(8,128)(2,1)S(1)} %get-tuple-element.49), channel_id=1, source_target_pairs={{0,4},{2,6},{4,0},{6,2},{8,12},{10,14},{12,8},{14,10},{1,5},{3,7},... | collective-permute-start | bytes 589832 | tf_op jit(solution)/shard_map/ppermute | solution.py:338
  10.6 54.8 %copy-start.6 = (s32[4,2]{0,1:T(2,128)S(1)}, s32[4,2]{0,1:T(2,128)}, u32[]{:S(2)}) copy-start(s32[4,2]{0,1:T(2,128)} %param.6) | copy-start | bytes 100
  10.7 11.9 %collective-permute-start.3 = (bf16[2,2,128,256]{3,2,1,0:T(8,128)(2,1)S(1)}, bf16[2,2,128,256]{3,2,1,0:T(8,128)(2,1)S(1)}, u32[]{:S(2)}, u32[]{:S(2)}) collective-permute-start(bf16[2,2,128,256]{3,2,1,0:T(8,128)(2,1)S(1)} %get-tuple-element.53), channel_id=1, source_target_pairs={{0,12},{2,14},{4,8},{6,10},{8,4},{10,6},{12,0},{14,2},{1,13},{3,15... | collective-permute-start | bytes 786440 | tf_op jit(solution)/shard_map/ppermute | solution.py:338
  14.4 8.4 %collective-permute-start.2 = (bf16[3,64,256]{2,1,0:T(8,128)(2,1)S(1)}, bf16[3,64,256]{2,1,0:T(8,128)(2,1)S(1)}, u32[]{:S(2)}, u32[]{:S(2)}) collective-permute-start(bf16[3,64,256]{2,1,0:T(8,128)(2,1)S(1)} %get-tuple-element.52), channel_id=1, source_target_pairs={{0,4},{2,6},{4,0},{6,2},{8,12},{10,14},{12,8},{14,10},{1,5},{3,7},... | collective-permute-start | bytes 294920 | tf_op jit(solution)/shard_map/ppermute | solution.py:338
  16.3 6.5 %collective-permute-start.4 = (bf16[3,64,256]{2,1,0:T(8,128)(2,1)S(1)}, bf16[3,64,256]{2,1,0:T(8,128)(2,1)S(1)}, u32[]{:S(2)}, u32[]{:S(2)}) collective-permute-start(bf16[3,64,256]{2,1,0:T(8,128)(2,1)S(1)} %get-tuple-element.55), channel_id=1, source_target_pairs={{0,2},{2,0},{4,6},{6,4},{8,10},{10,8},{12,14},{14,12},{1,3},{3,1},... | collective-permute-start | bytes 294920 | tf_op jit(solution)/shard_map/ppermute | solution.py:338
  16.8 26.8 %collective-permute-start.7 = (bf16[4,2,128,256]{3,2,1,0:T(8,128)(2,1)S(1)}, bf16[4,2,128,256]{3,2,1,0:T(8,128)(2,1)S(1)}, u32[]{:S(2)}, u32[]{:S(2)}) collective-permute-start(bf16[4,2,128,256]{3,2,1,0:T(8,128)(2,1)S(1)} %get-tuple-element.58.refs_0_), channel_id=1, source_target_pairs={{0,2},{2,0},{4,6},{6,4},{8,10},{10,8},{12,14},{14,12},{1,3},{3,1},... | collective-permute-start | bytes 1572872 | tf_op jit(solution)/shard_map/ppermute | solution.py:338
  23.4 8.5 %collective-permute-start.5 = (bf16[3,32,512]{2,1,0:T(8,128)(2,1)S(1)}, bf16[3,32,512]{2,1,0:T(8,128)(2,1)S(1)}, u32[]{:S(2)}, u32[]{:S(2)}) collective-permute-start(bf16[3,32,512]{2,1,0:T(8,128)(2,1)S(1)} %get-tuple-element.57), channel_id=1, source_target_pairs={{0,8},{2,10},{4,12},{6,14},{8,0},{10,2},{12,4},{14,6},{1,9},{3,11}... | collective-permute-start | bytes 294920 | tf_op jit(solution)/shard_map/ppermute | solution.py:338
  28.3 18.0 %collective-permute-start.10 = (bf16[2,2,128,256]{3,2,1,0:T(8,128)(2,1)S(1)}, bf16[2,2,128,256]{3,2,1,0:T(8,128)(2,1)S(1)}, u32[]{:S(2)}, u32[]{:S(2)}) collective-permute-start(bf16[2,2,128,256]{3,2,1,0:T(8,128)(2,1)S(1)} %get-tuple-element.63), channel_id=1, source_target_pairs={{0,4},{2,6},{4,0},{6,2},{8,12},{10,14},{12,8},{14,10},{1,5},{3,7},... | collective-permute-start | bytes 786440 | tf_op jit(solution)/shard_map/ppermute | solution.py:338
  28.4 17.9 %collective-permute-start.9 = (bf16[2,2,128,256]{3,2,1,0:T(8,128)(2,1)S(1)}, bf16[2,2,128,256]{3,2,1,0:T(8,128)(2,1)S(1)}, u32[]{:S(2)}, u32[]{:S(2)}) collective-permute-start(bf16[2,2,128,256]{3,2,1,0:T(8,128)(2,1)S(1)} %collective-permute-done.3.refs_3_), channel_id=1, source_target_pairs={{0,2},{2,0},{4,6},{6,4},{8,10},{10,8},{12,14},{14,12},{1,3},{3,1},... | collective-permute-start | bytes 786440 | tf_op jit(solution)/shard_map/ppermute | solution.py:338
  32.0 11.6 %collective-permute-start.6 = (bf16[1,3,32,512]{3,2,1,0:T(8,128)(2,1)S(1)}, bf16[1,3,32,512]{3,2,1,0:T(8,128)(2,1)S(1)}, u32[]{:S(2)}, u32[]{:S(2)}) collective-permute-start(bf16[1,3,32,512]{3,2,1,0:T(8,128)(2,1)S(1)} %fusion.field), channel_id=1, source_target_pairs={{0,8},{2,10},{4,12},{6,14},{8,0},{10,2},{12,4},{14,6},{1,9},{3,11}... | collective-permute-start | bytes 294920 | tf_op jit(solution)/shard_map/ppermute | solution.py:338
  35.0 20.4 %collective-permute-start.13 = (bf16[2,2,128,256]{3,2,1,0:T(8,128)(2,1)S(1)}, bf16[2,2,128,256]{3,2,1,0:T(8,128)(2,1)S(1)}, u32[]{:S(2)}, u32[]{:S(2)}) collective-permute-start(bf16[2,2,128,256]{3,2,1,0:T(8,128)(2,1)S(1)} %get-tuple-element.67), channel_id=1, source_target_pairs={{0,12},{2,14},{4,8},{6,10},{8,4},{10,6},{12,0},{14,2},{1,13},{3,15... | collective-permute-start | bytes 786440 | tf_op jit(solution)/shard_map/ppermute | solution.py:338
  43.6 0.7 copy-start.1
  44.3 6.5 %collective-permute-start.8 = (bf16[2,3,32,256]{3,2,1,0:T(8,128)(2,1)S(1)}, bf16[2,3,32,256]{3,2,1,0:T(8,128)(2,1)S(1)}, u32[]{:S(2)}, u32[]{:S(2)}) collective-permute-start(bf16[2,3,32,256]{3,2,1,0:T(8,128)(2,1)S(1)} %get-tuple-element.61.own_a), channel_id=1, source_target_pairs={{0,4},{2,6},{4,0},{6,2},{8,12},{10,14},{12,8},{14,10},{1,5},{3,7},... | collective-permute-start | bytes 294920 | tf_op jit(solution)/shard_map/ppermute | solution.py:338
  44.3 13.7 %collective-permute-start.21 = (bf16[2,2,128,256]{3,2,1,0:T(8,128)(2,1)S(1)}, bf16[2,2,128,256]{3,2,1,0:T(8,128)(2,1)S(1)}, u32[]{:S(2)}, u32[]{:S(2)}) collective-permute-start(bf16[2,2,128,256]{3,2,1,0:T(8,128)(2,1)S(1)} %get-tuple-element.71), channel_id=1, source_target_pairs={{0,4},{2,6},{4,0},{6,2},{8,12},{10,14},{12,8},{14,10},{1,5},{3,7},... | collective-permute-start | bytes 786440 | tf_op jit(solution)/shard_map/ppermute | solution.py:338
  46.3 15.4 %collective-permute-start.19 = (bf16[2,2,128,256]{3,2,1,0:T(8,128)(2,1)S(1)}, bf16[2,2,128,256]{3,2,1,0:T(8,128)(2,1)S(1)}, u32[]{:S(2)}, u32[]{:S(2)}) collective-permute-start(bf16[2,2,128,256]{3,2,1,0:T(8,128)(2,1)S(1)} %get-tuple-element.70), channel_id=1, source_target_pairs={{0,8},{2,10},{4,12},{6,14},{8,0},{10,2},{12,4},{14,6},{1,9},{3,11}... | collective-permute-start | bytes 786440 | tf_op jit(solution)/shard_map/ppermute | solution.py:338
  46.4 5.5 %collective-permute-start.11 = (bf16[2,3,32,256]{3,2,1,0:T(8,128)(2,1)S(1)}, bf16[2,3,32,256]{3,2,1,0:T(8,128)(2,1)S(1)}, u32[]{:S(2)}, u32[]{:S(2)}) collective-permute-start(bf16[2,3,32,256]{3,2,1,0:T(8,128)(2,1)S(1)} %get-tuple-element.62.own_b), channel_id=1, source_target_pairs={{0,2},{2,0},{4,6},{6,4},{8,10},{10,8},{12,14},{14,12},{1,3},{3,1},... | collective-permute-start | bytes 294920 | tf_op jit(solution)/shard_map/ppermute | solution.py:338
  50.8 11.5 %collective-permute-start.14 = (bf16[2,2,128,256]{3,2,1,0:T(8,128)(2,1)S(1)}, bf16[2,2,128,256]{3,2,1,0:T(8,128)(2,1)S(1)}, u32[]{:S(2)}, u32[]{:S(2)}) collective-permute-start(bf16[2,2,128,256]{3,2,1,0:T(8,128)(2,1)S(1)} %collective-permute-done.10.refs_1_), channel_id=1, source_target_pairs={{0,2},{2,0},{4,6},{6,4},{8,10},{10,8},{12,14},{14,12},{1,3},{3,1},... | collective-permute-start | bytes 786440 | tf_op jit(solution)/shard_map/ppermute | solution.py:338
  52.6 0.7 copy-start.3
  53.3 9.6 %collective-permute-start.12 = (bf16[4,3,32,256]{3,2,1,0:T(8,128)(2,1)}, bf16[4,3,32,256]{3,2,1,0:T(8,128)(2,1)}, u32[]{:S(2)}, u32[]{:S(2)}) collective-permute-start(bf16[4,3,32,256]{3,2,1,0:T(8,128)(2,1)} %get-tuple-element.66), channel_id=1, source_target_pairs={{0,2},{2,0},{4,6},{6,4},{8,10},{10,8},{12,14},{14,12},{1,3},{3,1},... | collective-permute-start | bytes 589832 | tf_op jit(solution)/shard_map/ppermute | solution.py:338
  55.4 8.9 %collective-permute-start.15 = (bf16[4,3,32,256]{3,2,1,0:T(8,128)(2,1)}, bf16[4,3,32,256]{3,2,1,0:T(8,128)(2,1)}, u32[]{:S(2)}, u32[]{:S(2)}) collective-permute-start(bf16[4,3,32,256]{3,2,1,0:T(8,128)(2,1)} %get-tuple-element.69), channel_id=1, source_target_pairs={{0,4},{2,6},{4,0},{6,2},{8,12},{10,14},{12,8},{14,10},{1,5},{3,7},... | collective-permute-start | bytes 589832 | tf_op jit(solution)/shard_map/ppermute | solution.py:338
  58.0 9.5 %collective-permute-start.23 = (bf16[2,2,128,256]{3,2,1,0:T(8,128)(2,1)S(1)}, bf16[2,2,128,256]{3,2,1,0:T(8,128)(2,1)S(1)}, u32[]{:S(2)}, u32[]{:S(2)}) collective-permute-start(bf16[2,2,128,256]{3,2,1,0:T(8,128)(2,1)S(1)} %collective-permute-done.21.refs_1_), channel_id=1, source_target_pairs={{0,2},{2,0},{4,6},{6,4},{8,10},{10,8},{12,14},{14,12},{1,3},{3,1},... | collective-permute-start | bytes 786440 | tf_op jit(solution)/shard_map/ppermute | solution.py:338
  61.8 9.0 %collective-permute-start.22 = (bf16[2,2,128,256]{3,2,1,0:T(8,128)(2,1)}, bf16[2,2,128,256]{3,2,1,0:T(8,128)(2,1)S(1)}, u32[]{:S(2)}, u32[]{:S(2)}) collective-permute-start(bf16[2,2,128,256]{3,2,1,0:T(8,128)(2,1)} %get-tuple-element.77), channel_id=1, source_target_pairs={{0,8},{2,10},{4,12},{6,14},{8,0},{10,2},{12,4},{14,6},{1,9},{3,11}... | collective-permute-start | bytes 786440 | tf_op jit(solution)/shard_map/ppermute | solution.py:338
  62.3 8.6 %collective-permute-start.20 = (bf16[2,2,128,256]{3,2,1,0:T(8,128)(2,1)S(1)}, bf16[2,2,128,256]{3,2,1,0:T(8,128)(2,1)S(1)}, u32[]{:S(2)}, u32[]{:S(2)}) collective-permute-start(bf16[2,2,128,256]{3,2,1,0:T(8,128)(2,1)S(1)} %collective-permute-done.13.refs_3_), channel_id=1, source_target_pairs={{0,2},{2,0},{4,6},{6,4},{8,10},{10,8},{12,14},{14,12},{1,3},{3,1},... | collective-permute-start | bytes 786440 | tf_op jit(solution)/shard_map/ppermute | solution.py:338
  62.8 12.6 %collective-permute-start.25 = (bf16[2,2,128,256]{3,2,1,0:T(8,128)(2,1)S(1)}, bf16[2,2,128,256]{3,2,1,0:T(8,128)(2,1)S(1)}, u32[]{:S(2)}, u32[]{:S(2)}) collective-permute-start(bf16[2,2,128,256]{3,2,1,0:T(8,128)(2,1)S(1)} %collective-permute-done.19.refs_2_), channel_id=1, source_target_pairs={{0,2},{2,0},{4,6},{6,4},{8,10},{10,8},{12,14},{14,12},{1,3},{3,1},... | collective-permute-start | bytes 786440 | tf_op jit(solution)/shard_map/ppermute | solution.py:338
  65.4 6.9 %collective-permute-start.18 = (bf16[2,4,3,32,256]{4,3,2,1,0:T(8,128)(2,1)S(1)}, bf16[2,4,3,32,256]{4,3,2,1,0:T(8,128)(2,1)S(1)}, u32[]{:S(2)}, u32[]{:S(2)}) collective-permute-start(bf16[2,4,3,32,256]{4,3,2,1,0:T(8,128)(2,1)S(1)} %gather.5.refs_2_), channel_id=1, source_target_pairs={{0,1},{1,0},{2,3},{3,2},{4,5},{5,4},{6,7},{7,6},{8,9},{9,8},{10,11... | collective-permute-start | bytes 1179656 | tf_op jit(solution)/shard_map/ppermute | solution.py:338
  67.6 4.8 %collective-permute-start.16 = (bf16[2,2,3,32,256]{4,3,2,1,0:T(8,128)(2,1)}, bf16[2,2,3,32,256]{4,3,2,1,0:T(8,128)(2,1)S(1)}, u32[]{:S(2)}, u32[]{:S(2)}) collective-permute-start(bf16[2,2,3,32,256]{4,3,2,1,0:T(8,128)(2,1)} %copy-done.1), channel_id=1, source_target_pairs={{0,1},{1,0},{2,3},{3,2},{4,5},{5,4},{6,7},{7,6},{8,9},{9,8},{10,11... | collective-permute-start | bytes 589832 | tf_op jit(solution)/shard_map/ppermute | solution.py:338
  70.8 1.7 %collective-permute-start.17 = (bf16[2,2,3,32,256]{4,3,2,1,0:T(8,128)(2,1)}, bf16[2,2,3,32,256]{4,3,2,1,0:T(8,128)(2,1)S(1)}, u32[]{:S(2)}, u32[]{:S(2)}) collective-permute-start(bf16[2,2,3,32,256]{4,3,2,1,0:T(8,128)(2,1)} %copy-done.3), channel_id=1, source_target_pairs={{0,1},{1,0},{2,3},{3,2},{4,5},{5,4},{6,7},{7,6},{8,9},{9,8},{10,11... | collective-permute-start | bytes 589832 | tf_op jit(solution)/shard_map/ppermute | solution.py:338
  70.9 10.5 %collective-permute-start.24 = (bf16[2,2,128,256]{3,2,1,0:T(8,128)(2,1)S(1)}, bf16[2,2,128,256]{3,2,1,0:T(8,128)(2,1)S(1)}, u32[]{:S(2)}, u32[]{:S(2)}) collective-permute-start(bf16[2,2,128,256]{3,2,1,0:T(8,128)(2,1)S(1)} %collective-permute-done.22.refs_2_), channel_id=1, source_target_pairs={{0,2},{2,0},{4,6},{6,4},{8,10},{10,8},{12,14},{14,12},{1,3},{3,1},... | collective-permute-start | bytes 786440 | tf_op jit(solution)/shard_map/ppermute | solution.py:338
  72.5 0.9 %copy-start.2 = (bf16[2,2,3,32,256]{4,3,2,1,0:T(8,128)(2,1)S(1)}, bf16[2,2,3,32,256]{4,3,2,1,0:T(8,128)(2,1)}, u32[]{:S(2)}) copy-start(bf16[2,2,3,32,256]{4,3,2,1,0:T(8,128)(2,1)} %copy-done.1) | copy-start | bytes 589828
  73.4 0.9 %copy-start.4 = (bf16[2,2,3,32,256]{4,3,2,1,0:T(8,128)(2,1)S(1)}, bf16[2,2,3,32,256]{4,3,2,1,0:T(8,128)(2,1)}, u32[]{:S(2)}) copy-start(bf16[2,2,3,32,256]{4,3,2,1,0:T(8,128)(2,1)} %copy-done.3) | copy-start | bytes 589828

commit v5 on v4

--- a/solution.py
+++ b/solution.py
@@ -241,24 +241,19 @@
     )(place, *own, *oth)
 
 
-def dress_kernel(dists, chained, first_pair, place, other_src, other_snk, left, sink, *refs):
-    count = len(dists)
+def dress_kernel(count, chained, place, other_src, other_snk, left, sink, *refs):
     mine, near = refs[:count], refs[count : 2 * count]
-    out, panel, done, sems = refs[2 * count + chained :]
+    out, panel = refs[2 * count + chained :]
     moms, width, vectors = sink.shape[1:]
     columns = out.shape[3]
-    pair, last = pl.program_id(0), pl.num_programs(0) - 1
+    pair = pl.program_id(0)
     x, z = place[X], place[Z]
     src, snk = other_src[pair], other_snk[pair]
     block = mine[0].shape[2]
-
-    def store(k, of_pair):
-        lanes = pl.ds(pl.multiple_of((z ^ dists[k]) * vectors, vectors), vectors)
-        return pltpu.make_async_copy(done.at[k], out.at[of_pair + first_pair, :, :, :, lanes], sems.at[k])
-
     for k in range(count):
-        at_mine = pl.ds(pl.multiple_of(k * vectors + x * block, block), block)
-        at_near = pl.ds(pl.multiple_of(k * vectors + (1 - x) * block, block), block)
+        base = (z ^ k) * vectors
+        at_mine = pl.ds(pl.multiple_of(base + x * block, block), block)
+        at_near = pl.ds(pl.multiple_of(base + (1 - x) * block, block), block)
         for part in range(2):
             lanes = slice(part * vectors, (part + 1) * vectors)
             panel[at_mine, lanes] = mine[k][0, part]
@@ -266,31 +261,19 @@
 
     contract = (((1,), (1,)), ((), ()))
     right = lax.dot_general(left[src], panel[...], contract, preferred_element_type=F32).astype(BF16)
-
-    @pl.when(pair > 0)
-    def _():
-        for k in range(count):
-            store(k, pair - 1).wait()
-
     for m in range(moms):
         part = right[2 * m * columns : 2 * (m + 1) * columns]
         rows = jnp.concatenate([part[:, k * vectors : (k + 1) * vectors] for k in range(count)], 0)
         both = lax.dot_general(rows, sink[snk, m], contract, preferred_element_type=F32)
         for k in range(count):
+            at = slice(k * vectors, (k + 1) * vectors)
             re = both[2 * k * columns : (2 * k + 1) * columns]
             im = both[(2 * k + 1) * columns : (2 * k + 2) * columns]
-            done[k, m, 0] = (re[:, :vectors] - im[:, vectors:]).astype(BF16)
-            done[k, m, 1] = (re[:, vectors:] + im[:, :vectors]).astype(BF16)
-    for k in range(count):
-        store(k, pair).start()
-
-    @pl.when(pair == last)
-    def _():
-        for k in range(count):
-            store(k, pair).wait()
-
-
-def dress(out, out_shape, first_pair, pairs, dists, mine, near, left, sink, place, other_src, other_snk):
+            out[0, m, 0, :, at] = (re[:, :vectors] - im[:, vectors:]).astype(BF16)
+            out[0, m, 1, :, at] = (re[:, vectors:] + im[:, :vectors]).astype(BF16)
+
+
+def dress(out, out_shape, first_pair, pairs, mine, near, left, sink, place, other_src, other_snk):
     _, _, block, vectors = mine[0][0].shape
     count = len(mine)
     moms = sink.shape[1]
@@ -305,18 +288,16 @@
     in_specs = [whole, whole] + chunks + [pl.BlockSpec(memory_space=pl.ANY)] * chained
     macs = pairs * count * 2 * (2 * moms * columns) * (2 * vectors) * vectors
     return pl.pallas_call(
-        functools.partial(dress_kernel, dists, chained, first_pair),
+        functools.partial(dress_kernel, count, chained),
         out_shape=out_shape,
         grid_spec=pltpu.PrefetchScalarGridSpec(
             num_scalar_prefetch=3,
             grid=(pairs,),
             in_specs=in_specs,
-            out_specs=pl.BlockSpec(memory_space=pl.ANY),
-            scratch_shapes=[
-                pltpu.VMEM((count * 2 * block, 2 * vectors), BF16),
-                pltpu.VMEM((count, moms, 2, columns, vectors), BF16),
-                pltpu.SemaphoreType.DMA((count,)),
-            ],
+            out_specs=pl.BlockSpec(
+                (1, moms, 2, columns, count * vectors), lambda p, *_: (p + first_pair, 0, 0, 0, 0)
+            ),
+            scratch_shapes=[pltpu.VMEM((count * 2 * block, 2 * vectors), BF16)],
         ),
         input_output_aliases={3 + len(operands) - 1: 0} if chained else {},
         compiler_params=params(1),
@@ -326,12 +307,18 @@
 
 
 CHUNKS = (1, 2, 2, 2)
-HOOKS = [[], [('z', 3, 0)], [], [('x', 0, 0)], [('x', 3, 0), ('z', 1, 0)], [('z', 3, 1), ('x', 1, 0)], [('z', 2, 0), ('x', 3, 1), ('z', 1, 1)]]
-LOCK = (False, False)
-CALLS = ((0, 2, (0, 1, 2, 3)), (2, 2, (0, 1, 2, 3)))
-GATES = {}
-AFTER = {('x', 2, 1): [('x', 1, 1)]}
-FROM = {('z', 2, 1): 4}
+HOOKS = [
+    [],
+    [("z", 3, 0)],
+    [],
+    [("x", 0, 0), ("z", 1, 0)],
+    [("x", 3, 0)],
+    [("z", 3, 1), ("x", 1, 0)],
+    [("z", 2, 0), ("x", 3, 1), ("z", 1, 1)],
+]
+CALLS = ((0, 2), (2, 2))
+AFTER = {("x", 2, 1): [("x", 1, 1)]}
+FROM = {("z", 2, 1): 4}
 
 
 def exchange(value, axis, mask, among=lambda i: True):
@@ -402,21 +389,12 @@
         own.append(both)
         oth.append(exchange(both, "tm", 1))
 
-    def after_share(value, count):
-        if len(oth) >= count:
-            value, oth[count - 1] = lax.optimization_barrier((value, oth[count - 1]))
-        return value
-
     *parts, both = gather(halve_kernel, field, came)
     share(both)
     came = step((parts[0], low_z), (parts[1], along_x))
-    if LOCK[0]:
-        came[0] = after_share(came[0], 1)
     *parts, both = gather(pair_kernel, *parts, *came)
     share(both)
     came = step((parts[0], along_x), (parts[1], low_z))
-    if LOCK[1]:
-        came[0] = after_share(came[0], 2)
     share(*gather(both_kernel, *came))
     oth[2] = meet(oth[2], HOOKS[6])
 
@@ -432,14 +410,12 @@
 
     left, sink = prepare(own, oth, columns, place)
     out = None
-    for call, (first, pairs, dists) in enumerate(CALLS):
-        for _, d, c in GATES.get(call, ()):
-            value, out = lax.optimization_barrier((fetch(("z", d, c)), out))
-            raw["z", d, c] = held["z", d, c] = value
+    dists = range(spins)
+    for first, pairs in CALLS:
         mine = [part("z", d, first) for d in dists]
         near = [part("x", d, first) for d in dists]
         out = dress(
-            out, out_shape, first, pairs, dists, mine, near, left, sink, place, other_src, other_snk
+            out, out_shape, first, pairs, mine, near, left, sink, place, other_src, other_snk
         )
     return out
 

time: 87.6 us -> 86.7 us (0.990)
  Pallas kernels: 20.1 us -> 19.2 us
  transfers between devices with their start and end apart: 26 -> 26, of which waited for: 12 -> 13; matrix products, arithmetic and copies ran while one was open for 0% -> 0% of each run, Pallas kernels for 13% -> 13%
where the time goes in v5:
time: 86.7 us; the launch traced here: 86.5 us
  starting transfers between devices  31.8 us (37%)
  waiting for transfers between devices  30 us (35%)
  Pallas kernels  19.2 us (22%)
  local copies, waits for them, and re-layouts  5.35 us (6%)
    ppermute x26, starting transfers between devices, exchange(): lax.ppermute(value, axis, [(i, i ^ mask) for i in range(lax.axis_size(axi...  31.8 us
    ppermute x26, waiting for transfers between devices, exchange(): lax.ppermute(value, axis, [(i, i ^ mask) for i in range(lax.axis_size(axi...  30 us
    pallas_call x2, Pallas kernels, dress(): pl.pallas_call(functools.partial(dress_kernel, count, chained), out_shape...  11.1 us
    unnamed x14, local copies, waits for them, and re-layouts  4.28 us
    pallas_call x1, Pallas kernels, gram_halves(): pl.pallas_call(functools.partial(gram_kernel, factor), out_shape=[jax.Sha...  2.34 us
    pallas_call x3, Pallas kernels, gather(): pl.pallas_call(kernel, out_shape=[jax.ShapeDtypeStruct(shape, BF16) for s...  1.86 us
  transfers between devices with their start and end apart: 26, of which 13 were waited for; matrix products, arithmetic and copies ran while one was open for 0% of the time, Pallas kernels for 13%

profile of v5, /device:TPU:0, one launch (start us, length us, event | category | flops | bytes accessed | tf_op | source)
XLA Modules:
  0.0 86.5 jit_solution(62193992575053094)
XLA Ops:
  0.0 0.9 %reshape.7 = s32[9]{0:T(128)S(1)} reshape(s32[3,3]{1,0:T(4,128)} %param.5) | data formatting | bytes 72 | tf_op jit(solution)/shard_map/reshape | solution.py:339
  1.0 1.1 %copy-done.5 = bf16[1,2,3,192,256]{4,3,2,1,0:T(8,128)(2,1)S(1)} copy-done((bf16[1,2,3,192,256]{4,3,2,1,0:T(8,128)(2,1)S(1)}, bf16[1,2,3,192,256]{4,3,2,1,0:T(8,128)(2,1)}, u32[]{:S(2)}) %copy-start.5) | copy-done | bytes 589848
  2.1 2.3 %gram.1 = (bf16[3,128,256]{2,1,0:T(8,128)(2,1)S(1)}, bf16[3,128,256]{2,1,0:T(8,128)(2,1)S(1)}, f32[3,128,256]{2,1,0:T(8,128)S(1)}, f32[3,128,256]{2,1,0:T(8,128)S(1)}) custom-call(s32[16]{0:T(128)S(1)} %stack.31.place, bf16[2,3,192,256]{3,2,1,0:T(8,128)(2,1)S(1)} %bitcast.18), custom_call_target="tpu_custom_call" | custom-call | flops 905969664 | bytes 3145728 | tf_op jit(solution)/shard_map/gram/pallas_call | solution.py:70
  4.4 3.0 %collective-permute-start = (bf16[3,128,256]{2,1,0:T(8,128)(2,1)S(1)}, bf16[3,128,256]{2,1,0:T(8,128)(2,1)S(1)}, u32[]{:S(2)}, u32[]{:S(2)}) collective-permute-start(bf16[3,128,256]{2,1,0:T(8,128)(2,1)S(1)} %get-tuple-element.48), channel_id=1, source_target_pairs={{0,2},{2,0},{4,6},{6,4},{8,10},{10,8},{12,14},{14,12},{1,3},{3,1},... | collective-permute-start | bytes 589832 | tf_op jit(solution)/shard_map/ppermute | solution.py:325
  7.4 1.6 %collective-permute-start.1 = (bf16[3,128,256]{2,1,0:T(8,128)(2,1)S(1)}, bf16[3,128,256]{2,1,0:T(8,128)(2,1)S(1)}, u32[]{:S(2)}, u32[]{:S(2)}) collective-permute-start(bf16[3,128,256]{2,1,0:T(8,128)(2,1)S(1)} %get-tuple-element.49), channel_id=1, source_target_pairs={{0,4},{2,6},{4,0},{6,2},{8,12},{10,14},{12,8},{14,10},{1,5},{3,7},... | collective-permute-start | bytes 589832 | tf_op jit(solution)/shard_map/ppermute | solution.py:325
  9.0 1.6 %cut.1 = (bf16[4,2,128,256]{3,2,1,0:T(8,128)(2,1)S(1)}, bf16[2,2,128,256]{3,2,1,0:T(8,128)(2,1)S(1)}, bf16[2,2,128,256]{3,2,1,0:T(8,128)(2,1)S(1)}, bf16[2,2,128...) custom-call(s32[16]{0:T(128)S(1)} %stack.31.place, ...), custom_call_target="tpu_custom_call" | custom-call | bytes 4194304 | tf_op jit(solution)/shard_map/cut/pallas_call | solution.py:99
  10.7 2.6 %collective-permute-start.3 = (bf16[2,2,128,256]{3,2,1,0:T(8,128)(2,1)S(1)}, bf16[2,2,128,256]{3,2,1,0:T(8,128)(2,1)S(1)}, u32[]{:S(2)}, u32[]{:S(2)}) collective-permute-start(bf16[2,2,128,256]{3,2,1,0:T(8,128)(2,1)S(1)} %get-tuple-element.53), channel_id=1, source_target_pairs={{0,12},{2,14},{4,8},{6,10},{8,4},{10,6},{12,0},{14,2},{1,13},{3,15... | collective-permute-start | bytes 786440 | tf_op jit(solution)/shard_map/ppermute | solution.py:325
  13.2 0.6 collective-permute-done.1.came_b
  13.8 0.6 fold.2
  14.4 1.9 %collective-permute-start.2 = (bf16[3,64,256]{2,1,0:T(8,128)(2,1)S(1)}, bf16[3,64,256]{2,1,0:T(8,128)(2,1)S(1)}, u32[]{:S(2)}, u32[]{:S(2)}) collective-permute-start(bf16[3,64,256]{2,1,0:T(8,128)(2,1)S(1)} %get-tuple-element.52), channel_id=1, source_target_pairs={{0,4},{2,6},{4,0},{6,2},{8,12},{10,14},{12,8},{14,10},{1,5},{3,7},... | collective-permute-start | bytes 294920 | tf_op jit(solution)/shard_map/ppermute | solution.py:325
  16.3 0.5 collective-permute-start.4
  16.8 1.5 %collective-permute-start.7 = (bf16[4,2,128,256]{3,2,1,0:T(8,128)(2,1)S(1)}, bf16[4,2,128,256]{3,2,1,0:T(8,128)(2,1)S(1)}, u32[]{:S(2)}, u32[]{:S(2)}) collective-permute-start(bf16[4,2,128,256]{3,2,1,0:T(8,128)(2,1)S(1)} %get-tuple-element.58.refs_0_), channel_id=1, source_target_pairs={{0,2},{2,0},{4,6},{6,4},{8,10},{10,8},{12,14},{14,12},{1,3},{3,1},... | collective-permute-start | bytes 1572872 | tf_op jit(solution)/shard_map/ppermute | solution.py:325
  18.3 4.3 %collective-permute-done.3.refs_3_ = bf16[2,2,128,256]{3,2,1,0:T(8,128)(2,1)S(1)} collective-permute-done((bf16[2,2,128,256]{3,2,1,0:T(8,128)(2,1)S(1)}, bf16[2,2,128,256]{3,2,1,0:T(8,128)(2,1)S(1)}, u32[]{:S(2)}, u32[]{:S(2)}) %collective-permute-start.3) | collective-permute-done | bytes 262176 | tf_op jit(solution)/shard_map/ppermute | solution.py:325
  22.6 0.2 collective-permute-done.2.came_a
  22.8 0.6 fold.3
  23.4 4.9 %collective-permute-start.5 = (bf16[3,32,512]{2,1,0:T(8,128)(2,1)S(1)}, bf16[3,32,512]{2,1,0:T(8,128)(2,1)S(1)}, u32[]{:S(2)}, u32[]{:S(2)}) collective-permute-start(bf16[3,32,512]{2,1,0:T(8,128)(2,1)S(1)} %get-tuple-element.57), channel_id=1, source_target_pairs={{0,8},{2,10},{4,12},{6,14},{8,0},{10,2},{12,4},{14,6},{1,9},{3,11}... | collective-permute-start | bytes 294920 | tf_op jit(solution)/shard_map/ppermute | solution.py:325
  28.3 0.1 collective-permute-start.8
  28.4 0.7 collective-permute-start.10
  29.1 2.8 %collective-permute-done.5 = bf16[3,32,512]{2,1,0:T(8,128)(2,1)S(1)} collective-permute-done((bf16[3,32,512]{2,1,0:T(8,128)(2,1)S(1)}, bf16[3,32,512]{2,1,0:T(8,128)(2,1)S(1)}, u32[]{:S(2)}, u32[]{:S(2)}) %collective-permute-start.5) | collective-permute-done | bytes 98336 | tf_op jit(solution)/shard_map/ppermute | solution.py:325
  32.0 3.0 %collective-permute-start.6 = (bf16[1,3,32,512]{3,2,1,0:T(8,128)(2,1)S(1)}, bf16[1,3,32,512]{3,2,1,0:T(8,128)(2,1)S(1)}, u32[]{:S(2)}, u32[]{:S(2)}) collective-permute-start(bf16[1,3,32,512]{3,2,1,0:T(8,128)(2,1)S(1)} %fusion.field), channel_id=1, source_target_pairs={{0,8},{2,10},{4,12},{6,14},{8,0},{10,2},{12,4},{14,6},{1,9},{3,11}... | collective-permute-start | bytes 294920 | tf_op jit(solution)/shard_map/ppermute | solution.py:325
  35.0 2.1 %collective-permute-done.8.refs_1_ = bf16[2,2,128,256]{3,2,1,0:T(8,128)(2,1)S(1)} collective-permute-done((bf16[2,2,128,256]{3,2,1,0:T(8,128)(2,1)S(1)}, bf16[2,2,128,256]{3,2,1,0:T(8,128)(2,1)S(1)}, u32[]{:S(2)}, u32[]{:S(2)}) %collective-permute-start.8) | collective-permute-done | bytes 262176 | tf_op jit(solution)/shard_map/ppermute | solution.py:325
  37.1 6.5 %collective-permute-done.6.came = bf16[1,3,32,512]{3,2,1,0:T(8,128)(2,1)S(1)} collective-permute-done((bf16[1,3,32,512]{3,2,1,0:T(8,128)(2,1)S(1)}, bf16[1,3,32,512]{3,2,1,0:T(8,128)(2,1)S(1)}, u32[]{:S(2)}, u32[]{:S(2)}) %collective-permute-start.6) | collective-permute-done | bytes 98336 | tf_op jit(solution)/shard_map/ppermute | solution.py:325
  43.7 0.7 copy-done.1
  44.3 2.0 %collective-permute-start.21 = (bf16[2,2,128,256]{3,2,1,0:T(8,128)(2,1)S(1)}, bf16[2,2,128,256]{3,2,1,0:T(8,128)(2,1)S(1)}, u32[]{:S(2)}, u32[]{:S(2)}) collective-permute-start(bf16[2,2,128,256]{3,2,1,0:T(8,128)(2,1)S(1)} %get-tuple-element.71), channel_id=1, source_target_pairs={{0,4},{2,6},{4,0},{6,2},{8,12},{10,14},{12,8},{14,10},{1,5},{3,7},... | collective-permute-start | bytes 786440 | tf_op jit(solution)/shard_map/ppermute | solution.py:325
  46.4 1.9 %collective-permute-start.11 = (bf16[2,3,32,256]{3,2,1,0:T(8,128)(2,1)S(1)}, bf16[2,3,32,256]{3,2,1,0:T(8,128)(2,1)S(1)}, u32[]{:S(2)}, u32[]{:S(2)}) collective-permute-start(bf16[2,3,32,256]{3,2,1,0:T(8,128)(2,1)S(1)} %get-tuple-element.63.own_b), channel_id=1, source_target_pairs={{0,2},{2,0},{4,6},{6,4},{8,10},{10,8},{12,14},{14,12},{1,3},{3,1},... | collective-permute-start | bytes 294920 | tf_op jit(solution)/shard_map/ppermute | solution.py:325
  48.2 2.5 %collective-permute-done.9.came_a = bf16[2,3,32,256]{3,2,1,0:T(8,128)(2,1)S(1)} collective-permute-done((bf16[2,3,32,256]{3,2,1,0:T(8,128)(2,1)S(1)}, bf16[2,3,32,256]{3,2,1,0:T(8,128)(2,1)S(1)}, u32[]{:S(2)}, u32[]{:S(2)}) %collective-permute-start.9) | collective-permute-done | bytes 98336 | tf_op jit(solution)/shard_map/ppermute | solution.py:325
  50.8 0.2 collective-permute-start.14
  51.0 0.8 collective-permute-done.11.came_b
  51.8 0.8 gather.4
  52.6 0.7 copy-done.3
  53.2 2.2 %collective-permute-start.12 = (bf16[4,3,32,256]{3,2,1,0:T(8,128)(2,1)}, bf16[4,3,32,256]{3,2,1,0:T(8,128)(2,1)}, u32[]{:S(2)}, u32[]{:S(2)}) collective-permute-start(bf16[4,3,32,256]{3,2,1,0:T(8,128)(2,1)} %get-tuple-element.66), channel_id=1, source_target_pairs={{0,2},{2,0},{4,6},{6,4},{8,10},{10,8},{12,14},{14,12},{1,3},{3,1},... | collective-permute-start | bytes 589832 | tf_op jit(solution)/shard_map/ppermute | solution.py:325
  55.4 1.1 %collective-permute-start.15 = (bf16[4,3,32,256]{3,2,1,0:T(8,128)(2,1)}, bf16[4,3,32,256]{3,2,1,0:T(8,128)(2,1)}, u32[]{:S(2)}, u32[]{:S(2)}) collective-permute-start(bf16[4,3,32,256]{3,2,1,0:T(8,128)(2,1)} %get-tuple-element.69), channel_id=1, source_target_pairs={{0,4},{2,6},{4,0},{6,2},{8,12},{10,14},{12,8},{14,10},{1,5},{3,7},... | collective-permute-start | bytes 589832 | tf_op jit(solution)/shard_map/ppermute | solution.py:325
  56.5 1.5 %collective-permute-done.21.refs_1_ = bf16[2,2,128,256]{3,2,1,0:T(8,128)(2,1)S(1)} collective-permute-done((bf16[2,2,128,256]{3,2,1,0:T(8,128)(2,1)S(1)}, bf16[2,2,128,256]{3,2,1,0:T(8,128)(2,1)S(1)}, u32[]{:S(2)}, u32[]{:S(2)}) %collective-permute-start.21) | collective-permute-done | bytes 262176 | tf_op jit(solution)/shard_map/ppermute | solution.py:325
  58.0 0.5 collective-permute-start.23
  58.6 3.2 %collective-permute-done.19.refs_2_ = bf16[2,2,128,256]{3,2,1,0:T(8,128)(2,1)S(1)} collective-permute-done((bf16[2,2,128,256]{3,2,1,0:T(8,128)(2,1)S(1)}, bf16[2,2,128,256]{3,2,1,0:T(8,128)(2,1)S(1)}, u32[]{:S(2)}, u32[]{:S(2)}) %collective-permute-start.19) | collective-permute-done | bytes 262176 | tf_op jit(solution)/shard_map/ppermute | solution.py:325
  61.8 0.5 collective-permute-start.22
  62.3 0.5 collective-permute-start.20
  62.8 1.5 %collective-permute-start.25 = (bf16[2,2,128,256]{3,2,1,0:T(8,128)(2,1)S(1)}, bf16[2,2,128,256]{3,2,1,0:T(8,128)(2,1)S(1)}, u32[]{:S(2)}, u32[]{:S(2)}) collective-permute-start(bf16[2,2,128,256]{3,2,1,0:T(8,128)(2,1)S(1)} %collective-permute-done.19.refs_2_), channel_id=1, source_target_pairs={{0,2},{2,0},{4,6},{6,4},{8,10},{10,8},{12,14},{14,12},{1,3},{3,1},... | collective-permute-start | bytes 786440 | tf_op jit(solution)/shard_map/ppermute | solution.py:325
  64.3 1.0 %gather.5.refs_2_ = bf16[2,4,3,32,256]{4,3,2,1,0:T(8,128)(2,1)S(1)} custom-call(bf16[4,3,32,256]{3,2,1,0:T(8,128)(2,1)} %collective-permute-done.12.came_a, bf16[4,3,32,256]{3,2,1,0:T(8,128)(2,1)} %collective-permute-done.15.came_b), custom_call_target="tpu_custom_call" | custom-call | bytes 786432 | tf_op jit(solution)/shard_map/gather/pallas_call | solution.py:185
  65.5 2.1 %collective-permute-done.23.refs_5_ = bf16[2,2,128,256]{3,2,1,0:T(8,128)(2,1)S(1)} collective-permute-done((bf16[2,2,128,256]{3,2,1,0:T(8,128)(2,1)S(1)}, bf16[2,2,128,256]{3,2,1,0:T(8,128)(2,1)S(1)}, u32[]{:S(2)}, u32[]{:S(2)}) %collective-permute-start.23) | collective-permute-done | bytes 262176 | tf_op jit(solution)/shard_map/ppermute | solution.py:325
  67.6 3.2 %collective-permute-done.22.refs_2_ = bf16[2,2,128,256]{3,2,1,0:T(8,128)(2,1)S(1)} collective-permute-done((bf16[2,2,128,256]{3,2,1,0:T(8,128)(2,1)}, bf16[2,2,128,256]{3,2,1,0:T(8,128)(2,1)S(1)}, u32[]{:S(2)}, u32[]{:S(2)}) %collective-permute-start.22) | collective-permute-done | bytes 262176 | tf_op jit(solution)/shard_map/ppermute | solution.py:325
  70.9 1.4 %collective-permute-start.24 = (bf16[2,2,128,256]{3,2,1,0:T(8,128)(2,1)S(1)}, bf16[2,2,128,256]{3,2,1,0:T(8,128)(2,1)S(1)}, u32[]{:S(2)}, u32[]{:S(2)}) collective-permute-start(bf16[2,2,128,256]{3,2,1,0:T(8,128)(2,1)S(1)} %collective-permute-done.22.refs_2_), channel_id=1, source_target_pairs={{0,2},{2,0},{4,6},{6,4},{8,10},{10,8},{12,14},{14,12},{1,3},{3,1},... | collective-permute-start | bytes 786440 | tf_op jit(solution)/shard_map/ppermute | solution.py:325
  72.3 0.1 collective-permute-done.17.refs_4_
  72.5 0.9 %copy-done.2 = bf16[2,2,3,32,256]{4,3,2,1,0:T(8,128)(2,1)S(1)} copy-done((bf16[2,2,3,32,256]{4,3,2,1,0:T(8,128)(2,1)S(1)}, bf16[2,2,3,32,256]{4,3,2,1,0:T(8,128)(2,1)}, u32[]{:S(2)}) %copy-start.2) | copy-done | bytes 196632
  73.4 0.9 %copy-done.4 = bf16[2,2,3,32,256]{4,3,2,1,0:T(8,128)(2,1)S(1)} copy-done((bf16[2,2,3,32,256]{4,3,2,1,0:T(8,128)(2,1)S(1)}, bf16[2,2,3,32,256]{4,3,2,1,0:T(8,128)(2,1)}, u32[]{:S(2)}) %copy-start.4) | copy-done | bytes 196632
  74.3 1.1 %prepare.1 = (bf16[2,768,512]{2,1,0:T(8,128)(2,1)S(1)}, bf16[2,3,512,256]{3,2,1,0:T(8,128)(2,1)S(1)}) custom-call(s32[16]{0:T(128)S(1)} %stack.31.place, bf16[2,2,3,32,256]{4,3,2,1,0:T(8,128)(2,1)S(1)} %copy-done.2, bf16[2,2,3,32,256]{4,3,2,1,0:T(8,128)(2,1)S(1)} %copy-done.4, bf16[2,4,3,32,256]{4,3,2,1,0:T(8,128)(2,1)S(1)} %gather.5.refs_2_, ...), custom_call_target="tpu_custom_call" | custom-call | bytes 3145728 | tf_op jit(solution)/shard_map/prepare/pallas_call | solution.py:230
  75.4 5.6 %dress.2.refs_8_ = bf16[4,3,2,128,1024]{4,3,2,1,0:T(8,128)(2,1)} custom-call(s32[16]{0:T(128)S(1)} %stack.31.place, s32[2]{0:T(128)S(1)} %get-tuple-element.88.other_src, s32[2]{0:T(128)S(1)} %get-tuple-element.87.other_snk, bf16[2,768,512]{2,1,0:T(8,128)(2,1)S(1)} %get-tuple-element.73.left, bf16[2,3,512,256]{3,2,1,0:T(8,128)(2,1)S(1)} %get-tuple-element.74.sink, ...), custom_call_target="tpu_custom_call" | custom-call | flops 3221225472 | bytes 2097152 | tf_op jit(solution)/shard_map/dress/pallas_call | solution.py:290
  81.0 5.5 %dress.3 = bf16[4,3,2,128,1024]{4,3,2,1,0:T(8,128)(2,1)} custom-call(s32[16]{0:T(128)S(1)} %stack.31.place, s32[2]{0:T(128)S(1)} %get-tuple-element.90.other_src, s32[2]{0:T(128)S(1)} %get-tuple-element.89.other_snk, bf16[2,768,512]{2,1,0:T(8,128)(2,1)S(1)} %get-tuple-element.73.left, ...), custom_call_target="tpu_custom_call", output_to_operand_aliasing={{}: (13, {})} | custom-call | flops 3221225472 | bytes 2097152 | tf_op jit(solution)/shard_map/dress/pallas_call | solution.py:290
  (33 shorter events, 0.3 us)
Async XLA Ops:
  0.0 9.0 %copy-start = (bf16[4,2,128,1024]{3,2,1,0:T(8,128)(2,1)S(1)}, bf16[4,2,128,1024]{3,2,1,0:T(8,128)(2,1)}, u32[]{:S(2)}) copy-start(bf16[4,2,128,1024]{3,2,1,0:T(8,128)(2,1)} %panels.1) | copy-start | bytes 6291460
  1.0 1.1 %copy-start.5 = (bf16[1,2,3,192,256]{4,3,2,1,0:T(8,128)(2,1)S(1)}, bf16[1,2,3,192,256]{4,3,2,1,0:T(8,128)(2,1)}, u32[]{:S(2)}) copy-start(bf16[1,2,3,192,256]{4,3,2,1,0:T(8,128)(2,1)} %param.4) | copy-start | bytes 1769476
  4.4 8.8 %collective-permute-start = (bf16[3,128,256]{2,1,0:T(8,128)(2,1)S(1)}, bf16[3,128,256]{2,1,0:T(8,128)(2,1)S(1)}, u32[]{:S(2)}, u32[]{:S(2)}) collective-permute-start(bf16[3,128,256]{2,1,0:T(8,128)(2,1)S(1)} %get-tuple-element.48), channel_id=1, source_target_pairs={{0,2},{2,0},{4,6},{6,4},{8,10},{10,8},{12,14},{14,12},{1,3},{3,1},... | collective-permute-start | bytes 589832 | tf_op jit(solution)/shard_map/ppermute | solution.py:325
  7.4 6.4 %collective-permute-start.1 = (bf16[3,128,256]{2,1,0:T(8,128)(2,1)S(1)}, bf16[3,128,256]{2,1,0:T(8,128)(2,1)S(1)}, u32[]{:S(2)}, u32[]{:S(2)}) collective-permute-start(bf16[3,128,256]{2,1,0:T(8,128)(2,1)S(1)} %get-tuple-element.49), channel_id=1, source_target_pairs={{0,4},{2,6},{4,0},{6,2},{8,12},{10,14},{12,8},{14,10},{1,5},{3,7},... | collective-permute-start | bytes 589832 | tf_op jit(solution)/shard_map/ppermute | solution.py:325
  10.6 54.8 %copy-start.6 = (s32[4,2]{0,1:T(2,128)S(1)}, s32[4,2]{0,1:T(2,128)}, u32[]{:S(2)}) copy-start(s32[4,2]{0,1:T(2,128)} %param.6) | copy-start | bytes 100
  10.7 11.9 %collective-permute-start.3 = (bf16[2,2,128,256]{3,2,1,0:T(8,128)(2,1)S(1)}, bf16[2,2,128,256]{3,2,1,0:T(8,128)(2,1)S(1)}, u32[]{:S(2)}, u32[]{:S(2)}) collective-permute-start(bf16[2,2,128,256]{3,2,1,0:T(8,128)(2,1)S(1)} %get-tuple-element.53), channel_id=1, source_target_pairs={{0,12},{2,14},{4,8},{6,10},{8,4},{10,6},{12,0},{14,2},{1,13},{3,15... | collective-permute-start | bytes 786440 | tf_op jit(solution)/shard_map/ppermute | solution.py:325
  14.4 8.4 %collective-permute-start.2 = (bf16[3,64,256]{2,1,0:T(8,128)(2,1)S(1)}, bf16[3,64,256]{2,1,0:T(8,128)(2,1)S(1)}, u32[]{:S(2)}, u32[]{:S(2)}) collective-permute-start(bf16[3,64,256]{2,1,0:T(8,128)(2,1)S(1)} %get-tuple-element.52), channel_id=1, source_target_pairs={{0,4},{2,6},{4,0},{6,2},{8,12},{10,14},{12,8},{14,10},{1,5},{3,7},... | collective-permute-start | bytes 294920 | tf_op jit(solution)/shard_map/ppermute | solution.py:325
  16.3 6.5 %collective-permute-start.4 = (bf16[3,64,256]{2,1,0:T(8,128)(2,1)S(1)}, bf16[3,64,256]{2,1,0:T(8,128)(2,1)S(1)}, u32[]{:S(2)}, u32[]{:S(2)}) collective-permute-start(bf16[3,64,256]{2,1,0:T(8,128)(2,1)S(1)} %get-tuple-element.55), channel_id=1, source_target_pairs={{0,2},{2,0},{4,6},{6,4},{8,10},{10,8},{12,14},{14,12},{1,3},{3,1},... | collective-permute-start | bytes 294920 | tf_op jit(solution)/shard_map/ppermute | solution.py:325
  16.8 26.8 %collective-permute-start.7 = (bf16[4,2,128,256]{3,2,1,0:T(8,128)(2,1)S(1)}, bf16[4,2,128,256]{3,2,1,0:T(8,128)(2,1)S(1)}, u32[]{:S(2)}, u32[]{:S(2)}) collective-permute-start(bf16[4,2,128,256]{3,2,1,0:T(8,128)(2,1)S(1)} %get-tuple-element.58.refs_0_), channel_id=1, source_target_pairs={{0,2},{2,0},{4,6},{6,4},{8,10},{10,8},{12,14},{14,12},{1,3},{3,1},... | collective-permute-start | bytes 1572872 | tf_op jit(solution)/shard_map/ppermute | solution.py:325
  23.4 8.5 %collective-permute-start.5 = (bf16[3,32,512]{2,1,0:T(8,128)(2,1)S(1)}, bf16[3,32,512]{2,1,0:T(8,128)(2,1)S(1)}, u32[]{:S(2)}, u32[]{:S(2)}) collective-permute-start(bf16[3,32,512]{2,1,0:T(8,128)(2,1)S(1)} %get-tuple-element.57), channel_id=1, source_target_pairs={{0,8},{2,10},{4,12},{6,14},{8,0},{10,2},{12,4},{14,6},{1,9},{3,11}... | collective-permute-start | bytes 294920 | tf_op jit(solution)/shard_map/ppermute | solution.py:325
  28.3 8.8 %collective-permute-start.8 = (bf16[2,2,128,256]{3,2,1,0:T(8,128)(2,1)S(1)}, bf16[2,2,128,256]{3,2,1,0:T(8,128)(2,1)S(1)}, u32[]{:S(2)}, u32[]{:S(2)}) collective-permute-start(bf16[2,2,128,256]{3,2,1,0:T(8,128)(2,1)S(1)} %get-tuple-element.59), channel_id=1, source_target_pairs={{0,4},{2,6},{4,0},{6,2},{8,12},{10,14},{12,8},{14,10},{1,5},{3,7},... | collective-permute-start | bytes 786440 | tf_op jit(solution)/shard_map/ppermute | solution.py:325
  28.4 17.9 %collective-permute-start.10 = (bf16[2,2,128,256]{3,2,1,0:T(8,128)(2,1)S(1)}, bf16[2,2,128,256]{3,2,1,0:T(8,128)(2,1)S(1)}, u32[]{:S(2)}, u32[]{:S(2)}) collective-permute-start(bf16[2,2,128,256]{3,2,1,0:T(8,128)(2,1)S(1)} %collective-permute-done.3.refs_3_), channel_id=1, source_target_pairs={{0,2},{2,0},{4,6},{6,4},{8,10},{10,8},{12,14},{14,12},{1,3},{3,1},... | collective-permute-start | bytes 786440 | tf_op jit(solution)/shard_map/ppermute | solution.py:325
  32.0 11.6 %collective-permute-start.6 = (bf16[1,3,32,512]{3,2,1,0:T(8,128)(2,1)S(1)}, bf16[1,3,32,512]{3,2,1,0:T(8,128)(2,1)S(1)}, u32[]{:S(2)}, u32[]{:S(2)}) collective-permute-start(bf16[1,3,32,512]{3,2,1,0:T(8,128)(2,1)S(1)} %fusion.field), channel_id=1, source_target_pairs={{0,8},{2,10},{4,12},{6,14},{8,0},{10,2},{12,4},{14,6},{1,9},{3,11}... | collective-permute-start | bytes 294920 | tf_op jit(solution)/shard_map/ppermute | solution.py:325
  35.0 20.4 %collective-permute-start.13 = (bf16[2,2,128,256]{3,2,1,0:T(8,128)(2,1)S(1)}, bf16[2,2,128,256]{3,2,1,0:T(8,128)(2,1)S(1)}, u32[]{:S(2)}, u32[]{:S(2)}) collective-permute-start(bf16[2,2,128,256]{3,2,1,0:T(8,128)(2,1)S(1)} %get-tuple-element.67), channel_id=1, source_target_pairs={{0,12},{2,14},{4,8},{6,10},{8,4},{10,6},{12,0},{14,2},{1,13},{3,15... | collective-permute-start | bytes 786440 | tf_op jit(solution)/shard_map/ppermute | solution.py:325
  43.6 0.7 copy-start.1
  44.3 6.5 %collective-permute-start.9 = (bf16[2,3,32,256]{3,2,1,0:T(8,128)(2,1)S(1)}, bf16[2,3,32,256]{3,2,1,0:T(8,128)(2,1)S(1)}, u32[]{:S(2)}, u32[]{:S(2)}) collective-permute-start(bf16[2,3,32,256]{3,2,1,0:T(8,128)(2,1)S(1)} %get-tuple-element.62.own_a), channel_id=1, source_target_pairs={{0,4},{2,6},{4,0},{6,2},{8,12},{10,14},{12,8},{14,10},{1,5},{3,7},... | collective-permute-start | bytes 294920 | tf_op jit(solution)/shard_map/ppermute | solution.py:325
  44.3 13.7 %collective-permute-start.21 = (bf16[2,2,128,256]{3,2,1,0:T(8,128)(2,1)S(1)}, bf16[2,2,128,256]{3,2,1,0:T(8,128)(2,1)S(1)}, u32[]{:S(2)}, u32[]{:S(2)}) collective-permute-start(bf16[2,2,128,256]{3,2,1,0:T(8,128)(2,1)S(1)} %get-tuple-element.71), channel_id=1, source_target_pairs={{0,4},{2,6},{4,0},{6,2},{8,12},{10,14},{12,8},{14,10},{1,5},{3,7},... | collective-permute-start | bytes 786440 | tf_op jit(solution)/shard_map/ppermute | solution.py:325
  46.3 15.4 %collective-permute-start.19 = (bf16[2,2,128,256]{3,2,1,0:T(8,128)(2,1)S(1)}, bf16[2,2,128,256]{3,2,1,0:T(8,128)(2,1)S(1)}, u32[]{:S(2)}, u32[]{:S(2)}) collective-permute-start(bf16[2,2,128,256]{3,2,1,0:T(8,128)(2,1)S(1)} %get-tuple-element.70), channel_id=1, source_target_pairs={{0,8},{2,10},{4,12},{6,14},{8,0},{10,2},{12,4},{14,6},{1,9},{3,11}... | collective-permute-start | bytes 786440 | tf_op jit(solution)/shard_map/ppermute | solution.py:325
  46.4 5.4 %collective-permute-start.11 = (bf16[2,3,32,256]{3,2,1,0:T(8,128)(2,1)S(1)}, bf16[2,3,32,256]{3,2,1,0:T(8,128)(2,1)S(1)}, u32[]{:S(2)}, u32[]{:S(2)}) collective-permute-start(bf16[2,3,32,256]{3,2,1,0:T(8,128)(2,1)S(1)} %get-tuple-element.63.own_b), channel_id=1, source_target_pairs={{0,2},{2,0},{4,6},{6,4},{8,10},{10,8},{12,14},{14,12},{1,3},{3,1},... | collective-permute-start | bytes 294920 | tf_op jit(solution)/shard_map/ppermute | solution.py:325
  50.8 11.5 %collective-permute-start.14 = (bf16[2,2,128,256]{3,2,1,0:T(8,128)(2,1)S(1)}, bf16[2,2,128,256]{3,2,1,0:T(8,128)(2,1)S(1)}, u32[]{:S(2)}, u32[]{:S(2)}) collective-permute-start(bf16[2,2,128,256]{3,2,1,0:T(8,128)(2,1)S(1)} %collective-permute-done.8.refs_1_), channel_id=1, source_target_pairs={{0,2},{2,0},{4,6},{6,4},{8,10},{10,8},{12,14},{14,12},{1,3},{3,1},... | collective-permute-start | bytes 786440 | tf_op jit(solution)/shard_map/ppermute | solution.py:325
  52.6 0.7 copy-start.3
  53.2 9.6 %collective-permute-start.12 = (bf16[4,3,32,256]{3,2,1,0:T(8,128)(2,1)}, bf16[4,3,32,256]{3,2,1,0:T(8,128)(2,1)}, u32[]{:S(2)}, u32[]{:S(2)}) collective-permute-start(bf16[4,3,32,256]{3,2,1,0:T(8,128)(2,1)} %get-tuple-element.66), channel_id=1, source_target_pairs={{0,2},{2,0},{4,6},{6,4},{8,10},{10,8},{12,14},{14,12},{1,3},{3,1},... | collective-permute-start | bytes 589832 | tf_op jit(solution)/shard_map/ppermute | solution.py:325
  55.4 8.9 %collective-permute-start.15 = (bf16[4,3,32,256]{3,2,1,0:T(8,128)(2,1)}, bf16[4,3,32,256]{3,2,1,0:T(8,128)(2,1)}, u32[]{:S(2)}, u32[]{:S(2)}) collective-permute-start(bf16[4,3,32,256]{3,2,1,0:T(8,128)(2,1)} %get-tuple-element.69), channel_id=1, source_target_pairs={{0,4},{2,6},{4,0},{6,2},{8,12},{10,14},{12,8},{14,10},{1,5},{3,7},... | collective-permute-start | bytes 589832 | tf_op jit(solution)/shard_map/ppermute | solution.py:325
  58.0 9.5 %collective-permute-start.23 = (bf16[2,2,128,256]{3,2,1,0:T(8,128)(2,1)S(1)}, bf16[2,2,128,256]{3,2,1,0:T(8,128)(2,1)S(1)}, u32[]{:S(2)}, u32[]{:S(2)}) collective-permute-start(bf16[2,2,128,256]{3,2,1,0:T(8,128)(2,1)S(1)} %collective-permute-done.21.refs_1_), channel_id=1, source_target_pairs={{0,2},{2,0},{4,6},{6,4},{8,10},{10,8},{12,14},{14,12},{1,3},{3,1},... | collective-permute-start | bytes 786440 | tf_op jit(solution)/shard_map/ppermute | solution.py:325
  61.8 9.0 %collective-permute-start.22 = (bf16[2,2,128,256]{3,2,1,0:T(8,128)(2,1)}, bf16[2,2,128,256]{3,2,1,0:T(8,128)(2,1)S(1)}, u32[]{:S(2)}, u32[]{:S(2)}) collective-permute-start(bf16[2,2,128,256]{3,2,1,0:T(8,128)(2,1)} %get-tuple-element.77), channel_id=1, source_target_pairs={{0,8},{2,10},{4,12},{6,14},{8,0},{10,2},{12,4},{14,6},{1,9},{3,11}... | collective-permute-start | bytes 786440 | tf_op jit(solution)/shard_map/ppermute | solution.py:325
  62.3 8.6 %collective-permute-start.20 = (bf16[2,2,128,256]{3,2,1,0:T(8,128)(2,1)S(1)}, bf16[2,2,128,256]{3,2,1,0:T(8,128)(2,1)S(1)}, u32[]{:S(2)}, u32[]{:S(2)}) collective-permute-start(bf16[2,2,128,256]{3,2,1,0:T(8,128)(2,1)S(1)} %collective-permute-done.13.refs_3_), channel_id=1, source_target_pairs={{0,2},{2,0},{4,6},{6,4},{8,10},{10,8},{12,14},{14,12},{1,3},{3,1},... | collective-permute-start | bytes 786440 | tf_op jit(solution)/shard_map/ppermute | solution.py:325
  62.8 12.6 %collective-permute-start.25 = (bf16[2,2,128,256]{3,2,1,0:T(8,128)(2,1)S(1)}, bf16[2,2,128,256]{3,2,1,0:T(8,128)(2,1)S(1)}, u32[]{:S(2)}, u32[]{:S(2)}) collective-permute-start(bf16[2,2,128,256]{3,2,1,0:T(8,128)(2,1)S(1)} %collective-permute-done.19.refs_2_), channel_id=1, source_target_pairs={{0,2},{2,0},{4,6},{6,4},{8,10},{10,8},{12,14},{14,12},{1,3},{3,1},... | collective-permute-start | bytes 786440 | tf_op jit(solution)/shard_map/ppermute | solution.py:325
  65.4 6.9 %collective-permute-start.18 = (bf16[2,4,3,32,256]{4,3,2,1,0:T(8,128)(2,1)S(1)}, bf16[2,4,3,32,256]{4,3,2,1,0:T(8,128)(2,1)S(1)}, u32[]{:S(2)}, u32[]{:S(2)}) collective-permute-start(bf16[2,4,3,32,256]{4,3,2,1,0:T(8,128)(2,1)S(1)} %gather.5.refs_2_), channel_id=1, source_target_pairs={{0,1},{1,0},{2,3},{3,2},{4,5},{5,4},{6,7},{7,6},{8,9},{9,8},{10,11... | collective-permute-start | bytes 1179656 | tf_op jit(solution)/shard_map/ppermute | solution.py:325
  67.6 4.8 %collective-permute-start.16 = (bf16[2,2,3,32,256]{4,3,2,1,0:T(8,128)(2,1)}, bf16[2,2,3,32,256]{4,3,2,1,0:T(8,128)(2,1)S(1)}, u32[]{:S(2)}, u32[]{:S(2)}) collective-permute-start(bf16[2,2,3,32,256]{4,3,2,1,0:T(8,128)(2,1)} %copy-done.1), channel_id=1, source_target_pairs={{0,1},{1,0},{2,3},{3,2},{4,5},{5,4},{6,7},{7,6},{8,9},{9,8},{10,11... | collective-permute-start | bytes 589832 | tf_op jit(solution)/shard_map/ppermute | solution.py:325
  70.8 1.7 %collective-permute-start.17 = (bf16[2,2,3,32,256]{4,3,2,1,0:T(8,128)(2,1)}, bf16[2,2,3,32,256]{4,3,2,1,0:T(8,128)(2,1)S(1)}, u32[]{:S(2)}, u32[]{:S(2)}) collective-permute-start(bf16[2,2,3,32,256]{4,3,2,1,0:T(8,128)(2,1)} %copy-done.3), channel_id=1, source_target_pairs={{0,1},{1,0},{2,3},{3,2},{4,5},{5,4},{6,7},{7,6},{8,9},{9,8},{10,11... | collective-permute-start | bytes 589832 | tf_op jit(solution)/shard_map/ppermute | solution.py:325
  70.9 10.1 %collective-permute-start.24 = (bf16[2,2,128,256]{3,2,1,0:T(8,128)(2,1)S(1)}, bf16[2,2,128,256]{3,2,1,0:T(8,128)(2,1)S(1)}, u32[]{:S(2)}, u32[]{:S(2)}) collective-permute-start(bf16[2,2,128,256]{3,2,1,0:T(8,128)(2,1)S(1)} %collective-permute-done.22.refs_2_), channel_id=1, source_target_pairs={{0,2},{2,0},{4,6},{6,4},{8,10},{10,8},{12,14},{14,12},{1,3},{3,1},... | collective-permute-start | bytes 786440 | tf_op jit(solution)/shard_map/ppermute | solution.py:325
  72.5 0.9 %copy-start.2 = (bf16[2,2,3,32,256]{4,3,2,1,0:T(8,128)(2,1)S(1)}, bf16[2,2,3,32,256]{4,3,2,1,0:T(8,128)(2,1)}, u32[]{:S(2)}) copy-start(bf16[2,2,3,32,256]{4,3,2,1,0:T(8,128)(2,1)} %copy-done.1) | copy-start | bytes 589828
  73.4 0.9 %copy-start.4 = (bf16[2,2,3,32,256]{4,3,2,1,0:T(8,128)(2,1)S(1)}, bf16[2,2,3,32,256]{4,3,2,1,0:T(8,128)(2,1)}, u32[]{:S(2)}) copy-start(bf16[2,2,3,32,256]{4,3,2,1,0:T(8,128)(2,1)} %copy-done.3) | copy-start | bytes 589828

commit v6 on v5

--- a/solution.py
+++ b/solution.py
@@ -306,12 +306,12 @@
     )(place, other_src[first_pair : first_pair + pairs], other_snk[first_pair : first_pair + pairs], *operands)
 
 
-CHUNKS = (1, 2, 2, 2)
+CHUNKS = (2, 2, 2, 2)
 HOOKS = [
     [],
     [("z", 3, 0)],
-    [],
-    [("x", 0, 0), ("z", 1, 0)],
+    [("x", 0, 0)],
+    [("x", 0, 1), ("z", 1, 0)],
     [("x", 3, 0)],
     [("z", 3, 1), ("x", 1, 0)],
     [("z", 2, 0), ("x", 3, 1), ("z", 1, 1)],

time: 86.7 us -> 85.6 us (0.987)
  waiting for transfers between devices: 30 us -> 34.1 us
  starting transfers between devices: 31.8 us -> 29.1 us
  local copies, waits for them, and re-layouts: 5.35 us -> 2.86 us
    ppermute x26 -> x27, waiting for transfers between devices: 30 us -> 34.1 us  [exchange(): lax.ppermute(value, axis, [(i, i ^ mask) for i in range(lax.axis_size(axi...]
    ppermute x26 -> x27, starting transfers between devices: 31.8 us -> 29.1 us  [exchange(): lax.ppermute(value, axis, [(i, i ^ mask) for i in range(lax.axis_size(axi...]
    unnamed x14 -> x18, local copies, waits for them, and re-layouts: 4.28 us -> 1.79 us
    pallas_call x3, Pallas kernels: 1.86 us -> 0.82 us  [gather(): pl.pallas_call(kernel, out_shape=[jax.ShapeDtypeStruct(shape, BF16) for s...]
    pallas_call x2, Pallas kernels: 11.1 us -> 12 us  [dress(): pl.pallas_call(functools.partial(dress_kernel, count, chained), out_shape...]
  transfers between devices with their start and end apart: 26 -> 27, of which waited for: 13 -> 11; matrix products, arithmetic and copies ran while one was open for 0% -> 0% of each run, Pallas kernels for 13% -> 13%
where the time goes in v6:
time: 85.6 us; the launch traced here: 85.4 us
  waiting for transfers between devices  34.1 us (40%)
  starting transfers between devices  29.1 us (34%)
  Pallas kernels  19.2 us (22%)
  local copies, waits for them, and re-layouts  2.86 us (3%)
    ppermute x27, waiting for transfers between devices, exchange(): lax.ppermute(value, axis, [(i, i ^ mask) for i in range(lax.axis_size(axi...  34.1 us
    ppermute x27, starting transfers between devices, exchange(): lax.ppermute(value, axis, [(i, i ^ mask) for i in range(lax.axis_size(axi...  29.1 us
    pallas_call x2, Pallas kernels, dress(): pl.pallas_call(functools.partial(dress_kernel, count, chained), out_shape...  12 us
    pallas_call x1, Pallas kernels, gram_halves(): pl.pallas_call(functools.partial(gram_kernel, factor), out_shape=[jax.Sha...  2.39 us
    unnamed x18, local copies, waits for them, and re-layouts  1.79 us
  transfers between devices with their start and end apart: 27, of which 11 were waited for; matrix products, arithmetic and copies ran while one was open for 0% of the time, Pallas kernels for 13%

profile of v6, /device:TPU:0, one launch (start us, length us, event | category | flops | bytes accessed | tf_op | source)
XLA Modules:
  0.0 85.4 jit_solution(11985241341204631610)
XLA Ops:
  0.0 0.9 %reshape.7 = s32[9]{0:T(128)S(1)} reshape(s32[3,3]{1,0:T(4,128)} %param.5) | data formatting | bytes 72 | tf_op jit(solution)/shard_map/reshape | solution.py:339
  0.9 0.1 stack.31.place
  1.0 1.1 %copy-done.1 = bf16[1,2,3,192,256]{4,3,2,1,0:T(8,128)(2,1)S(1)} copy-done((bf16[1,2,3,192,256]{4,3,2,1,0:T(8,128)(2,1)S(1)}, bf16[1,2,3,192,256]{4,3,2,1,0:T(8,128)(2,1)}, u32[]{:S(2)}) %copy-start.1) | copy-done | bytes 589848
  2.1 2.4 %gram.1 = (bf16[3,128,256]{2,1,0:T(8,128)(2,1)S(1)}, bf16[3,128,256]{2,1,0:T(8,128)(2,1)S(1)}, f32[3,128,256]{2,1,0:T(8,128)S(1)}, f32[3,128,256]{2,1,0:T(8,128)S(1)}) custom-call(s32[16]{0:T(128)S(1)} %stack.31.place, bf16[2,3,192,256]{3,2,1,0:T(8,128)(2,1)S(1)} %bitcast.18), custom_call_target="tpu_custom_call" | custom-call | flops 905969664 | bytes 3145728 | tf_op jit(solution)/shard_map/gram/pallas_call | solution.py:70
  4.5 3.0 %collective-permute-start = (bf16[3,128,256]{2,1,0:T(8,128)(2,1)S(1)}, bf16[3,128,256]{2,1,0:T(8,128)(2,1)S(1)}, u32[]{:S(2)}, u32[]{:S(2)}) collective-permute-start(bf16[3,128,256]{2,1,0:T(8,128)(2,1)S(1)} %get-tuple-element.51), channel_id=1, source_target_pairs={{0,2},{2,0},{4,6},{6,4},{8,10},{10,8},{12,14},{14,12},{1,3},{3,1},... | collective-permute-start | bytes 589832 | tf_op jit(solution)/shard_map/ppermute | solution.py:325
  7.5 1.6 %collective-permute-start.1 = (bf16[3,128,256]{2,1,0:T(8,128)(2,1)S(1)}, bf16[3,128,256]{2,1,0:T(8,128)(2,1)S(1)}, u32[]{:S(2)}, u32[]{:S(2)}) collective-permute-start(bf16[3,128,256]{2,1,0:T(8,128)(2,1)S(1)} %get-tuple-element.52), channel_id=1, source_target_pairs={{0,4},{2,6},{4,0},{6,2},{8,12},{10,14},{12,8},{14,10},{1,5},{3,7},... | collective-permute-start | bytes 589832 | tf_op jit(solution)/shard_map/ppermute | solution.py:325
  9.1 1.7 %cut.1 = (bf16[2,2,128,256]{3,2,1,0:T(8,128)(2,1)S(1)}, bf16[2,2,128,256]{3,2,1,0:T(8,128)(2,1)S(1)}, bf16[2,2,128,256]{3,2,1,0:T(8,128)(2,1)S(1)}, bf16[2,2,128...) custom-call(s32[16]{0:T(128)S(1)} %stack.31.place, ...), custom_call_target="tpu_custom_call" | custom-call | bytes 4194304 | tf_op jit(solution)/shard_map/cut/pallas_call | solution.py:99
  10.7 2.5 %collective-permute-start.3 = (bf16[2,2,128,256]{3,2,1,0:T(8,128)(2,1)S(1)}, bf16[2,2,128,256]{3,2,1,0:T(8,128)(2,1)S(1)}, u32[]{:S(2)}, u32[]{:S(2)}) collective-permute-start(bf16[2,2,128,256]{3,2,1,0:T(8,128)(2,1)S(1)} %get-tuple-element.56), channel_id=1, source_target_pairs={{0,12},{2,14},{4,8},{6,10},{8,4},{10,6},{12,0},{14,2},{1,13},{3,15... | collective-permute-start | bytes 786440 | tf_op jit(solution)/shard_map/ppermute | solution.py:325
  13.3 0.5 collective-permute-start.6
  13.8 0.0 collective-permute-done.1.came_b
  13.8 0.6 fold.2
  14.5 1.8 %collective-permute-start.2 = (bf16[3,64,256]{2,1,0:T(8,128)(2,1)S(1)}, bf16[3,64,256]{2,1,0:T(8,128)(2,1)S(1)}, u32[]{:S(2)}, u32[]{:S(2)}) collective-permute-start(bf16[3,64,256]{2,1,0:T(8,128)(2,1)S(1)} %get-tuple-element.55), channel_id=1, source_target_pairs={{0,4},{2,6},{4,0},{6,2},{8,12},{10,14},{12,8},{14,10},{1,5},{3,7},... | collective-permute-start | bytes 294920 | tf_op jit(solution)/shard_map/ppermute | solution.py:325
  16.3 0.5 collective-permute-start.4
  16.8 5.8 %collective-permute-done.3.refs_3_ = bf16[2,2,128,256]{3,2,1,0:T(8,128)(2,1)S(1)} collective-permute-done((bf16[2,2,128,256]{3,2,1,0:T(8,128)(2,1)S(1)}, bf16[2,2,128,256]{3,2,1,0:T(8,128)(2,1)S(1)}, u32[]{:S(2)}, u32[]{:S(2)}) %collective-permute-start.3) | collective-permute-done | bytes 262176 | tf_op jit(solution)/shard_map/ppermute | solution.py:325
  22.6 0.3 collective-permute-done.2.came_a
  22.9 0.6 fold.3
  23.5 4.8 %collective-permute-start.5 = (bf16[3,32,512]{2,1,0:T(8,128)(2,1)S(1)}, bf16[3,32,512]{2,1,0:T(8,128)(2,1)S(1)}, u32[]{:S(2)}, u32[]{:S(2)}) collective-permute-start(bf16[3,32,512]{2,1,0:T(8,128)(2,1)S(1)} %get-tuple-element.60), channel_id=1, source_target_pairs={{0,8},{2,10},{4,12},{6,14},{8,0},{10,2},{12,4},{14,6},{1,9},{3,11}... | collective-permute-start | bytes 294920 | tf_op jit(solution)/shard_map/ppermute | solution.py:325
  28.3 0.1 collective-permute-start.9
  28.4 0.5 collective-permute-start.8
  28.9 1.5 %collective-permute-start.11 = (bf16[2,2,128,256]{3,2,1,0:T(8,128)(2,1)S(1)}, bf16[2,2,128,256]{3,2,1,0:T(8,128)(2,1)S(1)}, u32[]{:S(2)}, u32[]{:S(2)}) collective-permute-start(bf16[2,2,128,256]{3,2,1,0:T(8,128)(2,1)S(1)} %collective-permute-done.3.refs_3_), channel_id=1, source_target_pairs={{0,2},{2,0},{4,6},{6,4},{8,10},{10,8},{12,14},{14,12},{1,3},{3,1},... | collective-permute-start | bytes 786440 | tf_op jit(solution)/shard_map/ppermute | solution.py:325
  30.4 1.5 %collective-permute-done.5 = bf16[3,32,512]{2,1,0:T(8,128)(2,1)S(1)} collective-permute-done((bf16[3,32,512]{2,1,0:T(8,128)(2,1)S(1)}, bf16[3,32,512]{2,1,0:T(8,128)(2,1)S(1)}, u32[]{:S(2)}, u32[]{:S(2)}) %collective-permute-start.5) | collective-permute-done | bytes 98336 | tf_op jit(solution)/shard_map/ppermute | solution.py:325
  31.9 3.1 %collective-permute-start.7 = (bf16[1,3,32,512]{3,2,1,0:T(8,128)(2,1)S(1)}, bf16[1,3,32,512]{3,2,1,0:T(8,128)(2,1)S(1)}, u32[]{:S(2)}, u32[]{:S(2)}) collective-permute-start(bf16[1,3,32,512]{3,2,1,0:T(8,128)(2,1)S(1)} %fusion.field), channel_id=1, source_target_pairs={{0,8},{2,10},{4,12},{6,14},{8,0},{10,2},{12,4},{14,6},{1,9},{3,11}... | collective-permute-start | bytes 294920 | tf_op jit(solution)/shard_map/ppermute | solution.py:325
  35.1 2.1 %collective-permute-done.9.refs_1_ = bf16[2,2,128,256]{3,2,1,0:T(8,128)(2,1)S(1)} collective-permute-done((bf16[2,2,128,256]{3,2,1,0:T(8,128)(2,1)S(1)}, bf16[2,2,128,256]{3,2,1,0:T(8,128)(2,1)S(1)}, u32[]{:S(2)}, u32[]{:S(2)}) %collective-permute-start.9) | collective-permute-done | bytes 262176 | tf_op jit(solution)/shard_map/ppermute | solution.py:325
  37.1 6.5 %collective-permute-done.7.came = bf16[1,3,32,512]{3,2,1,0:T(8,128)(2,1)S(1)} collective-permute-done((bf16[1,3,32,512]{3,2,1,0:T(8,128)(2,1)S(1)}, bf16[1,3,32,512]{3,2,1,0:T(8,128)(2,1)S(1)}, u32[]{:S(2)}, u32[]{:S(2)}) %collective-permute-start.7) | collective-permute-done | bytes 98336 | tf_op jit(solution)/shard_map/ppermute | solution.py:325
  43.7 0.1 collective-permute-start.10
  43.8 2.0 %collective-permute-start.22 = (bf16[2,2,128,256]{3,2,1,0:T(8,128)(2,1)S(1)}, bf16[2,2,128,256]{3,2,1,0:T(8,128)(2,1)S(1)}, u32[]{:S(2)}, u32[]{:S(2)}) collective-permute-start(bf16[2,2,128,256]{3,2,1,0:T(8,128)(2,1)S(1)} %get-tuple-element.76), channel_id=1, source_target_pairs={{0,4},{2,6},{4,0},{6,2},{8,12},{10,14},{12,8},{14,10},{1,5},{3,7},... | collective-permute-start | bytes 786440 | tf_op jit(solution)/shard_map/ppermute | solution.py:325
  45.8 0.6 collective-permute-start.12
  46.4 4.0 %collective-permute-done.10.came_a = bf16[2,3,32,256]{3,2,1,0:T(8,128)(2,1)S(1)} collective-permute-done((bf16[2,3,32,256]{3,2,1,0:T(8,128)(2,1)S(1)}, bf16[2,3,32,256]{3,2,1,0:T(8,128)(2,1)S(1)}, u32[]{:S(2)}, u32[]{:S(2)}) %collective-permute-start.10) | collective-permute-done | bytes 98336 | tf_op jit(solution)/shard_map/ppermute | solution.py:325
  50.4 0.6 collective-permute-start.15
  51.0 0.8 gather.4
  51.7 1.4 %collective-permute-start.13 = (bf16[4,3,32,256]{3,2,1,0:T(8,128)(2,1)}, bf16[4,3,32,256]{3,2,1,0:T(8,128)(2,1)S(1)}, u32[]{:S(2)}, u32[]{:S(2)}) collective-permute-start(bf16[4,3,32,256]{3,2,1,0:T(8,128)(2,1)} %get-tuple-element.71), channel_id=1, source_target_pairs={{0,2},{2,0},{4,6},{6,4},{8,10},{10,8},{12,14},{14,12},{1,3},{3,1},... | collective-permute-start | bytes 589832 | tf_op jit(solution)/shard_map/ppermute | solution.py:325
  53.2 0.7 collective-permute-start.16
  53.9 4.0 %collective-permute-done.22.refs_1_ = bf16[2,2,128,256]{3,2,1,0:T(8,128)(2,1)S(1)} collective-permute-done((bf16[2,2,128,256]{3,2,1,0:T(8,128)(2,1)S(1)}, bf16[2,2,128,256]{3,2,1,0:T(8,128)(2,1)S(1)}, u32[]{:S(2)}, u32[]{:S(2)}) %collective-permute-start.22) | collective-permute-done | bytes 262176 | tf_op jit(solution)/shard_map/ppermute | solution.py:325
  57.9 0.5 collective-permute-start.24
  58.4 2.7 %collective-permute-done.20.refs_2_ = bf16[2,2,128,256]{3,2,1,0:T(8,128)(2,1)S(1)} collective-permute-done((bf16[2,2,128,256]{3,2,1,0:T(8,128)(2,1)S(1)}, bf16[2,2,128,256]{3,2,1,0:T(8,128)(2,1)S(1)}, u32[]{:S(2)}, u32[]{:S(2)}) %collective-permute-start.20) | collective-permute-done | bytes 262176 | tf_op jit(solution)/shard_map/ppermute | solution.py:325
  61.1 0.7 copy-done.6
  61.8 0.5 collective-permute-start.23
  62.3 1.5 %collective-permute-start.21 = (bf16[2,2,128,256]{3,2,1,0:T(8,128)(2,1)S(1)}, bf16[2,2,128,256]{3,2,1,0:T(8,128)(2,1)S(1)}, u32[]{:S(2)}, u32[]{:S(2)}) collective-permute-start(bf16[2,2,128,256]{3,2,1,0:T(8,128)(2,1)S(1)} %collective-permute-done.14.refs_3_), channel_id=1, source_target_pairs={{0,2},{2,0},{4,6},{6,4},{8,10},{10,8},{12,14},{14,12},{1,3},{3,1},... | collective-permute-start | bytes 786440 | tf_op jit(solution)/shard_map/ppermute | solution.py:325
  63.8 0.6 collective-permute-start.26
  64.5 0.1 collective-permute-start.19
  64.6 2.6 %collective-permute-done.24.refs_5_ = bf16[2,2,128,256]{3,2,1,0:T(8,128)(2,1)S(1)} collective-permute-done((bf16[2,2,128,256]{3,2,1,0:T(8,128)(2,1)S(1)}, bf16[2,2,128,256]{3,2,1,0:T(8,128)(2,1)S(1)}, u32[]{:S(2)}, u32[]{:S(2)}) %collective-permute-start.24) | collective-permute-done | bytes 262176 | tf_op jit(solution)/shard_map/ppermute | solution.py:325
  67.2 3.6 %collective-permute-done.23.refs_2_ = bf16[2,2,128,256]{3,2,1,0:T(8,128)(2,1)S(1)} collective-permute-done((bf16[2,2,128,256]{3,2,1,0:T(8,128)(2,1)}, bf16[2,2,128,256]{3,2,1,0:T(8,128)(2,1)S(1)}, u32[]{:S(2)}, u32[]{:S(2)}) %collective-permute-start.23) | collective-permute-done | bytes 262176 | tf_op jit(solution)/shard_map/ppermute | solution.py:325
  70.8 0.1 slice_bitcast_fusion
  70.9 0.4 collective-permute-start.25
  71.3 0.9 %collective-permute-done.18.refs_4_ = bf16[2,2,3,32,256]{4,3,2,1,0:T(8,128)(2,1)S(1)} collective-permute-done((bf16[2,2,3,32,256]{4,3,2,1,0:T(8,128)(2,1)S(1)}, bf16[2,2,3,32,256]{4,3,2,1,0:T(8,128)(2,1)S(1)}, u32[]{:S(2)}, u32[]{:S(2)}) %collective-permute-start.18) | collective-permute-done | bytes 196640 | tf_op jit(solution)/shard_map/ppermute | solution.py:325
  72.2 1.1 %prepare.1 = (bf16[2,768,512]{2,1,0:T(8,128)(2,1)S(1)}, bf16[2,3,512,256]{3,2,1,0:T(8,128)(2,1)S(1)}) custom-call(s32[16]{0:T(128)S(1)} %stack.31.place, bf16[2,2,3,32,256]{4,3,2,1,0:T(8,128)(2,1)S(1)} %get-tuple-element.66.refs_0_, bf16[2,2,3,32,256]{4,3,2,1,0:T(8,128)(2,1)S(1)} %get-tuple-element.70.refs_1_, ...), custom_call_target="tpu_custom_call" | custom-call | bytes 3145728 | tf_op jit(solution)/shard_map/prepare/pallas_call | solution.py:230
  73.4 6.5 %dress.2.refs_8_ = bf16[4,3,2,128,1024]{4,3,2,1,0:T(8,128)(2,1)} custom-call(s32[16]{0:T(128)S(1)} %stack.31.place, s32[2]{0:T(128)S(1)} %get-tuple-element.94.other_src, s32[2]{0:T(128)S(1)} %get-tuple-element.93.other_snk, bf16[2,768,512]{2,1,0:T(8,128)(2,1)S(1)} %get-tuple-element.78.left, bf16[2,3,512,256]{3,2,1,0:T(8,128)(2,1)S(1)} %get-tuple-element.79.sink, ...), custom_call_target="tpu_custom_call" | custom-call | flops 3221225472 | bytes 2097152 | tf_op jit(solution)/shard_map/dress/pallas_call | solution.py:290
  79.9 5.6 %dress.3 = bf16[4,3,2,128,1024]{4,3,2,1,0:T(8,128)(2,1)} custom-call(s32[16]{0:T(128)S(1)} %stack.31.place, s32[2]{0:T(128)S(1)} %get-tuple-element.96.other_src, s32[2]{0:T(128)S(1)} %get-tuple-element.95.other_snk, bf16[2,768,512]{2,1,0:T(8,128)(2,1)S(1)} %get-tuple-element.78.left, ...), custom_call_target="tpu_custom_call", output_to_operand_aliasing={{}: (13, {})} | custom-call | flops 3221225472 | bytes 2097152 | tf_op jit(solution)/shard_map/dress/pallas_call | solution.py:290
  (39 shorter events, 0.2 us)
Async XLA Ops:
  0.0 9.1 %copy-start = (bf16[4,2,128,1024]{3,2,1,0:T(8,128)(2,1)S(1)}, bf16[4,2,128,1024]{3,2,1,0:T(8,128)(2,1)}, u32[]{:S(2)}) copy-start(bf16[4,2,128,1024]{3,2,1,0:T(8,128)(2,1)} %panels.1) | copy-start | bytes 6291460
  1.0 1.1 %copy-start.1 = (bf16[1,2,3,192,256]{4,3,2,1,0:T(8,128)(2,1)S(1)}, bf16[1,2,3,192,256]{4,3,2,1,0:T(8,128)(2,1)}, u32[]{:S(2)}) copy-start(bf16[1,2,3,192,256]{4,3,2,1,0:T(8,128)(2,1)} %param.4) | copy-start | bytes 1769476
  4.5 9.3 %collective-permute-start = (bf16[3,128,256]{2,1,0:T(8,128)(2,1)S(1)}, bf16[3,128,256]{2,1,0:T(8,128)(2,1)S(1)}, u32[]{:S(2)}, u32[]{:S(2)}) collective-permute-start(bf16[3,128,256]{2,1,0:T(8,128)(2,1)S(1)} %get-tuple-element.51), channel_id=1, source_target_pairs={{0,2},{2,0},{4,6},{6,4},{8,10},{10,8},{12,14},{14,12},{1,3},{3,1},... | collective-permute-start | bytes 589832 | tf_op jit(solution)/shard_map/ppermute | solution.py:325
  7.5 6.4 %collective-permute-start.1 = (bf16[3,128,256]{2,1,0:T(8,128)(2,1)S(1)}, bf16[3,128,256]{2,1,0:T(8,128)(2,1)S(1)}, u32[]{:S(2)}, u32[]{:S(2)}) collective-permute-start(bf16[3,128,256]{2,1,0:T(8,128)(2,1)S(1)} %get-tuple-element.52), channel_id=1, source_target_pairs={{0,4},{2,6},{4,0},{6,2},{8,12},{10,14},{12,8},{14,10},{1,5},{3,7},... | collective-permute-start | bytes 589832 | tf_op jit(solution)/shard_map/ppermute | solution.py:325
  10.7 53.8 %copy-start.8 = (s32[4,2]{0,1:T(2,128)S(1)}, s32[4,2]{0,1:T(2,128)}, u32[]{:S(2)}) copy-start(s32[4,2]{0,1:T(2,128)} %param.6) | copy-start | bytes 100
  10.7 11.9 %collective-permute-start.3 = (bf16[2,2,128,256]{3,2,1,0:T(8,128)(2,1)S(1)}, bf16[2,2,128,256]{3,2,1,0:T(8,128)(2,1)S(1)}, u32[]{:S(2)}, u32[]{:S(2)}) collective-permute-start(bf16[2,2,128,256]{3,2,1,0:T(8,128)(2,1)S(1)} %get-tuple-element.56), channel_id=1, source_target_pairs={{0,12},{2,14},{4,8},{6,10},{8,4},{10,6},{12,0},{14,2},{1,13},{3,15... | collective-permute-start | bytes 786440 | tf_op jit(solution)/shard_map/ppermute | solution.py:325
  13.3 17.2 %collective-permute-start.6 = (bf16[2,2,128,256]{3,2,1,0:T(8,128)(2,1)S(1)}, bf16[2,2,128,256]{3,2,1,0:T(8,128)(2,1)S(1)}, u32[]{:S(2)}, u32[]{:S(2)}) collective-permute-start(bf16[2,2,128,256]{3,2,1,0:T(8,128)(2,1)S(1)} %get-tuple-element.61.refs_0_), channel_id=1, source_target_pairs={{0,2},{2,0},{4,6},{6,4},{8,10},{10,8},{12,14},{14,12},{1,3},{3,1},... | collective-permute-start | bytes 786440 | tf_op jit(solution)/shard_map/ppermute | solution.py:325
  14.5 8.4 %collective-permute-start.2 = (bf16[3,64,256]{2,1,0:T(8,128)(2,1)S(1)}, bf16[3,64,256]{2,1,0:T(8,128)(2,1)S(1)}, u32[]{:S(2)}, u32[]{:S(2)}) collective-permute-start(bf16[3,64,256]{2,1,0:T(8,128)(2,1)S(1)} %get-tuple-element.55), channel_id=1, source_target_pairs={{0,4},{2,6},{4,0},{6,2},{8,12},{10,14},{12,8},{14,10},{1,5},{3,7},... | collective-permute-start | bytes 294920 | tf_op jit(solution)/shard_map/ppermute | solution.py:325
  16.3 6.6 %collective-permute-start.4 = (bf16[3,64,256]{2,1,0:T(8,128)(2,1)S(1)}, bf16[3,64,256]{2,1,0:T(8,128)(2,1)S(1)}, u32[]{:S(2)}, u32[]{:S(2)}) collective-permute-start(bf16[3,64,256]{2,1,0:T(8,128)(2,1)S(1)} %get-tuple-element.58), channel_id=1, source_target_pairs={{0,2},{2,0},{4,6},{6,4},{8,10},{10,8},{12,14},{14,12},{1,3},{3,1},... | collective-permute-start | bytes 294920 | tf_op jit(solution)/shard_map/ppermute | solution.py:325
  23.5 8.4 %collective-permute-start.5 = (bf16[3,32,512]{2,1,0:T(8,128)(2,1)S(1)}, bf16[3,32,512]{2,1,0:T(8,128)(2,1)S(1)}, u32[]{:S(2)}, u32[]{:S(2)}) collective-permute-start(bf16[3,32,512]{2,1,0:T(8,128)(2,1)S(1)} %get-tuple-element.60), channel_id=1, source_target_pairs={{0,8},{2,10},{4,12},{6,14},{8,0},{10,2},{12,4},{14,6},{1,9},{3,11}... | collective-permute-start | bytes 294920 | tf_op jit(solution)/shard_map/ppermute | solution.py:325
  28.3 8.8 %collective-permute-start.9 = (bf16[2,2,128,256]{3,2,1,0:T(8,128)(2,1)S(1)}, bf16[2,2,128,256]{3,2,1,0:T(8,128)(2,1)S(1)}, u32[]{:S(2)}, u32[]{:S(2)}) collective-permute-start(bf16[2,2,128,256]{3,2,1,0:T(8,128)(2,1)S(1)} %get-tuple-element.64), channel_id=1, source_target_pairs={{0,4},{2,6},{4,0},{6,2},{8,12},{10,14},{12,8},{14,10},{1,5},{3,7},... | collective-permute-start | bytes 786440 | tf_op jit(solution)/shard_map/ppermute | solution.py:325
  28.4 8.7 %collective-permute-start.8 = (bf16[2,2,128,256]{3,2,1,0:T(8,128)(2,1)S(1)}, bf16[2,2,128,256]{3,2,1,0:T(8,128)(2,1)S(1)}, u32[]{:S(2)}, u32[]{:S(2)}) collective-permute-start(bf16[2,2,128,256]{3,2,1,0:T(8,128)(2,1)S(1)} %get-tuple-element.63.refs_0_), channel_id=1, source_target_pairs={{0,2},{2,0},{4,6},{6,4},{8,10},{10,8},{12,14},{14,12},{1,3},{3,1},... | collective-permute-start | bytes 786440 | tf_op jit(solution)/shard_map/ppermute | solution.py:325
  28.9 16.8 %collective-permute-start.11 = (bf16[2,2,128,256]{3,2,1,0:T(8,128)(2,1)S(1)}, bf16[2,2,128,256]{3,2,1,0:T(8,128)(2,1)S(1)}, u32[]{:S(2)}, u32[]{:S(2)}) collective-permute-start(bf16[2,2,128,256]{3,2,1,0:T(8,128)(2,1)S(1)} %collective-permute-done.3.refs_3_), channel_id=1, source_target_pairs={{0,2},{2,0},{4,6},{6,4},{8,10},{10,8},{12,14},{14,12},{1,3},{3,1},... | collective-permute-start | bytes 786440 | tf_op jit(solution)/shard_map/ppermute | solution.py:325
  31.9 11.7 %collective-permute-start.7 = (bf16[1,3,32,512]{3,2,1,0:T(8,128)(2,1)S(1)}, bf16[1,3,32,512]{3,2,1,0:T(8,128)(2,1)S(1)}, u32[]{:S(2)}, u32[]{:S(2)}) collective-permute-start(bf16[1,3,32,512]{3,2,1,0:T(8,128)(2,1)S(1)} %fusion.field), channel_id=1, source_target_pairs={{0,8},{2,10},{4,12},{6,14},{8,0},{10,2},{12,4},{14,6},{1,9},{3,11}... | collective-permute-start | bytes 294920 | tf_op jit(solution)/shard_map/ppermute | solution.py:325
  35.1 18.1 %collective-permute-start.14 = (bf16[2,2,128,256]{3,2,1,0:T(8,128)(2,1)S(1)}, bf16[2,2,128,256]{3,2,1,0:T(8,128)(2,1)S(1)}, u32[]{:S(2)}, u32[]{:S(2)}) collective-permute-start(bf16[2,2,128,256]{3,2,1,0:T(8,128)(2,1)S(1)} %get-tuple-element.72), channel_id=1, source_target_pairs={{0,12},{2,14},{4,8},{6,10},{8,4},{10,6},{12,0},{14,2},{1,13},{3,15... | collective-permute-start | bytes 786440 | tf_op jit(solution)/shard_map/ppermute | solution.py:325
  37.1 25.2 %copy-start.2 = (bf16[2,2,128,256]{3,2,1,0:T(8,128)(2,1)}, bf16[2,2,128,256]{3,2,1,0:T(8,128)(2,1)S(1)}, u32[]{:S(2)}) copy-start(bf16[2,2,128,256]{3,2,1,0:T(8,128)(2,1)S(1)} %collective-permute-done.9.refs_1_) | copy-start | bytes 786436
  43.7 6.7 %collective-permute-start.10 = (bf16[2,3,32,256]{3,2,1,0:T(8,128)(2,1)S(1)}, bf16[2,3,32,256]{3,2,1,0:T(8,128)(2,1)S(1)}, u32[]{:S(2)}, u32[]{:S(2)}) collective-permute-start(bf16[2,3,32,256]{3,2,1,0:T(8,128)(2,1)S(1)} %get-tuple-element.67.own_a), channel_id=1, source_target_pairs={{0,4},{2,6},{4,0},{6,2},{8,12},{10,14},{12,8},{14,10},{1,5},{3,7},... | collective-permute-start | bytes 294920 | tf_op jit(solution)/shard_map/ppermute | solution.py:325
  43.8 14.2 %collective-permute-start.22 = (bf16[2,2,128,256]{3,2,1,0:T(8,128)(2,1)S(1)}, bf16[2,2,128,256]{3,2,1,0:T(8,128)(2,1)S(1)}, u32[]{:S(2)}, u32[]{:S(2)}) collective-permute-start(bf16[2,2,128,256]{3,2,1,0:T(8,128)(2,1)S(1)} %get-tuple-element.76), channel_id=1, source_target_pairs={{0,4},{2,6},{4,0},{6,2},{8,12},{10,14},{12,8},{14,10},{1,5},{3,7},... | collective-permute-start | bytes 786440 | tf_op jit(solution)/shard_map/ppermute | solution.py:325
  45.8 15.3 %collective-permute-start.20 = (bf16[2,2,128,256]{3,2,1,0:T(8,128)(2,1)S(1)}, bf16[2,2,128,256]{3,2,1,0:T(8,128)(2,1)S(1)}, u32[]{:S(2)}, u32[]{:S(2)}) collective-permute-start(bf16[2,2,128,256]{3,2,1,0:T(8,128)(2,1)S(1)} %get-tuple-element.75), channel_id=1, source_target_pairs={{0,8},{2,10},{4,12},{6,14},{8,0},{10,2},{12,4},{14,6},{1,9},{3,11}... | collective-permute-start | bytes 786440 | tf_op jit(solution)/shard_map/ppermute | solution.py:325
  45.8 8.1 %copy-start.4 = (bf16[2,2,128,256]{3,2,1,0:T(8,128)(2,1)}, bf16[2,2,128,256]{3,2,1,0:T(8,128)(2,1)S(1)}, u32[]{:S(2)}) copy-start(bf16[2,2,128,256]{3,2,1,0:T(8,128)(2,1)S(1)} %collective-permute-done.11.refs_7_) | copy-start | bytes 786436
  45.8 5.2 %collective-permute-start.12 = (bf16[2,3,32,256]{3,2,1,0:T(8,128)(2,1)S(1)}, bf16[2,3,32,256]{3,2,1,0:T(8,128)(2,1)S(1)}, u32[]{:S(2)}, u32[]{:S(2)}) collective-permute-start(bf16[2,3,32,256]{3,2,1,0:T(8,128)(2,1)S(1)} %get-tuple-element.68.own_b), channel_id=1, source_target_pairs={{0,2},{2,0},{4,6},{6,4},{8,10},{10,8},{12,14},{14,12},{1,3},{3,1},... | collective-permute-start | bytes 294920 | tf_op jit(solution)/shard_map/ppermute | solution.py:325
  50.4 11.9 %collective-permute-start.15 = (bf16[2,2,128,256]{3,2,1,0:T(8,128)(2,1)S(1)}, bf16[2,2,128,256]{3,2,1,0:T(8,128)(2,1)}, u32[]{:S(2)}, u32[]{:S(2)}) collective-permute-start(bf16[2,2,128,256]{3,2,1,0:T(8,128)(2,1)S(1)} %collective-permute-done.9.refs_1_), channel_id=1, source_target_pairs={{0,2},{2,0},{4,6},{6,4},{8,10},{10,8},{12,14},{14,12},{1,3},{3,1},... | collective-permute-start | bytes 786440 | tf_op jit(solution)/shard_map/ppermute | solution.py:325
  51.7 12.1 %collective-permute-start.13 = (bf16[4,3,32,256]{3,2,1,0:T(8,128)(2,1)}, bf16[4,3,32,256]{3,2,1,0:T(8,128)(2,1)S(1)}, u32[]{:S(2)}, u32[]{:S(2)}) collective-permute-start(bf16[4,3,32,256]{3,2,1,0:T(8,128)(2,1)} %get-tuple-element.71), channel_id=1, source_target_pairs={{0,2},{2,0},{4,6},{6,4},{8,10},{10,8},{12,14},{14,12},{1,3},{3,1},... | collective-permute-start | bytes 589832 | tf_op jit(solution)/shard_map/ppermute | solution.py:325
  53.2 11.2 %collective-permute-start.16 = (bf16[4,3,32,256]{3,2,1,0:T(8,128)(2,1)}, bf16[4,3,32,256]{3,2,1,0:T(8,128)(2,1)S(1)}, u32[]{:S(2)}, u32[]{:S(2)}) collective-permute-start(bf16[4,3,32,256]{3,2,1,0:T(8,128)(2,1)} %get-tuple-element.74), channel_id=1, source_target_pairs={{0,4},{2,6},{4,0},{6,2},{8,12},{10,14},{12,8},{14,10},{1,5},{3,7},... | collective-permute-start | bytes 589832 | tf_op jit(solution)/shard_map/ppermute | solution.py:325
  57.9 9.2 %collective-permute-start.24 = (bf16[2,2,128,256]{3,2,1,0:T(8,128)(2,1)S(1)}, bf16[2,2,128,256]{3,2,1,0:T(8,128)(2,1)S(1)}, u32[]{:S(2)}, u32[]{:S(2)}) collective-permute-start(bf16[2,2,128,256]{3,2,1,0:T(8,128)(2,1)S(1)} %collective-permute-done.22.refs_1_), channel_id=1, source_target_pairs={{0,2},{2,0},{4,6},{6,4},{8,10},{10,8},{12,14},{14,12},{1,3},{3,1},... | collective-permute-start | bytes 786440 | tf_op jit(solution)/shard_map/ppermute | solution.py:325
  61.1 0.7 copy-start.6
  61.8 9.0 %collective-permute-start.23 = (bf16[2,2,128,256]{3,2,1,0:T(8,128)(2,1)}, bf16[2,2,128,256]{3,2,1,0:T(8,128)(2,1)S(1)}, u32[]{:S(2)}, u32[]{:S(2)}) collective-permute-start(bf16[2,2,128,256]{3,2,1,0:T(8,128)(2,1)} %get-tuple-element.82), channel_id=1, source_target_pairs={{0,8},{2,10},{4,12},{6,14},{8,0},{10,2},{12,4},{14,6},{1,9},{3,11}... | collective-permute-start | bytes 786440 | tf_op jit(solution)/shard_map/ppermute | solution.py:325
  62.3 11.0 %copy-start.5 = (bf16[2,2,128,256]{3,2,1,0:T(8,128)(2,1)S(1)}, bf16[2,2,128,256]{3,2,1,0:T(8,128)(2,1)}, u32[]{:S(2)}) copy-start(bf16[2,2,128,256]{3,2,1,0:T(8,128)(2,1)} %copy-done.4) | copy-start | bytes 786436
  62.3 11.0 %copy-start.7 = (bf16[2,2,128,256]{3,2,1,0:T(8,128)(2,1)S(1)}, bf16[2,2,128,256]{3,2,1,0:T(8,128)(2,1)}, u32[]{:S(2)}) copy-start(bf16[2,2,128,256]{3,2,1,0:T(8,128)(2,1)} %copy-done.6) | copy-start | bytes 786436
  62.3 11.0 %copy-start.3 = (bf16[2,2,128,256]{3,2,1,0:T(8,128)(2,1)S(1)}, bf16[2,2,128,256]{3,2,1,0:T(8,128)(2,1)}, u32[]{:S(2)}) copy-start(bf16[2,2,128,256]{3,2,1,0:T(8,128)(2,1)} %copy-done.2) | copy-start | bytes 786436
  62.3 8.5 %collective-permute-start.21 = (bf16[2,2,128,256]{3,2,1,0:T(8,128)(2,1)S(1)}, bf16[2,2,128,256]{3,2,1,0:T(8,128)(2,1)S(1)}, u32[]{:S(2)}, u32[]{:S(2)}) collective-permute-start(bf16[2,2,128,256]{3,2,1,0:T(8,128)(2,1)S(1)} %collective-permute-done.14.refs_3_), channel_id=1, source_target_pairs={{0,2},{2,0},{4,6},{6,4},{8,10},{10,8},{12,14},{14,12},{1,3},{3,1},... | collective-permute-start | bytes 786440 | tf_op jit(solution)/shard_map/ppermute | solution.py:325
  63.8 9.5 %collective-permute-start.26 = (bf16[2,2,128,256]{3,2,1,0:T(8,128)(2,1)}, bf16[2,2,128,256]{3,2,1,0:T(8,128)(2,1)S(1)}, u32[]{:S(2)}, u32[]{:S(2)}) collective-permute-start(bf16[2,2,128,256]{3,2,1,0:T(8,128)(2,1)} %copy-done.6), channel_id=1, source_target_pairs={{0,2},{2,0},{4,6},{6,4},{8,10},{10,8},{12,14},{14,12},{1,3},{3,1},... | collective-permute-start | bytes 786440 | tf_op jit(solution)/shard_map/ppermute | solution.py:325
  64.5 6.9 %collective-permute-start.19 = (bf16[2,4,3,32,256]{4,3,2,1,0:T(8,128)(2,1)S(1)}, bf16[2,4,3,32,256]{4,3,2,1,0:T(8,128)(2,1)S(1)}, u32[]{:S(2)}, u32[]{:S(2)}) collective-permute-start(bf16[2,4,3,32,256]{4,3,2,1,0:T(8,128)(2,1)S(1)} %gather.5.refs_2_), channel_id=1, source_target_pairs={{0,1},{1,0},{2,3},{3,2},{4,5},{5,4},{6,7},{7,6},{8,9},{9,8},{10,11... | collective-permute-start | bytes 1179656 | tf_op jit(solution)/shard_map/ppermute | solution.py:325
  67.2 4.2 %collective-permute-start.17 = (bf16[2,2,3,32,256]{4,3,2,1,0:T(8,128)(2,1)S(1)}, bf16[2,2,3,32,256]{4,3,2,1,0:T(8,128)(2,1)S(1)}, u32[]{:S(2)}, u32[]{:S(2)}) collective-permute-start(bf16[2,2,3,32,256]{4,3,2,1,0:T(8,128)(2,1)S(1)} %get-tuple-element.66.refs_0_), channel_id=1, source_target_pairs={{0,1},{1,0},{2,3},{3,2},{4,5},{5,4},{6,7},{7,6},{8,9},{9,8},{10,11... | collective-permute-start | bytes 589832 | tf_op jit(solution)/shard_map/ppermute | solution.py:325
  70.8 1.4 %collective-permute-start.18 = (bf16[2,2,3,32,256]{4,3,2,1,0:T(8,128)(2,1)S(1)}, bf16[2,2,3,32,256]{4,3,2,1,0:T(8,128)(2,1)S(1)}, u32[]{:S(2)}, u32[]{:S(2)}) collective-permute-start(bf16[2,2,3,32,256]{4,3,2,1,0:T(8,128)(2,1)S(1)} %get-tuple-element.70.refs_1_), channel_id=1, source_target_pairs={{0,1},{1,0},{2,3},{3,2},{4,5},{5,4},{6,7},{7,6},{8,9},{9,8},{10,11... | collective-permute-start | bytes 589832 | tf_op jit(solution)/shard_map/ppermute | solution.py:325
  70.9 9.0 %collective-permute-start.25 = (bf16[2,2,128,256]{3,2,1,0:T(8,128)(2,1)S(1)}, bf16[2,2,128,256]{3,2,1,0:T(8,128)(2,1)S(1)}, u32[]{:S(2)}, u32[]{:S(2)}) collective-permute-start(bf16[2,2,128,256]{3,2,1,0:T(8,128)(2,1)S(1)} %collective-permute-done.23.refs_2_), channel_id=1, source_target_pairs={{0,2},{2,0},{4,6},{6,4},{8,10},{10,8},{12,14},{14,12},{1,3},{3,1},... | collective-permute-start | bytes 786440 | tf_op jit(solution)/shard_map/ppermute | solution.py:325

commit v7 on v6

--- a/solution.py
+++ b/solution.py
@@ -313,8 +313,8 @@
     [("x", 0, 0)],
     [("x", 0, 1), ("z", 1, 0)],
     [("x", 3, 0)],
-    [("z", 3, 1), ("x", 1, 0)],
-    [("z", 2, 0), ("x", 3, 1), ("z", 1, 1)],
+    [("z", 3, 1), ("x", 1, 0), ("z", 1, 1)],
+    [("z", 2, 0), ("x", 3, 1)],
 ]
 CALLS = ((0, 2), (2, 2))
 AFTER = {("x", 2, 1): [("x", 1, 1)]}

time: 85.6 us -> 85.6 us (level)
  no operation moved by 1% of the time
where the time goes in v7:
time: 85.6 us; the launch traced here: 85.4 us
  waiting for transfers between devices  34.1 us (40%)
  starting transfers between devices  29.1 us (34%)
  Pallas kernels  19.2 us (22%)
  local copies, waits for them, and re-layouts  2.86 us (3%)
    ppermute x27, waiting for transfers between devices, exchange(): lax.ppermute(value, axis, [(i, i ^ mask) for i in range(lax.axis_size(axi...  34.1 us
    ppermute x27, starting transfers between devices, exchange(): lax.ppermute(value, axis, [(i, i ^ mask) for i in range(lax.axis_size(axi...  29.1 us
    pallas_call x2, Pallas kernels, dress(): pl.pallas_call(functools.partial(dress_kernel, count, chained), out_shape...  12 us
    pallas_call x1, Pallas kernels, gram_halves(): pl.pallas_call(functools.partial(gram_kernel, factor), out_shape=[jax.Sha...  2.39 us
    unnamed x18, local copies, waits for them, and re-layouts  1.79 us
  transfers between devices with their start and end apart: 27, of which 11 were waited for; matrix products, arithmetic and copies ran while one was open for 0% of the time, Pallas kernels for 13%

profile of v7, /device:TPU:0, one launch (start us, length us, event | category | flops | bytes accessed | tf_op | source)
XLA Modules:
  0.0 85.4 jit_solution(11985241341204631610)
XLA Ops:
  0.0 0.9 %reshape.7 = s32[9]{0:T(128)S(1)} reshape(s32[3,3]{1,0:T(4,128)} %param.5) | data formatting | bytes 72 | tf_op jit(solution)/shard_map/reshape | solution.py:339
  0.9 0.1 stack.31.place
  1.0 1.1 %copy-done.1 = bf16[1,2,3,192,256]{4,3,2,1,0:T(8,128)(2,1)S(1)} copy-done((bf16[1,2,3,192,256]{4,3,2,1,0:T(8,128)(2,1)S(1)}, bf16[1,2,3,192,256]{4,3,2,1,0:T(8,128)(2,1)}, u32[]{:S(2)}) %copy-start.1) | copy-done | bytes 589848
  2.1 2.4 %gram.1 = (bf16[3,128,256]{2,1,0:T(8,128)(2,1)S(1)}, bf16[3,128,256]{2,1,0:T(8,128)(2,1)S(1)}, f32[3,128,256]{2,1,0:T(8,128)S(1)}, f32[3,128,256]{2,1,0:T(8,128)S(1)}) custom-call(s32[16]{0:T(128)S(1)} %stack.31.place, bf16[2,3,192,256]{3,2,1,0:T(8,128)(2,1)S(1)} %bitcast.18), custom_call_target="tpu_custom_call" | custom-call | flops 905969664 | bytes 3145728 | tf_op jit(solution)/shard_map/gram/pallas_call | solution.py:70
  4.5 3.0 %collective-permute-start = (bf16[3,128,256]{2,1,0:T(8,128)(2,1)S(1)}, bf16[3,128,256]{2,1,0:T(8,128)(2,1)S(1)}, u32[]{:S(2)}, u32[]{:S(2)}) collective-permute-start(bf16[3,128,256]{2,1,0:T(8,128)(2,1)S(1)} %get-tuple-element.51), channel_id=1, source_target_pairs={{0,2},{2,0},{4,6},{6,4},{8,10},{10,8},{12,14},{14,12},{1,3},{3,1},... | collective-permute-start | bytes 589832 | tf_op jit(solution)/shard_map/ppermute | solution.py:325
  7.5 1.6 %collective-permute-start.1 = (bf16[3,128,256]{2,1,0:T(8,128)(2,1)S(1)}, bf16[3,128,256]{2,1,0:T(8,128)(2,1)S(1)}, u32[]{:S(2)}, u32[]{:S(2)}) collective-permute-start(bf16[3,128,256]{2,1,0:T(8,128)(2,1)S(1)} %get-tuple-element.52), channel_id=1, source_target_pairs={{0,4},{2,6},{4,0},{6,2},{8,12},{10,14},{12,8},{14,10},{1,5},{3,7},... | collective-permute-start | bytes 589832 | tf_op jit(solution)/shard_map/ppermute | solution.py:325
  9.1 1.7 %cut.1 = (bf16[2,2,128,256]{3,2,1,0:T(8,128)(2,1)S(1)}, bf16[2,2,128,256]{3,2,1,0:T(8,128)(2,1)S(1)}, bf16[2,2,128,256]{3,2,1,0:T(8,128)(2,1)S(1)}, bf16[2,2,128...) custom-call(s32[16]{0:T(128)S(1)} %stack.31.place, ...), custom_call_target="tpu_custom_call" | custom-call | bytes 4194304 | tf_op jit(solution)/shard_map/cut/pallas_call | solution.py:99
  10.7 2.5 %collective-permute-start.3 = (bf16[2,2,128,256]{3,2,1,0:T(8,128)(2,1)S(1)}, bf16[2,2,128,256]{3,2,1,0:T(8,128)(2,1)S(1)}, u32[]{:S(2)}, u32[]{:S(2)}) collective-permute-start(bf16[2,2,128,256]{3,2,1,0:T(8,128)(2,1)S(1)} %get-tuple-element.56), channel_id=1, source_target_pairs={{0,12},{2,14},{4,8},{6,10},{8,4},{10,6},{12,0},{14,2},{1,13},{3,15... | collective-permute-start | bytes 786440 | tf_op jit(solution)/shard_map/ppermute | solution.py:325
  13.3 0.5 collective-permute-start.6
  13.8 0.0 collective-permute-done.1.came_b
  13.8 0.6 fold.2
  14.5 1.8 %collective-permute-start.2 = (bf16[3,64,256]{2,1,0:T(8,128)(2,1)S(1)}, bf16[3,64,256]{2,1,0:T(8,128)(2,1)S(1)}, u32[]{:S(2)}, u32[]{:S(2)}) collective-permute-start(bf16[3,64,256]{2,1,0:T(8,128)(2,1)S(1)} %get-tuple-element.55), channel_id=1, source_target_pairs={{0,4},{2,6},{4,0},{6,2},{8,12},{10,14},{12,8},{14,10},{1,5},{3,7},... | collective-permute-start | bytes 294920 | tf_op jit(solution)/shard_map/ppermute | solution.py:325
  16.3 0.5 collective-permute-start.4
  16.8 5.8 %collective-permute-done.3.refs_3_ = bf16[2,2,128,256]{3,2,1,0:T(8,128)(2,1)S(1)} collective-permute-done((bf16[2,2,128,256]{3,2,1,0:T(8,128)(2,1)S(1)}, bf16[2,2,128,256]{3,2,1,0:T(8,128)(2,1)S(1)}, u32[]{:S(2)}, u32[]{:S(2)}) %collective-permute-start.3) | collective-permute-done | bytes 262176 | tf_op jit(solution)/shard_map/ppermute | solution.py:325
  22.6 0.3 collective-permute-done.2.came_a
  22.9 0.6 fold.3
  23.5 4.8 %collective-permute-start.5 = (bf16[3,32,512]{2,1,0:T(8,128)(2,1)S(1)}, bf16[3,32,512]{2,1,0:T(8,128)(2,1)S(1)}, u32[]{:S(2)}, u32[]{:S(2)}) collective-permute-start(bf16[3,32,512]{2,1,0:T(8,128)(2,1)S(1)} %get-tuple-element.60), channel_id=1, source_target_pairs={{0,8},{2,10},{4,12},{6,14},{8,0},{10,2},{12,4},{14,6},{1,9},{3,11}... | collective-permute-start | bytes 294920 | tf_op jit(solution)/shard_map/ppermute | solution.py:325
  28.3 0.1 collective-permute-start.9
  28.4 0.5 collective-permute-start.8
  28.9 1.5 %collective-permute-start.11 = (bf16[2,2,128,256]{3,2,1,0:T(8,128)(2,1)S(1)}, bf16[2,2,128,256]{3,2,1,0:T(8,128)(2,1)S(1)}, u32[]{:S(2)}, u32[]{:S(2)}) collective-permute-start(bf16[2,2,128,256]{3,2,1,0:T(8,128)(2,1)S(1)} %collective-permute-done.3.refs_3_), channel_id=1, source_target_pairs={{0,2},{2,0},{4,6},{6,4},{8,10},{10,8},{12,14},{14,12},{1,3},{3,1},... | collective-permute-start | bytes 786440 | tf_op jit(solution)/shard_map/ppermute | solution.py:325
  30.4 1.5 %collective-permute-done.5 = bf16[3,32,512]{2,1,0:T(8,128)(2,1)S(1)} collective-permute-done((bf16[3,32,512]{2,1,0:T(8,128)(2,1)S(1)}, bf16[3,32,512]{2,1,0:T(8,128)(2,1)S(1)}, u32[]{:S(2)}, u32[]{:S(2)}) %collective-permute-start.5) | collective-permute-done | bytes 98336 | tf_op jit(solution)/shard_map/ppermute | solution.py:325
  31.9 3.1 %collective-permute-start.7 = (bf16[1,3,32,512]{3,2,1,0:T(8,128)(2,1)S(1)}, bf16[1,3,32,512]{3,2,1,0:T(8,128)(2,1)S(1)}, u32[]{:S(2)}, u32[]{:S(2)}) collective-permute-start(bf16[1,3,32,512]{3,2,1,0:T(8,128)(2,1)S(1)} %fusion.field), channel_id=1, source_target_pairs={{0,8},{2,10},{4,12},{6,14},{8,0},{10,2},{12,4},{14,6},{1,9},{3,11}... | collective-permute-start | bytes 294920 | tf_op jit(solution)/shard_map/ppermute | solution.py:325
  35.1 2.1 %collective-permute-done.9.refs_1_ = bf16[2,2,128,256]{3,2,1,0:T(8,128)(2,1)S(1)} collective-permute-done((bf16[2,2,128,256]{3,2,1,0:T(8,128)(2,1)S(1)}, bf16[2,2,128,256]{3,2,1,0:T(8,128)(2,1)S(1)}, u32[]{:S(2)}, u32[]{:S(2)}) %collective-permute-start.9) | collective-permute-done | bytes 262176 | tf_op jit(solution)/shard_map/ppermute | solution.py:325
  37.1 6.5 %collective-permute-done.7.came = bf16[1,3,32,512]{3,2,1,0:T(8,128)(2,1)S(1)} collective-permute-done((bf16[1,3,32,512]{3,2,1,0:T(8,128)(2,1)S(1)}, bf16[1,3,32,512]{3,2,1,0:T(8,128)(2,1)S(1)}, u32[]{:S(2)}, u32[]{:S(2)}) %collective-permute-start.7) | collective-permute-done | bytes 98336 | tf_op jit(solution)/shard_map/ppermute | solution.py:325
  43.7 0.1 collective-permute-start.10
  43.8 2.0 %collective-permute-start.16 = (bf16[2,2,128,256]{3,2,1,0:T(8,128)(2,1)S(1)}, bf16[2,2,128,256]{3,2,1,0:T(8,128)(2,1)S(1)}, u32[]{:S(2)}, u32[]{:S(2)}) collective-permute-start(bf16[2,2,128,256]{3,2,1,0:T(8,128)(2,1)S(1)} %get-tuple-element.73), channel_id=1, source_target_pairs={{0,4},{2,6},{4,0},{6,2},{8,12},{10,14},{12,8},{14,10},{1,5},{3,7},... | collective-permute-start | bytes 786440 | tf_op jit(solution)/shard_map/ppermute | solution.py:325
  45.8 0.6 collective-permute-start.12
  46.4 4.0 %collective-permute-done.10.came_a = bf16[2,3,32,256]{3,2,1,0:T(8,128)(2,1)S(1)} collective-permute-done((bf16[2,3,32,256]{3,2,1,0:T(8,128)(2,1)S(1)}, bf16[2,3,32,256]{3,2,1,0:T(8,128)(2,1)S(1)}, u32[]{:S(2)}, u32[]{:S(2)}) %collective-permute-start.10) | collective-permute-done | bytes 98336 | tf_op jit(solution)/shard_map/ppermute | solution.py:325
  50.4 0.6 collective-permute-start.15
  51.0 0.8 gather.4
  51.7 1.4 %collective-permute-start.13 = (bf16[4,3,32,256]{3,2,1,0:T(8,128)(2,1)}, bf16[4,3,32,256]{3,2,1,0:T(8,128)(2,1)S(1)}, u32[]{:S(2)}, u32[]{:S(2)}) collective-permute-start(bf16[4,3,32,256]{3,2,1,0:T(8,128)(2,1)} %get-tuple-element.71), channel_id=1, source_target_pairs={{0,2},{2,0},{4,6},{6,4},{8,10},{10,8},{12,14},{14,12},{1,3},{3,1},... | collective-permute-start | bytes 589832 | tf_op jit(solution)/shard_map/ppermute | solution.py:325
  53.2 0.7 collective-permute-start.17
  53.9 4.0 %collective-permute-done.16.refs_1_ = bf16[2,2,128,256]{3,2,1,0:T(8,128)(2,1)S(1)} collective-permute-done((bf16[2,2,128,256]{3,2,1,0:T(8,128)(2,1)S(1)}, bf16[2,2,128,256]{3,2,1,0:T(8,128)(2,1)S(1)}, u32[]{:S(2)}, u32[]{:S(2)}) %collective-permute-start.16) | collective-permute-done | bytes 262176 | tf_op jit(solution)/shard_map/ppermute | solution.py:325
  57.9 0.5 collective-permute-start.24
  58.4 2.7 %collective-permute-done.21.refs_2_ = bf16[2,2,128,256]{3,2,1,0:T(8,128)(2,1)S(1)} collective-permute-done((bf16[2,2,128,256]{3,2,1,0:T(8,128)(2,1)S(1)}, bf16[2,2,128,256]{3,2,1,0:T(8,128)(2,1)S(1)}, u32[]{:S(2)}, u32[]{:S(2)}) %collective-permute-start.21) | collective-permute-done | bytes 262176 | tf_op jit(solution)/shard_map/ppermute | solution.py:325
  61.1 0.7 copy-done.6
  61.8 0.5 collective-permute-start.23
  62.3 1.5 %collective-permute-start.22 = (bf16[2,2,128,256]{3,2,1,0:T(8,128)(2,1)S(1)}, bf16[2,2,128,256]{3,2,1,0:T(8,128)(2,1)S(1)}, u32[]{:S(2)}, u32[]{:S(2)}) collective-permute-start(bf16[2,2,128,256]{3,2,1,0:T(8,128)(2,1)S(1)} %collective-permute-done.14.refs_3_), channel_id=1, source_target_pairs={{0,2},{2,0},{4,6},{6,4},{8,10},{10,8},{12,14},{14,12},{1,3},{3,1},... | collective-permute-start | bytes 786440 | tf_op jit(solution)/shard_map/ppermute | solution.py:325
  63.8 0.6 collective-permute-start.26
  64.5 0.1 collective-permute-start.20
  64.6 2.6 %collective-permute-done.24.refs_5_ = bf16[2,2,128,256]{3,2,1,0:T(8,128)(2,1)S(1)} collective-permute-done((bf16[2,2,128,256]{3,2,1,0:T(8,128)(2,1)S(1)}, bf16[2,2,128,256]{3,2,1,0:T(8,128)(2,1)S(1)}, u32[]{:S(2)}, u32[]{:S(2)}) %collective-permute-start.24) | collective-permute-done | bytes 262176 | tf_op jit(solution)/shard_map/ppermute | solution.py:325
  67.2 3.6 %collective-permute-done.23.refs_2_ = bf16[2,2,128,256]{3,2,1,0:T(8,128)(2,1)S(1)} collective-permute-done((bf16[2,2,128,256]{3,2,1,0:T(8,128)(2,1)}, bf16[2,2,128,256]{3,2,1,0:T(8,128)(2,1)S(1)}, u32[]{:S(2)}, u32[]{:S(2)}) %collective-permute-start.23) | collective-permute-done | bytes 262176 | tf_op jit(solution)/shard_map/ppermute | solution.py:325
  70.8 0.1 slice_bitcast_fusion
  70.9 0.4 collective-permute-start.25
  71.3 0.9 %collective-permute-done.19.refs_4_ = bf16[2,2,3,32,256]{4,3,2,1,0:T(8,128)(2,1)S(1)} collective-permute-done((bf16[2,2,3,32,256]{4,3,2,1,0:T(8,128)(2,1)S(1)}, bf16[2,2,3,32,256]{4,3,2,1,0:T(8,128)(2,1)S(1)}, u32[]{:S(2)}, u32[]{:S(2)}) %collective-permute-start.19) | collective-permute-done | bytes 196640 | tf_op jit(solution)/shard_map/ppermute | solution.py:325
  72.2 1.1 %prepare.1 = (bf16[2,768,512]{2,1,0:T(8,128)(2,1)S(1)}, bf16[2,3,512,256]{3,2,1,0:T(8,128)(2,1)S(1)}) custom-call(s32[16]{0:T(128)S(1)} %stack.31.place, bf16[2,2,3,32,256]{4,3,2,1,0:T(8,128)(2,1)S(1)} %get-tuple-element.66.refs_0_, bf16[2,2,3,32,256]{4,3,2,1,0:T(8,128)(2,1)S(1)} %get-tuple-element.70.refs_1_, ...), custom_call_target="tpu_custom_call" | custom-call | bytes 3145728 | tf_op jit(solution)/shard_map/prepare/pallas_call | solution.py:230
  73.4 6.5 %dress.2.refs_8_ = bf16[4,3,2,128,1024]{4,3,2,1,0:T(8,128)(2,1)} custom-call(s32[16]{0:T(128)S(1)} %stack.31.place, s32[2]{0:T(128)S(1)} %get-tuple-element.94.other_src, s32[2]{0:T(128)S(1)} %get-tuple-element.93.other_snk, bf16[2,768,512]{2,1,0:T(8,128)(2,1)S(1)} %get-tuple-element.78.left, bf16[2,3,512,256]{3,2,1,0:T(8,128)(2,1)S(1)} %get-tuple-element.79.sink, ...), custom_call_target="tpu_custom_call" | custom-call | flops 3221225472 | bytes 2097152 | tf_op jit(solution)/shard_map/dress/pallas_call | solution.py:290
  79.9 5.6 %dress.3 = bf16[4,3,2,128,1024]{4,3,2,1,0:T(8,128)(2,1)} custom-call(s32[16]{0:T(128)S(1)} %stack.31.place, s32[2]{0:T(128)S(1)} %get-tuple-element.96.other_src, s32[2]{0:T(128)S(1)} %get-tuple-element.95.other_snk, bf16[2,768,512]{2,1,0:T(8,128)(2,1)S(1)} %get-tuple-element.78.left, ...), custom_call_target="tpu_custom_call", output_to_operand_aliasing={{}: (13, {})} | custom-call | flops 3221225472 | bytes 2097152 | tf_op jit(solution)/shard_map/dress/pallas_call | solution.py:290
  (39 shorter events, 0.2 us)
Async XLA Ops:
  0.0 9.1 %copy-start = (bf16[4,2,128,1024]{3,2,1,0:T(8,128)(2,1)S(1)}, bf16[4,2,128,1024]{3,2,1,0:T(8,128)(2,1)}, u32[]{:S(2)}) copy-start(bf16[4,2,128,1024]{3,2,1,0:T(8,128)(2,1)} %panels.1) | copy-start | bytes 6291460
  1.0 1.1 %copy-start.1 = (bf16[1,2,3,192,256]{4,3,2,1,0:T(8,128)(2,1)S(1)}, bf16[1,2,3,192,256]{4,3,2,1,0:T(8,128)(2,1)}, u32[]{:S(2)}) copy-start(bf16[1,2,3,192,256]{4,3,2,1,0:T(8,128)(2,1)} %param.4) | copy-start | bytes 1769476
  4.5 9.3 %collective-permute-start = (bf16[3,128,256]{2,1,0:T(8,128)(2,1)S(1)}, bf16[3,128,256]{2,1,0:T(8,128)(2,1)S(1)}, u32[]{:S(2)}, u32[]{:S(2)}) collective-permute-start(bf16[3,128,256]{2,1,0:T(8,128)(2,1)S(1)} %get-tuple-element.51), channel_id=1, source_target_pairs={{0,2},{2,0},{4,6},{6,4},{8,10},{10,8},{12,14},{14,12},{1,3},{3,1},... | collective-permute-start | bytes 589832 | tf_op jit(solution)/shard_map/ppermute | solution.py:325
  7.5 6.4 %collective-permute-start.1 = (bf16[3,128,256]{2,1,0:T(8,128)(2,1)S(1)}, bf16[3,128,256]{2,1,0:T(8,128)(2,1)S(1)}, u32[]{:S(2)}, u32[]{:S(2)}) collective-permute-start(bf16[3,128,256]{2,1,0:T(8,128)(2,1)S(1)} %get-tuple-element.52), channel_id=1, source_target_pairs={{0,4},{2,6},{4,0},{6,2},{8,12},{10,14},{12,8},{14,10},{1,5},{3,7},... | collective-permute-start | bytes 589832 | tf_op jit(solution)/shard_map/ppermute | solution.py:325
  10.7 53.8 %copy-start.8 = (s32[4,2]{0,1:T(2,128)S(1)}, s32[4,2]{0,1:T(2,128)}, u32[]{:S(2)}) copy-start(s32[4,2]{0,1:T(2,128)} %param.6) | copy-start | bytes 100
  10.7 11.9 %collective-permute-start.3 = (bf16[2,2,128,256]{3,2,1,0:T(8,128)(2,1)S(1)}, bf16[2,2,128,256]{3,2,1,0:T(8,128)(2,1)S(1)}, u32[]{:S(2)}, u32[]{:S(2)}) collective-permute-start(bf16[2,2,128,256]{3,2,1,0:T(8,128)(2,1)S(1)} %get-tuple-element.56), channel_id=1, source_target_pairs={{0,12},{2,14},{4,8},{6,10},{8,4},{10,6},{12,0},{14,2},{1,13},{3,15... | collective-permute-start | bytes 786440 | tf_op jit(solution)/shard_map/ppermute | solution.py:325
  13.3 17.2 %collective-permute-start.6 = (bf16[2,2,128,256]{3,2,1,0:T(8,128)(2,1)S(1)}, bf16[2,2,128,256]{3,2,1,0:T(8,128)(2,1)S(1)}, u32[]{:S(2)}, u32[]{:S(2)}) collective-permute-start(bf16[2,2,128,256]{3,2,1,0:T(8,128)(2,1)S(1)} %get-tuple-element.61.refs_0_), channel_id=1, source_target_pairs={{0,2},{2,0},{4,6},{6,4},{8,10},{10,8},{12,14},{14,12},{1,3},{3,1},... | collective-permute-start | bytes 786440 | tf_op jit(solution)/shard_map/ppermute | solution.py:325
  14.5 8.4 %collective-permute-start.2 = (bf16[3,64,256]{2,1,0:T(8,128)(2,1)S(1)}, bf16[3,64,256]{2,1,0:T(8,128)(2,1)S(1)}, u32[]{:S(2)}, u32[]{:S(2)}) collective-permute-start(bf16[3,64,256]{2,1,0:T(8,128)(2,1)S(1)} %get-tuple-element.55), channel_id=1, source_target_pairs={{0,4},{2,6},{4,0},{6,2},{8,12},{10,14},{12,8},{14,10},{1,5},{3,7},... | collective-permute-start | bytes 294920 | tf_op jit(solution)/shard_map/ppermute | solution.py:325
  16.3 6.6 %collective-permute-start.4 = (bf16[3,64,256]{2,1,0:T(8,128)(2,1)S(1)}, bf16[3,64,256]{2,1,0:T(8,128)(2,1)S(1)}, u32[]{:S(2)}, u32[]{:S(2)}) collective-permute-start(bf16[3,64,256]{2,1,0:T(8,128)(2,1)S(1)} %get-tuple-element.58), channel_id=1, source_target_pairs={{0,2},{2,0},{4,6},{6,4},{8,10},{10,8},{12,14},{14,12},{1,3},{3,1},... | collective-permute-start | bytes 294920 | tf_op jit(solution)/shard_map/ppermute | solution.py:325
  23.5 8.4 %collective-permute-start.5 = (bf16[3,32,512]{2,1,0:T(8,128)(2,1)S(1)}, bf16[3,32,512]{2,1,0:T(8,128)(2,1)S(1)}, u32[]{:S(2)}, u32[]{:S(2)}) collective-permute-start(bf16[3,32,512]{2,1,0:T(8,128)(2,1)S(1)} %get-tuple-element.60), channel_id=1, source_target_pairs={{0,8},{2,10},{4,12},{6,14},{8,0},{10,2},{12,4},{14,6},{1,9},{3,11}... | collective-permute-start | bytes 294920 | tf_op jit(solution)/shard_map/ppermute | solution.py:325
  28.3 8.8 %collective-permute-start.9 = (bf16[2,2,128,256]{3,2,1,0:T(8,128)(2,1)S(1)}, bf16[2,2,128,256]{3,2,1,0:T(8,128)(2,1)S(1)}, u32[]{:S(2)}, u32[]{:S(2)}) collective-permute-start(bf16[2,2,128,256]{3,2,1,0:T(8,128)(2,1)S(1)} %get-tuple-element.64), channel_id=1, source_target_pairs={{0,4},{2,6},{4,0},{6,2},{8,12},{10,14},{12,8},{14,10},{1,5},{3,7},... | collective-permute-start | bytes 786440 | tf_op jit(solution)/shard_map/ppermute | solution.py:325
  28.4 8.7 %collective-permute-start.8 = (bf16[2,2,128,256]{3,2,1,0:T(8,128)(2,1)S(1)}, bf16[2,2,128,256]{3,2,1,0:T(8,128)(2,1)S(1)}, u32[]{:S(2)}, u32[]{:S(2)}) collective-permute-start(bf16[2,2,128,256]{3,2,1,0:T(8,128)(2,1)S(1)} %get-tuple-element.63.refs_0_), channel_id=1, source_target_pairs={{0,2},{2,0},{4,6},{6,4},{8,10},{10,8},{12,14},{14,12},{1,3},{3,1},... | collective-permute-start | bytes 786440 | tf_op jit(solution)/shard_map/ppermute | solution.py:325
  28.9 16.8 %collective-permute-start.11 = (bf16[2,2,128,256]{3,2,1,0:T(8,128)(2,1)S(1)}, bf16[2,2,128,256]{3,2,1,0:T(8,128)(2,1)S(1)}, u32[]{:S(2)}, u32[]{:S(2)}) collective-permute-start(bf16[2,2,128,256]{3,2,1,0:T(8,128)(2,1)S(1)} %collective-permute-done.3.refs_3_), channel_id=1, source_target_pairs={{0,2},{2,0},{4,6},{6,4},{8,10},{10,8},{12,14},{14,12},{1,3},{3,1},... | collective-permute-start | bytes 786440 | tf_op jit(solution)/shard_map/ppermute | solution.py:325
  31.9 11.7 %collective-permute-start.7 = (bf16[1,3,32,512]{3,2,1,0:T(8,128)(2,1)S(1)}, bf16[1,3,32,512]{3,2,1,0:T(8,128)(2,1)S(1)}, u32[]{:S(2)}, u32[]{:S(2)}) collective-permute-start(bf16[1,3,32,512]{3,2,1,0:T(8,128)(2,1)S(1)} %fusion.field), channel_id=1, source_target_pairs={{0,8},{2,10},{4,12},{6,14},{8,0},{10,2},{12,4},{14,6},{1,9},{3,11}... | collective-permute-start | bytes 294920 | tf_op jit(solution)/shard_map/ppermute | solution.py:325
  35.1 18.1 %collective-permute-start.14 = (bf16[2,2,128,256]{3,2,1,0:T(8,128)(2,1)S(1)}, bf16[2,2,128,256]{3,2,1,0:T(8,128)(2,1)S(1)}, u32[]{:S(2)}, u32[]{:S(2)}) collective-permute-start(bf16[2,2,128,256]{3,2,1,0:T(8,128)(2,1)S(1)} %get-tuple-element.72), channel_id=1, source_target_pairs={{0,12},{2,14},{4,8},{6,10},{8,4},{10,6},{12,0},{14,2},{1,13},{3,15... | collective-permute-start | bytes 786440 | tf_op jit(solution)/shard_map/ppermute | solution.py:325
  37.1 25.2 %copy-start.2 = (bf16[2,2,128,256]{3,2,1,0:T(8,128)(2,1)}, bf16[2,2,128,256]{3,2,1,0:T(8,128)(2,1)S(1)}, u32[]{:S(2)}) copy-start(bf16[2,2,128,256]{3,2,1,0:T(8,128)(2,1)S(1)} %collective-permute-done.9.refs_1_) | copy-start | bytes 786436
  43.7 6.7 %collective-permute-start.10 = (bf16[2,3,32,256]{3,2,1,0:T(8,128)(2,1)S(1)}, bf16[2,3,32,256]{3,2,1,0:T(8,128)(2,1)S(1)}, u32[]{:S(2)}, u32[]{:S(2)}) collective-permute-start(bf16[2,3,32,256]{3,2,1,0:T(8,128)(2,1)S(1)} %get-tuple-element.67.own_a), channel_id=1, source_target_pairs={{0,4},{2,6},{4,0},{6,2},{8,12},{10,14},{12,8},{14,10},{1,5},{3,7},... | collective-permute-start | bytes 294920 | tf_op jit(solution)/shard_map/ppermute | solution.py:325
  43.8 14.2 %collective-permute-start.16 = (bf16[2,2,128,256]{3,2,1,0:T(8,128)(2,1)S(1)}, bf16[2,2,128,256]{3,2,1,0:T(8,128)(2,1)S(1)}, u32[]{:S(2)}, u32[]{:S(2)}) collective-permute-start(bf16[2,2,128,256]{3,2,1,0:T(8,128)(2,1)S(1)} %get-tuple-element.73), channel_id=1, source_target_pairs={{0,4},{2,6},{4,0},{6,2},{8,12},{10,14},{12,8},{14,10},{1,5},{3,7},... | collective-permute-start | bytes 786440 | tf_op jit(solution)/shard_map/ppermute | solution.py:325
  45.8 15.3 %collective-permute-start.21 = (bf16[2,2,128,256]{3,2,1,0:T(8,128)(2,1)S(1)}, bf16[2,2,128,256]{3,2,1,0:T(8,128)(2,1)S(1)}, u32[]{:S(2)}, u32[]{:S(2)}) collective-permute-start(bf16[2,2,128,256]{3,2,1,0:T(8,128)(2,1)S(1)} %get-tuple-element.76), channel_id=1, source_target_pairs={{0,8},{2,10},{4,12},{6,14},{8,0},{10,2},{12,4},{14,6},{1,9},{3,11}... | collective-permute-start | bytes 786440 | tf_op jit(solution)/shard_map/ppermute | solution.py:325
  45.8 8.1 %copy-start.4 = (bf16[2,2,128,256]{3,2,1,0:T(8,128)(2,1)}, bf16[2,2,128,256]{3,2,1,0:T(8,128)(2,1)S(1)}, u32[]{:S(2)}) copy-start(bf16[2,2,128,256]{3,2,1,0:T(8,128)(2,1)S(1)} %collective-permute-done.11.refs_7_) | copy-start | bytes 786436
  45.8 5.2 %collective-permute-start.12 = (bf16[2,3,32,256]{3,2,1,0:T(8,128)(2,1)S(1)}, bf16[2,3,32,256]{3,2,1,0:T(8,128)(2,1)S(1)}, u32[]{:S(2)}, u32[]{:S(2)}) collective-permute-start(bf16[2,3,32,256]{3,2,1,0:T(8,128)(2,1)S(1)} %get-tuple-element.68.own_b), channel_id=1, source_target_pairs={{0,2},{2,0},{4,6},{6,4},{8,10},{10,8},{12,14},{14,12},{1,3},{3,1},... | collective-permute-start | bytes 294920 | tf_op jit(solution)/shard_map/ppermute | solution.py:325
  50.4 11.9 %collective-permute-start.15 = (bf16[2,2,128,256]{3,2,1,0:T(8,128)(2,1)S(1)}, bf16[2,2,128,256]{3,2,1,0:T(8,128)(2,1)}, u32[]{:S(2)}, u32[]{:S(2)}) collective-permute-start(bf16[2,2,128,256]{3,2,1,0:T(8,128)(2,1)S(1)} %collective-permute-done.9.refs_1_), channel_id=1, source_target_pairs={{0,2},{2,0},{4,6},{6,4},{8,10},{10,8},{12,14},{14,12},{1,3},{3,1},... | collective-permute-start | bytes 786440 | tf_op jit(solution)/shard_map/ppermute | solution.py:325
  51.7 12.1 %collective-permute-start.13 = (bf16[4,3,32,256]{3,2,1,0:T(8,128)(2,1)}, bf16[4,3,32,256]{3,2,1,0:T(8,128)(2,1)S(1)}, u32[]{:S(2)}, u32[]{:S(2)}) collective-permute-start(bf16[4,3,32,256]{3,2,1,0:T(8,128)(2,1)} %get-tuple-element.71), channel_id=1, source_target_pairs={{0,2},{2,0},{4,6},{6,4},{8,10},{10,8},{12,14},{14,12},{1,3},{3,1},... | collective-permute-start | bytes 589832 | tf_op jit(solution)/shard_map/ppermute | solution.py:325
  53.2 11.2 %collective-permute-start.17 = (bf16[4,3,32,256]{3,2,1,0:T(8,128)(2,1)}, bf16[4,3,32,256]{3,2,1,0:T(8,128)(2,1)S(1)}, u32[]{:S(2)}, u32[]{:S(2)}) collective-permute-start(bf16[4,3,32,256]{3,2,1,0:T(8,128)(2,1)} %get-tuple-element.75), channel_id=1, source_target_pairs={{0,4},{2,6},{4,0},{6,2},{8,12},{10,14},{12,8},{14,10},{1,5},{3,7},... | collective-permute-start | bytes 589832 | tf_op jit(solution)/shard_map/ppermute | solution.py:325
  57.9 9.2 %collective-permute-start.24 = (bf16[2,2,128,256]{3,2,1,0:T(8,128)(2,1)S(1)}, bf16[2,2,128,256]{3,2,1,0:T(8,128)(2,1)S(1)}, u32[]{:S(2)}, u32[]{:S(2)}) collective-permute-start(bf16[2,2,128,256]{3,2,1,0:T(8,128)(2,1)S(1)} %collective-permute-done.16.refs_1_), channel_id=1, source_target_pairs={{0,2},{2,0},{4,6},{6,4},{8,10},{10,8},{12,14},{14,12},{1,3},{3,1},... | collective-permute-start | bytes 786440 | tf_op jit(solution)/shard_map/ppermute | solution.py:325
  61.1 0.7 copy-start.6
  61.8 9.0 %collective-permute-start.23 = (bf16[2,2,128,256]{3,2,1,0:T(8,128)(2,1)}, bf16[2,2,128,256]{3,2,1,0:T(8,128)(2,1)S(1)}, u32[]{:S(2)}, u32[]{:S(2)}) collective-permute-start(bf16[2,2,128,256]{3,2,1,0:T(8,128)(2,1)} %get-tuple-element.82), channel_id=1, source_target_pairs={{0,8},{2,10},{4,12},{6,14},{8,0},{10,2},{12,4},{14,6},{1,9},{3,11}... | collective-permute-start | bytes 786440 | tf_op jit(solution)/shard_map/ppermute | solution.py:325
  62.3 11.0 %copy-start.5 = (bf16[2,2,128,256]{3,2,1,0:T(8,128)(2,1)S(1)}, bf16[2,2,128,256]{3,2,1,0:T(8,128)(2,1)}, u32[]{:S(2)}) copy-start(bf16[2,2,128,256]{3,2,1,0:T(8,128)(2,1)} %copy-done.4) | copy-start | bytes 786436
  62.3 11.0 %copy-start.7 = (bf16[2,2,128,256]{3,2,1,0:T(8,128)(2,1)S(1)}, bf16[2,2,128,256]{3,2,1,0:T(8,128)(2,1)}, u32[]{:S(2)}) copy-start(bf16[2,2,128,256]{3,2,1,0:T(8,128)(2,1)} %copy-done.6) | copy-start | bytes 786436
  62.3 11.0 %copy-start.3 = (bf16[2,2,128,256]{3,2,1,0:T(8,128)(2,1)S(1)}, bf16[2,2,128,256]{3,2,1,0:T(8,128)(2,1)}, u32[]{:S(2)}) copy-start(bf16[2,2,128,256]{3,2,1,0:T(8,128)(2,1)} %copy-done.2) | copy-start | bytes 786436
  62.3 8.5 %collective-permute-start.22 = (bf16[2,2,128,256]{3,2,1,0:T(8,128)(2,1)S(1)}, bf16[2,2,128,256]{3,2,1,0:T(8,128)(2,1)S(1)}, u32[]{:S(2)}, u32[]{:S(2)}) collective-permute-start(bf16[2,2,128,256]{3,2,1,0:T(8,128)(2,1)S(1)} %collective-permute-done.14.refs_3_), channel_id=1, source_target_pairs={{0,2},{2,0},{4,6},{6,4},{8,10},{10,8},{12,14},{14,12},{1,3},{3,1},... | collective-permute-start | bytes 786440 | tf_op jit(solution)/shard_map/ppermute | solution.py:325
  63.8 9.5 %collective-permute-start.26 = (bf16[2,2,128,256]{3,2,1,0:T(8,128)(2,1)}, bf16[2,2,128,256]{3,2,1,0:T(8,128)(2,1)S(1)}, u32[]{:S(2)}, u32[]{:S(2)}) collective-permute-start(bf16[2,2,128,256]{3,2,1,0:T(8,128)(2,1)} %copy-done.6), channel_id=1, source_target_pairs={{0,2},{2,0},{4,6},{6,4},{8,10},{10,8},{12,14},{14,12},{1,3},{3,1},... | collective-permute-start | bytes 786440 | tf_op jit(solution)/shard_map/ppermute | solution.py:325
  64.5 6.9 %collective-permute-start.20 = (bf16[2,4,3,32,256]{4,3,2,1,0:T(8,128)(2,1)S(1)}, bf16[2,4,3,32,256]{4,3,2,1,0:T(8,128)(2,1)S(1)}, u32[]{:S(2)}, u32[]{:S(2)}) collective-permute-start(bf16[2,4,3,32,256]{4,3,2,1,0:T(8,128)(2,1)S(1)} %gather.5.refs_2_), channel_id=1, source_target_pairs={{0,1},{1,0},{2,3},{3,2},{4,5},{5,4},{6,7},{7,6},{8,9},{9,8},{10,11... | collective-permute-start | bytes 1179656 | tf_op jit(solution)/shard_map/ppermute | solution.py:325
  67.2 4.2 %collective-permute-start.18 = (bf16[2,2,3,32,256]{4,3,2,1,0:T(8,128)(2,1)S(1)}, bf16[2,2,3,32,256]{4,3,2,1,0:T(8,128)(2,1)S(1)}, u32[]{:S(2)}, u32[]{:S(2)}) collective-permute-start(bf16[2,2,3,32,256]{4,3,2,1,0:T(8,128)(2,1)S(1)} %get-tuple-element.66.refs_0_), channel_id=1, source_target_pairs={{0,1},{1,0},{2,3},{3,2},{4,5},{5,4},{6,7},{7,6},{8,9},{9,8},{10,11... | collective-permute-start | bytes 589832 | tf_op jit(solution)/shard_map/ppermute | solution.py:325
  70.8 1.4 %collective-permute-start.19 = (bf16[2,2,3,32,256]{4,3,2,1,0:T(8,128)(2,1)S(1)}, bf16[2,2,3,32,256]{4,3,2,1,0:T(8,128)(2,1)S(1)}, u32[]{:S(2)}, u32[]{:S(2)}) collective-permute-start(bf16[2,2,3,32,256]{4,3,2,1,0:T(8,128)(2,1)S(1)} %get-tuple-element.70.refs_1_), channel_id=1, source_target_pairs={{0,1},{1,0},{2,3},{3,2},{4,5},{5,4},{6,7},{7,6},{8,9},{9,8},{10,11... | collective-permute-start | bytes 589832 | tf_op jit(solution)/shard_map/ppermute | solution.py:325
  70.9 9.0 %collective-permute-start.25 = (bf16[2,2,128,256]{3,2,1,0:T(8,128)(2,1)S(1)}, bf16[2,2,128,256]{3,2,1,0:T(8,128)(2,1)S(1)}, u32[]{:S(2)}, u32[]{:S(2)}) collective-permute-start(bf16[2,2,128,256]{3,2,1,0:T(8,128)(2,1)S(1)} %collective-permute-done.23.refs_2_), channel_id=1, source_target_pairs={{0,2},{2,0},{4,6},{6,4},{8,10},{10,8},{12,14},{14,12},{1,3},{3,1},... | collective-permute-start | bytes 786440 | tf_op jit(solution)/shard_map/ppermute | solution.py:325
